TPU v7x, 32 devices: a whole 2x2x4 slice. The times are simulated.
32 devices in a mesh: dp: 8 (over z, y), head: 4 (over x, core).
Axes of the slice: x: 2, y: 2, z: 4, core: 2. Of those that a mesh axis runs over, the one named last changes fastest.
Arguments:
- tokens: float32 [16384, 512], P('dp'), may hold values from -6 to 6
- cotangent: float32 [16384, 512], P('dp'), may hold values from -6 to 6
- timesteps: int32 [64], P('dp'), may hold values from 1 to 1000
- bands: int32 [64], P('dp'), may hold values from 0 to 7
- lengths: int32 [64], P('dp'), may hold values from 1 to 256, as said below
- owners: int32 [16], replicated, may hold values from 0 to 7, as said below
- master_slots: float32 [24, 196608], P('dp', 'head'), as said below
- first_slots: float32 [24, 196608], P('dp', 'head'), as said below
- second_slots: float32 [24, 196608], P('dp', 'head'), as said below
- norm_master: float32 [4, 512], P(None, 'dp'), as said below
- norm_first: float32 [4, 512], P(None, 'dp')
- norm_second: float32 [4, 512], P(None, 'dp'), as said below
Outputs:
- block_output: float32 [16384, 512], P('dp')
- input_grad: float32 [16384, 512], P('dp')
- new_master: float32 [24, 196608], P('dp', 'head')
- new_first: float32 [24, 196608], P('dp', 'head')
- new_second: float32 [24, 196608], P('dp', 'head')
- new_norms: float32 [4, 512], P(None, 'dp')
- new_norm_first: float32 [4, 512], P(None, 'dp')
- new_norm_second: float32 [4, 512], P(None, 'dp')
Inputs may be any that keep to these rules, and one draw needn't show every extreme that they name: `lengths`: positions at or past an item's length are padding; the items of higher indices of dp tend to be longer, and some item has all 256 characters. `owners`: every index of dp holds 1 to 3 of the 16 blocks and some holds exactly 3. `master_slots`: row 3 * o + c holds the block that is the c-th, in block order, held by index o; rows past an owner's count are unused. `first_slots`: laid out as master_slots. `second_slots`: laid out as master_slots; positive. `norm_master`: Rows: gain1, shift1, gain2, shift2. `norm_second`: Positive.
All inputs are finite; a program needn't handle non-finite values.
Results may differ from a plain program's by a relative error of at most 0.025.
Values may be sent and summed in bfloat16 or wider, within the bound.
A program may use at most 128 MiB of HBM per device.

v0:
```python
import math

import jax
import jax.numpy as jnp
from jax import lax
from jax.sharding import PartitionSpec as P

D = 512
H = 8
HD = 64
FF = 2048
SEQ = 256
TSTEPS = 1000
NBANDS = 8
CAP = 3
STEP = 5


beta_one = 0.5
beta_two = 0.5
learn_rate = 0.04
norm_rate = 0.4
weight_decay = 0.1
adam_eps = 1e-08
norm_eps = 1e-05


def contract_rows(left_side, right_side):
    return lax.dot_general(
        left_side, right_side, (((0,), (0,)), ((), ())), preferred_element_type=jnp.float32
    )


def contract_cols(left_side, right_side):
    return lax.dot_general(
        left_side, right_side, (((1,), (1,)), ((), ())), preferred_element_type=jnp.float32
    )


def gelu_tanh(values):
    return jax.nn.gelu(values, approximate=True)


def norm_forward(values, gain_row, shift_row):
    average = jnp.mean(values, axis=-1, keepdims=True)
    centred = values - average
    inverse = lax.rsqrt(jnp.mean(centred * centred, axis=-1, keepdims=True) + norm_eps)
    scaled = centred * inverse
    return (scaled * gain_row + shift_row, scaled, inverse)


def norm_backward(grad_normed, scaled, inverse, gain_row):
    grad_scaled = grad_normed * gain_row
    centre_term = jnp.mean(grad_scaled, axis=-1, keepdims=True)
    slope_term = jnp.mean(grad_scaled * scaled, axis=-1, keepdims=True)
    return inverse * (grad_scaled - centre_term - scaled * slope_term)


def slot_rows(owners, capacity):
    block_index = jnp.arange(owners.shape[0], dtype=jnp.int32)
    earlier = (owners[None, :] == owners[:, None]) & (block_index[None, :] < block_index[:, None])
    return owners * capacity + jnp.sum(earlier.astype(jnp.int32), axis=1)


def attention_scores(query_heads, key_heads, key_valid):
    scores = jnp.einsum(
        "gqad,gkad->gaqk", query_heads, key_heads, preferred_element_type=jnp.float32
    ) / math.sqrt(HD)
    return jnp.where(key_valid[:, None, None, :], scores, -1e30)


def adamw_update(weight, first_moment, second, gradient, decay_rate, step_rate):
    new_first = beta_one * first_moment + (1.0 - beta_one) * gradient
    new_second = beta_two * second + (1.0 - beta_two) * gradient * gradient
    first_hat = new_first / (1.0 - beta_one**STEP)
    second_hat = new_second / (1.0 - beta_two**STEP)
    new_weight = weight - step_rate * (
        first_hat / (jnp.sqrt(second_hat) + adam_eps) + decay_rate * weight
    )
    return (new_weight, new_first, new_second)


def shards(
    tokens,
    cotangent,
    timesteps,
    bands,
    lengths,
    owners,
    master_slots,
    first_slots,
    second_slots,
    norm_master,
    norm_first,
    norm_second,
):
    head_count = lax.axis_size("head")
    owner_index = lax.axis_index("dp")
    heads_here = H // head_count
    width_here = heads_here * HD
    units_here = FF // head_count
    block_len = master_slots.shape[1]
    norm_cols = norm_master.shape[1]
    row_count = tokens.shape[0]
    item_count = lengths.shape[0]
    block_count = owners.shape[0]
    slot_row = slot_rows(owners, CAP)
    gathered, norm_whole = (
        lax.all_gather(master_slots.astype(jnp.bfloat16), "dp", axis=0, tiled=True),
        lax.all_gather(norm_master.astype(jnp.bfloat16), "dp", axis=1, tiled=True),
    )
    flat_params = gathered[slot_row].reshape(-1)
    qkv_end = 3 * D * width_here
    out_end = qkv_end + width_here * D
    up_end = out_end + D * units_here
    qkv_weight = flat_params[:qkv_end].reshape(D, 3 * width_here)
    out_weight = flat_params[qkv_end:out_end].reshape(width_here, D)
    up_weight = flat_params[out_end:up_end].reshape(D, units_here)
    down_weight = flat_params[up_end:].reshape(units_here, D)
    norm_params = norm_whole.astype(jnp.float32)
    item_weight = jnp.exp(-2.0 * timesteps.astype(jnp.float32) / TSTEPS)
    item_length = lengths.astype(jnp.float32)
    band_table = (bands[:, None] == jnp.arange(NBANDS, dtype=jnp.int32)[None, :]).astype(
        jnp.float32
    )
    weight_sums, count_sums = lax.psum(
        (
            jnp.sum(band_table * (item_weight * item_length)[:, None], axis=0),
            jnp.sum(band_table * item_length[:, None], axis=0),
        ),
        "dp",
    )
    item_scale = (
        item_weight
        * jnp.sum(band_table * count_sums[None, :], axis=1)
        / jnp.sum(band_table * weight_sums[None, :], axis=1)
    )
    key_valid = jnp.arange(SEQ, dtype=jnp.int32)[None, :] < lengths[:, None]
    token_scale = jnp.where(key_valid, item_scale[:, None], 0.0).reshape(row_count)
    normed_one, scaled_one, inverse_one = norm_forward(tokens, norm_params[0], norm_params[1])
    normed_one_low = normed_one.astype(jnp.bfloat16)
    projected_low = jnp.dot(normed_one_low, qkv_weight, preferred_element_type=jnp.float32).astype(
        jnp.bfloat16
    )
    head_shape = (item_count, SEQ, heads_here, HD)
    query_heads = projected_low[:, :width_here].reshape(head_shape)
    key_heads = projected_low[:, width_here : 2 * width_here].reshape(head_shape)
    value_heads = projected_low[:, 2 * width_here :].reshape(head_shape)
    scores = attention_scores(query_heads, key_heads, key_valid)
    row_max = jnp.max(scores, axis=-1, keepdims=True)
    exp_scores = jnp.exp(scores - row_max)
    row_total = jnp.sum(exp_scores, axis=-1, keepdims=True)
    log_total = row_max + jnp.log(row_total)
    prob_low = (exp_scores / row_total).astype(jnp.bfloat16)
    attended_low = (
        jnp.einsum("gaqk,gkad->gqad", prob_low, value_heads, preferred_element_type=jnp.float32)
        .astype(jnp.bfloat16)
        .reshape(row_count, width_here)
    )
    attn_sum = lax.psum(
        jnp.dot(attended_low, out_weight, preferred_element_type=jnp.float32).astype(jnp.bfloat16),
        "head",
    ).astype(jnp.float32)
    mixed_state = tokens + attn_sum
    normed_two, scaled_two, inverse_two = norm_forward(mixed_state, norm_params[2], norm_params[3])
    normed_two_low = normed_two.astype(jnp.bfloat16)
    hidden = jnp.dot(normed_two_low, up_weight, preferred_element_type=jnp.float32)
    activated, gelu_pull = jax.vjp(gelu_tanh, hidden)
    activated_low = activated.astype(jnp.bfloat16)
    ffn_sum = lax.psum(
        jnp.dot(activated_low, down_weight, preferred_element_type=jnp.float32).astype(
            jnp.bfloat16
        ),
        "head",
    ).astype(jnp.float32)
    block_output = mixed_state + ffn_sum
    grad_state = cotangent * token_scale[:, None]
    grad_low_two = grad_state.astype(jnp.bfloat16)
    grad_down = contract_rows(activated_low, grad_low_two)
    grad_activated = contract_cols(grad_low_two, down_weight)
    grad_hidden_low = gelu_pull(grad_activated)[0].astype(jnp.bfloat16)
    grad_up = contract_rows(normed_two_low, grad_hidden_low)
    grad_normed_two = lax.psum(
        contract_cols(grad_hidden_low, up_weight).astype(jnp.bfloat16), "head"
    ).astype(jnp.float32)
    grad_mixed = grad_state + norm_backward(
        grad_normed_two, scaled_two, inverse_two, norm_params[2]
    )
    grad_low_one = grad_mixed.astype(jnp.bfloat16)
    grad_out_proj = contract_rows(attended_low, grad_low_one)
    grad_attended_low = (
        contract_cols(grad_low_one, out_weight).astype(jnp.bfloat16).reshape(head_shape)
    )
    scores_again = attention_scores(query_heads, key_heads, key_valid)
    probabilities = jnp.exp(scores_again - log_total)
    prob_again_low = probabilities.astype(jnp.bfloat16)
    grad_values = jnp.einsum(
        "gaqk,gqad->gkad", prob_again_low, grad_attended_low, preferred_element_type=jnp.float32
    )
    grad_probs = jnp.einsum(
        "gqad,gkad->gaqk", grad_attended_low, value_heads, preferred_element_type=jnp.float32
    )
    grad_scores_low = (
        probabilities * (grad_probs - jnp.sum(grad_probs * probabilities, axis=-1, keepdims=True))
    ).astype(jnp.bfloat16)
    grad_queries = jnp.einsum(
        "gaqk,gkad->gqad", grad_scores_low, key_heads, preferred_element_type=jnp.float32
    ) / math.sqrt(HD)
    grad_keys = jnp.einsum(
        "gaqk,gqad->gkad", grad_scores_low, query_heads, preferred_element_type=jnp.float32
    ) / math.sqrt(HD)
    grad_projected_low = jnp.concatenate(
        [
            grad_queries.reshape(row_count, width_here),
            grad_keys.reshape(row_count, width_here),
            grad_values.reshape(row_count, width_here),
        ],
        axis=1,
    ).astype(jnp.bfloat16)
    grad_qkv = contract_rows(normed_one_low, grad_projected_low)
    grad_normed_one = lax.psum(
        contract_cols(grad_projected_low, qkv_weight).astype(jnp.bfloat16), "head"
    ).astype(jnp.float32)
    input_grad = grad_mixed + norm_backward(
        grad_normed_one, scaled_one, inverse_one, norm_params[0]
    )
    norm_grads = jnp.stack(
        [
            jnp.sum(grad_normed_one * scaled_one, axis=0),
            jnp.sum(grad_normed_one, axis=0),
            jnp.sum(grad_normed_two * scaled_two, axis=0),
            jnp.sum(grad_normed_two, axis=0),
        ]
    )
    grad_blocks = jnp.concatenate(
        [
            grad_qkv.reshape(-1),
            grad_out_proj.reshape(-1),
            grad_up.reshape(-1),
            grad_down.reshape(-1),
        ]
    ).reshape(block_count, block_len)
    summed, norm_summed = (
        lax.psum(grad_blocks.astype(jnp.bfloat16), "dp").astype(jnp.float32),
        lax.psum(norm_grads.astype(jnp.bfloat16), "dp").astype(jnp.float32),
    )
    landing = jnp.where(owners == owner_index, slot_row - owner_index * CAP, CAP)
    owned_grad = jnp.zeros((CAP, block_len), jnp.float32).at[landing].set(summed, mode="drop")
    norm_owned = lax.dynamic_slice_in_dim(norm_summed, owner_index * norm_cols, norm_cols, 1)
    held_count = jnp.sum((owners == owner_index).astype(jnp.int32))
    used_slot = (jnp.arange(CAP, dtype=jnp.int32) < held_count)[:, None]
    new_master, new_first, new_second = adamw_update(
        master_slots, first_slots, second_slots, owned_grad, weight_decay, learn_rate
    )
    new_master = jnp.where(used_slot, new_master, 0.0)
    new_first = jnp.where(used_slot, new_first, 0.0)
    new_second = jnp.where(used_slot, new_second, 0.0)
    new_norms, new_norm_first, new_norm_second = adamw_update(
        norm_master, norm_first, norm_second, norm_owned, 0.0, norm_rate
    )
    return (
        block_output,
        input_grad,
        new_master,
        new_first,
        new_second,
        new_norms,
        new_norm_first,
        new_norm_second,
    )


def solution(mesh):
    placed = (
        P("dp", None),
        P("dp", None),
        P("dp"),
        P("dp"),
        P("dp"),
        P(),
        P("dp", "head"),
        P("dp", "head"),
        P("dp", "head"),
        P(None, "dp"),
        P(None, "dp"),
        P(None, "dp"),
    )
    return jax.shard_map(
        shards,
        mesh=mesh,
        in_specs=placed,
        out_specs=(
            P("dp", None),
            P("dp", None),
            P("dp", "head"),
            P("dp", "head"),
            P("dp", "head"),
            P(None, "dp"),
            P(None, "dp"),
            P(None, "dp"),
        ),
        check_vma=False,
    )
```

profile of v0, /device:TPU:0, one launch (start us, length us, event | category | flops | bytes accessed | tf_op | source)
XLA Modules:
  0.0 472.5 jit_solution(14784900503764084815)
XLA Ops:
  10.7 22.3 %all-gather = bf16[8,64,4]{1,2,0:T(4,128)(2,1)S(1)} all-gather(bf16[1,64,4]{1,2,0:T(4,128)(2,1)S(1)} %convert_bitcast_fusion.1), channel_id=1, replica_groups=mesh['dp'=8,'head'=4] {'dp'}, dimensions={0}, use_global_device_ids=true | all-gather | bytes 4608 | tf_op jit(solution)/shard_map/all_gather | solution.py:110
  41.9 32.1 %all-gather.4.cloned.1.call-done = bf16[8,3,49152]{2,1,0:T(4,128)(2,1)} async-done(((bf16[1,3,49152]{2,1,0:T(4,128)(2,1)}), bf16[8,3,49152]{2,1,0:T(4,128)(2,1)}) %all-gather.4.cloned.1.call-update) | async-done | bytes 2359312 | tf_op jit(solution)/shard_map/all_gather | solution.py:109
  73.9 3.8 reshape.213
  80.5 2.9 slice.47
  93.1 3.0 convolution_convert_fusion
  96.2 19.2 %all-reduce = (f32[8]{0:T(128)S(1)}, f32[8]{0:T(128)S(1)}) all-reduce(f32[8]{0:T(128)S(1)} %get-tuple-element.16, f32[8]{0:T(128)S(1)} %get-tuple-element.17), channel_id=1, replica_groups=mesh['dp'=8,'head'=4] {'dp'}, use_global_device_ids=true, to_apply=%region_10.11 | all-reduce | flops 16 | bytes 128 | tf_op jit(solution)/shard_map/psum | solution.py:126
  115.7 30.5 %all-reduce.7.cloned.1.call-done = bf16[2048,512]{1,0:T(8,128)(2,1)} async-done(((bf16[2048,512]{1,0:T(8,128)(2,1)}), bf16[2048,512]{1,0:T(8,128)(2,1)}) %all-reduce.7.cloned.1.call-update) | async-done | bytes 2097168 | tf_op jit(solution)/shard_map/psum | solution.py:160
  146.2 3.3 fusion.65
  154.6 4.2 fusion.22
  162.9 5.5 %fusion.41 = bf16[64,4,8,128]{3,2,1,0:T(8,128)(2,1)S(1)} fusion(f32[2048,512]{1,0:T(8,128)} %param.13, f32[2048]{0:T(1024)S(1)} %bitcast.97, f32[2048,512]{1,0:T(8,128)} %copy-done.9), kind=kOutput, calls=%fused_computation.74 | convolution fusion | flops 1085538304 | bytes 8921088 | tf_op jit(solution)/shard_map/dot_general | solution.py:29
  171.8 42.7 %all-reduce.9.cloned.1.call-done = bf16[2048,512]{1,0:T(8,128)(2,1)} async-done(((bf16[2048,512]{1,0:T(8,128)(2,1)}), bf16[2048,512]{1,0:T(8,128)(2,1)}) %all-reduce.9.cloned.1.call-update) | async-done | bytes 2097168 | tf_op jit(solution)/shard_map/psum | solution.py:183
  214.4 5.6 %fusion.10 = (bf16[512]{0:T(512)(128)(2,1)}, f32[2048]{0:T(1024)S(1)}, f32[2048]{0:T(1024)S(1)}) fusion(bf16[2048,512]{1,0:T(8,128)(2,1)} %all-reduce.9.cloned.1.call-done, f32[2048,512]{1,0:T(8,128)} %copy-done, f32[2048]{0:T(1024)S(1)} %add_rsqrt_fusion, f32[2048]{0:T(1024)S(1)} %broadcast_multiply_fusion.4, f32[512]{0:T(512)S(1)} %bitcast.100), kind=kLoop, calls=%fused_computation.18 | loop fusion | flops 9432576 | bytes 6327296 | tf_op jit(solution)/shard_map/reduce_sum | solution.py:231
  220.1 4.3 fusion.8
  227.5 3.2 reshape.218
  233.0 3.1 fusion.42
  252.4 5.4 %convolution_convert_fusion.3 = bf16[2048,512]{1,0:T(8,128)(2,1)} fusion(bf16[1536,512]{1,0:T(8,128)(2,1)} %slice.47, f32[2048,512]{1,0:T(8,128)} %copy-done.9), kind=kOutput, calls=%fused_computation.54 | convolution fusion | flops 1084227584 | bytes 6815744 | tf_op jit(solution)/shard_map/dot_general | solution.py:171
  258.1 4.0 convolution_convert_fusion.1
  262.2 78.3 %all-reduce.11.cloned.1.call-done = bf16[16,49152]{1,0:T(8,128)(2,1)} async-done(((bf16[16,49152]{1,0:T(8,128)(2,1)}), bf16[16,49152]{1,0:T(8,128)(2,1)}) %all-reduce.11.cloned.1.call-update) | async-done | bytes 1572880 | tf_op jit(solution)/shard_map/psum | solution.py:244
  340.5 5.2 %scatter_custom_fusion = f32[3,49152]{1,0:T(4,128)S(1)} fusion(s32[16]{0:T(128)} %get-tuple-element.37, bf16[16,49152]{1,0:T(8,128)(2,1)} %all-reduce.11.cloned.1.call-done, f32[]{:T(128)} %constant.25.clone.1), kind=kCustom, calls=%fused_computation.49 | custom fusion | flops 786432 | bytes 2163200 | tf_op jit(solution)/shard_map/scatter | solution.py:248
  345.7 3.1 broadcast_select_fusion
  348.8 79.6 %all-reduce.13.cloned.1.call-done = (bf16[2048,512]{1,0:T(8,128)(2,1)}, bf16[2048,512]{1,0:T(8,128)(2,1)}) async-done(((bf16[2048,512]{1,0:T(8,128)(2,1)}, bf16[2048,512]{1,0:T(8,128)(2,1)}), (bf16[2048,512]{1,0:T(8,128)(2,1)}, bf16[2048,512]{1,0:T(8,128)(2,1)})) %all-reduce.13.cloned.1.call-update) | async-done | bytes 4194320 | tf_op jit(solution)/shard_map/psum | solution.py:170
  430.4 4.4 fusion.15
  437.9 21.4 %psum.63 = bf16[4,512]{1,0:T(4,128)(2,1)S(1)} all-reduce(bf16[4,512]{1,0:T(4,128)(2,1)S(1)} %pad_maximum_fusion.1), channel_id=1, replica_groups=mesh['dp'=8,'head'=4] {'dp'}, use_global_device_ids=true, to_apply=%region_29.30 | all-reduce | flops 2048 | bytes 8192 | tf_op jit(solution)/shard_map/psum | solution.py:245
  459.4 5.5 %fusion.13 = f32[2048,512]{1,0:T(8,128)} fusion(f32[2048,512]{1,0:T(8,128)} %copy-done.6, bf16[2048,512]{1,0:T(8,128)(2,1)S(1)} %copy-done.8, f32[2048,512]{1,0:T(8,128)} %param.12, f32[2048]{0:T(1024)S(1)} %broadcast_multiply_fusion, f32[2048]{0:T(1024)S(1)} %broadcast_multiply_fusion.1, f32[512]{0:T(512)S(1)} %bitcast.105, f32[2048]{0:T(1024)S(1)} %add_rsqrt_fusion.1, ...), kind=kLoop, calls=%fused_computation.21 | loop fusion | flops 9437184 | bytes 14714880 | tf_op jit(solution)/shard_map/add | solution.py:224
  (170 shorter events, 65.0 us)
Async XLA Ops:
  7.2 29.9 %copy-start.36 = (s32[8]{0:T(128)S(1)}, s32[8]{0:T(128)}, u32[]{:S(2)}) copy-start(s32[8]{0:T(128)} %param.16) | copy-start | bytes 100
  7.2 28.4 %copy-start.37 = (s32[16]{0:T(128)S(1)}, s32[16]{0:T(128)}, u32[]{:S(2)}) copy-start(s32[16]{0:T(128)} %param.17) | copy-start | bytes 196
  7.2 66.7 %all-gather.4.cloned.1.call-start = ((), (), s32[]{:S(2)}) async-start(), calls=%async_computation.3 | async-start | bytes 3538944 | tf_op jit(solution)/shard_map/all_gather | solution.py:109
  9.3 136.9 %all-reduce.7.cloned.1.call-start = ((), (), s32[]{:S(2)}) async-start(), calls=%async_computation | async-start | bytes 4194304 | tf_op jit(solution)/shard_map/psum | solution.py:160
  37.1 4.7 %copy-start.29 = (f32[1,512]{1,0:T(1,128)}, f32[1,512]{1,0:T(1,128)S(1)}, u32[]{:S(2)}) copy-start(f32[1,512]{1,0:T(1,128)S(1)} %get-tuple-element.36) | copy-start | bytes 6148
  96.0 118.4 %all-reduce.9.cloned.1.call-start = ((), (), s32[]{:S(2)}) async-start(), calls=%async_computation.1 | async-start | bytes 4194304 | tf_op jit(solution)/shard_map/psum | solution.py:183
  153.7 5.1 %copy-start.9 = (f32[2048,512]{1,0:T(8,128)}, f32[2048,512]{1,0:T(8,128)S(1)}, u32[]{:S(2)}) copy-start(f32[2048,512]{1,0:T(8,128)S(1)} %fusion.55) | copy-start | bytes 12582916
  162.8 177.7 %all-reduce.11.cloned.1.call-start = ((), (), s32[]{:S(2)}) async-start(), calls=%async_computation.2 | async-start | bytes 3145728 | tf_op jit(solution)/shard_map/psum | solution.py:244
  162.9 6.6 %copy-start.19 = (bf16[2048,512]{1,0:T(8,128)(2,1)S(1)}, bf16[2048,512]{1,0:T(8,128)(2,1)}, u32[]{:S(2)}) copy-start(bf16[2048,512]{1,0:T(8,128)(2,1)} %copy-done.18) | copy-start | bytes 6291460
  214.4 5.6 %copy-start.1 = (f32[2048,512]{1,0:T(8,128)S(1)}, f32[2048,512]{1,0:T(8,128)}, u32[]{:S(2)}) copy-start(f32[2048,512]{1,0:T(8,128)} %copy-done) | copy-start | bytes 12582916
  214.4 5.6 %copy-start.7 = (bf16[2048,512]{1,0:T(8,128)(2,1)S(1)}, bf16[2048,512]{1,0:T(8,128)(2,1)}, u32[]{:S(2)}) copy-start(bf16[2048,512]{1,0:T(8,128)(2,1)} %all-reduce.9.cloned.1.call-done) | copy-start | bytes 6291460
  241.9 4.6 copy-start.20
  251.4 177.1 %all-reduce.13.cloned.1.call-start = ((), (), s32[]{:S(2)}) async-start(), calls=%async_computation.4 | async-start | bytes 8388608 | tf_op jit(solution)/shard_map/psum | solution.py:170
  252.4 5.8 %copy-start.32 = (bf16[512]{0:T(512)(128)(2,1)S(1)}, bf16[512]{0:T(512)(128)(2,1)}, u32[]{:S(2)}) copy-start(bf16[512]{0:T(512)(128)(2,1)} %get-tuple-element.10) | copy-start | bytes 3076
  252.4 5.8 %copy-start.27 = (bf16[512,384]{1,0:T(8,128)(2,1)S(1)}, bf16[512,384]{1,0:T(8,128)(2,1)}, u32[]{:S(2)}) copy-start(bf16[512,384]{1,0:T(8,128)(2,1)} %copy-done.26) | copy-start | bytes 1179652
  262.2 83.5 %copy-start.14 = (f32[3,49152]{1,0:T(4,128)S(1)}, f32[3,49152]{1,0:T(4,128)}, u32[]{:S(2)}) copy-start(f32[3,49152]{1,0:T(4,128)} %param.18) | copy-start | bytes 1769476
  262.2 83.5 %copy-start.24 = (f32[3,49152]{1,0:T(4,128)S(1)}, f32[3,49152]{1,0:T(4,128)}, u32[]{:S(2)}) copy-start(f32[3,49152]{1,0:T(4,128)} %param.20) | copy-start | bytes 1769476
  262.2 83.5 %copy-start.25 = (f32[3,49152]{1,0:T(4,128)S(1)}, f32[3,49152]{1,0:T(4,128)}, u32[]{:S(2)}) copy-start(f32[3,49152]{1,0:T(4,128)} %param.19) | copy-start | bytes 1769476
  345.7 84.7 %copy-start.30 = (f32[1,512]{1,0:T(1,128)S(1)}, f32[1,512]{1,0:T(1,128)}, u32[]{:S(2)}) copy-start(f32[1,512]{1,0:T(1,128)} %copy-done.29) | copy-start | bytes 6148
  430.4 4.7 %copy-start.15 = (bf16[2048,512]{1,0:T(8,128)(2,1)S(1)}, bf16[2048,512]{1,0:T(8,128)(2,1)}, u32[]{:S(2)}) copy-start(bf16[2048,512]{1,0:T(8,128)(2,1)} %get-tuple-element.20) | copy-start | bytes 6291460
  435.1 24.2 %copy-start.8 = (bf16[2048,512]{1,0:T(8,128)(2,1)S(1)}, bf16[2048,512]{1,0:T(8,128)(2,1)}, u32[]{:S(2)}) copy-start(bf16[2048,512]{1,0:T(8,128)(2,1)} %get-tuple-element.21) | copy-start | bytes 6291460
  459.3 5.5 %copy-start.31 = (f32[4,64]{1,0:T(4,128)S(1)}, f32[4,64]{1,0:T(4,128)}, u32[]{:S(2)}) copy-start(f32[4,64]{1,0:T(4,128)} %param.21) | copy-start | bytes 3076
  459.3 5.5 %copy-start.33 = (f32[4,64]{1,0:T(4,128)S(1)}, f32[4,64]{1,0:T(4,128)}, u32[]{:S(2)}) copy-start(f32[4,64]{1,0:T(4,128)} %param.22) | copy-start | bytes 3076
  459.3 5.5 %copy-start.34 = (f32[4,64]{1,0:T(4,128)S(1)}, f32[4,64]{1,0:T(4,128)}, u32[]{:S(2)}) copy-start(f32[4,64]{1,0:T(4,128)} %param.23) | copy-start | bytes 3076
  (21 other events, 56.4 us)
Sparse Core Ops, SparseCore 0:
  10.8 63.0 all-gather.3
  96.1 49.9 all-reduce.6
  162.9 51.4 all-reduce.8
  251.5 88.9 all-reduce.10
  343.3 85.0 all-reduce.12
where the time goes:
time: 481 us; the launch traced here: 472 us
  waiting for transfers between devices  263 us (55%)
  blocking collectives  62.9 us (13%)
  other arithmetic  55.8 us (12%)
  matrix products  41.4 us (9%)
  local copies, waits for them, and re-layouts  33.8 us (7%)
  between operations  14.9 us (3%)
    psum x1, waiting for transfers between devices, shards(): lax.psum(jnp.dot(activated_low, down_weight, preferred_element_type=jnp.f...  79.6 us
    psum x1, waiting for transfers between devices, shards(): lax.psum(grad_blocks.astype(jnp.bfloat16), 'dp').astype(jnp.float32)  78.3 us
    psum x1, waiting for transfers between devices, shards(): lax.psum(contract_cols(grad_hidden_low, up_weight).astype(jnp.bfloat16),...  42.7 us
    all_gather x1, waiting for transfers between devices, shards(): lax.all_gather(master_slots.astype(jnp.bfloat16), 'dp', axis=0, tiled=True)  32.1 us
    psum x1, waiting for transfers between devices, shards(): lax.psum(jnp.dot(attended_low, out_weight, preferred_element_type=jnp.flo...  30.5 us
    all_gather x1, blocking collectives, shards(): lax.all_gather(norm_master.astype(jnp.bfloat16), 'dp', axis=1, tiled=True)  22.3 us
    psum x1, blocking collectives, shards(): lax.psum(norm_grads.astype(jnp.bfloat16), 'dp').astype(jnp.float32)  21.4 us
    psum x1, blocking collectives, shards(): lax.psum((jnp.sum(band_table * (item_weight * item_length)[:, None], axis...  19.2 us
  transfers between devices with their start and end apart: 5, of which 5 were waited for; matrix products, arithmetic and copies ran while one was open for 8% of the time, Pallas kernels for 0%

commit v1 on v0

--- a/solution.py
+++ b/solution.py
@@ -3,6 +3,8 @@
 import jax
 import jax.numpy as jnp
 from jax import lax
+from jax.experimental import pallas as pl
+from jax.experimental.pallas import tpu as pltpu
 from jax.sharding import PartitionSpec as P
 
 D = 512
@@ -270,7 +272,718 @@
     )
 
 
+W = 128
+R = 384
+QB = 4
+CB = 12
+MESH = pl.DeviceIdType.MESH
+bf16 = jnp.bfloat16
+f32 = jnp.float32
+
+
+def place(sizes):
+    dp = lax.axis_index("dp")
+    head = lax.axis_index("head")
+    return dp // sizes.y, lax.rem(dp, sizes.y), head // sizes.c, lax.rem(head, sizes.c)
+
+
+class Sizes:
+    z, y, x, c = 4, 2, 2, 2
+
+
+def device(z, y, x, c):
+    return (z * Sizes.y + y, x * Sizes.c + c)
+
+
+def greet(partners):
+    barrier = pltpu.get_barrier_semaphore()
+    for partner in partners:
+        pl.semaphore_signal(barrier, inc=1, device_id=partner, device_id_type=MESH)
+    pl.semaphore_wait(barrier, len(partners))
+
+
+def block_rows(owners):
+    ids = [owners[j] for j in range(owners.shape[0])]
+    rows = []
+    for j, mine in enumerate(ids):
+        row = mine * CAP
+        for other in ids[:j]:
+            row = row + jnp.where(other == mine, 1, 0)
+        rows.append(row)
+    return rows
+
+
+def slot_is_wide(rows, slot_row):
+    flag = rows[0] == slot_row
+    for row in rows[1:QB]:
+        flag = jnp.logical_or(flag, row == slot_row)
+    return flag
+
+
+def gather_kernel(
+    master, norms, steps, bands, lens, owners, out, meta_out,
+    flat, own, mine, core_s, core_r, z_s, z_r, ya_s, ya_r, xa_s, xa_r, xb_s, xb_r, yb_s, yb_r, m_s, m_r, loc,
+):
+    z, y, x, c = place(Sizes)
+    nz = Sizes.z
+    partners = [device(lax.rem(z + k, nz), (y + j) % 2, x, c) for k in range(nz) for j in range(2) if k or j]
+    x_peer, y_peer, core_peer = device(z, y, 1 - x, c), device(z, 1 - y, x, c), device(z, y, x, 1 - c)
+    greet(partners + [x_peer, core_peer])
+
+    def remote(src, dst, send, recv, peer):
+        return pltpu.make_async_remote_copy(
+            src_ref=src, dst_ref=dst, send_sem=send, recv_sem=recv, device_id=peer, device_id_type=MESH
+        )
+
+    sent = []
+
+    def push(*args):
+        copy = remote(*args)
+        copy.start()
+        sent.append(copy)
+
+    rows = block_rows(owners)
+    dp = z * Sizes.y + y
+    for r in range(CAP):
+        flat[...] = master[:, r, :]
+        wide = jnp.concatenate([flat[pl.ds(p, W, stride=3), :] for p in range(3)], axis=0)
+        narrow = jnp.concatenate([flat[pl.ds(p, R // 4, stride=4), :] for p in range(4)], axis=0)
+        own[r] = jnp.where(slot_is_wide(rows, dp * CAP + r), wide, narrow).astype(bf16)
+    shard = x * 2 + c
+    far = (1 - x) * 2 + c
+
+    def at(sh, zz, yy):
+        return out.at[sh, zz, yy]
+
+    local = pltpu.make_async_copy(own, at(shard, z, y), loc)
+    local.start()
+    for k in range(1, nz):
+        push(own, at(shard, z, y), z_s.at[k], z_r.at[k], device(lax.rem(z + k, nz), y, x, c))
+
+    item_weight = jnp.exp(-2.0 * steps[...].astype(f32) / TSTEPS)
+    item_length = lens[...].astype(f32)
+    items = steps.shape[1]
+    table = (bands[...] == lax.broadcasted_iota(jnp.int32, (NBANDS, items), 0)).astype(f32)
+    mine[...] = jnp.zeros_like(mine)
+    mine[0:4, 0 : norms.shape[1]] = norms[...]
+    mine[:, 64:65] = jnp.sum(table * (item_weight * item_length), axis=1, keepdims=True)
+    mine[:, 65:66] = jnp.sum(table * item_length, axis=1, keepdims=True)
+    meta_out[dp] = mine[...]
+    for k, partner in enumerate(partners):
+        push(mine, meta_out.at[dp], m_s.at[k], m_r.at[k], partner)
+
+    ra = RA
+
+    def pa(sh, zz, yy):
+        return out.at[sh, zz, yy, :, pl.ds(0, ra), :]
+
+    def pb(sh, zz, yy):
+        return out.at[sh, zz, yy, :, pl.ds(ra, R - ra), :]
+
+    def zs(k):
+        return lax.rem(z + nz - k, nz)
+
+    def wait_recv(dst, send, recv, peer):
+        remote(dst, dst, send, recv, peer).wait_recv()
+
+    def stage0(k):
+        zz = zs(k)
+        if k:
+            wait_recv(at(shard, zz, y), z_s.at[k], z_r.at[k], x_peer)
+        whole = at(shard, zz, y) if k else own
+        first, second = whole.at[:, pl.ds(0, ra), :], whole.at[:, pl.ds(ra, R - ra), :]
+        push(first, pa(shard, zz, y), ya_s.at[k], ya_r.at[k], y_peer)
+        push(second, pb(shard, zz, y), xb_s.at[k], xb_r.at[k], x_peer)
+        push(first, pa(shard, zz, y), xa_s.at[k, 0], xa_r.at[k, 0], x_peer)
+        push(second, pb(shard, zz, y), yb_s.at[k, 0], yb_r.at[k, 0], y_peer)
+        push(whole, at(shard, zz, y), core_s.at[k, 0], core_r.at[k, 0], core_peer)
+
+    def stage1(k):
+        zz = zs(k)
+        wait_recv(pb(far, zz, y), xb_s.at[k], xb_r.at[k], x_peer)
+        push(pb(far, zz, y), pb(far, zz, y), yb_s.at[k, 1], yb_r.at[k, 1], y_peer)
+        wait_recv(pa(shard, zz, 1 - y), ya_s.at[k], ya_r.at[k], y_peer)
+        push(pa(shard, zz, 1 - y), pa(shard, zz, 1 - y), xa_s.at[k, 1], xa_r.at[k, 1], x_peer)
+
+    def stage2(k):
+        zz = zs(k)
+        wait_recv(pa(far, zz, y), xa_s.at[k, 0], xa_r.at[k, 0], x_peer)
+        push(at(far, zz, y), at(far, zz, y), core_s.at[k, 1], core_r.at[k, 1], core_peer)
+        wait_recv(pb(shard, zz, 1 - y), yb_s.at[k, 0], yb_r.at[k, 0], y_peer)
+        push(at(shard, zz, 1 - y), at(shard, zz, 1 - y), core_s.at[k, 2], core_r.at[k, 2], core_peer)
+        wait_recv(pa(far, zz, 1 - y), xa_s.at[k, 1], xa_r.at[k, 1], x_peer)
+        wait_recv(pb(far, zz, 1 - y), yb_s.at[k, 1], yb_r.at[k, 1], y_peer)
+        push(at(far, zz, 1 - y), at(far, zz, 1 - y), core_s.at[k, 3], core_r.at[k, 3], core_peer)
+
+    for step in range(nz + 2):
+        if step < nz:
+            stage0(step)
+        if 0 <= step - 1 < nz:
+            stage1(step - 1)
+        if 0 <= step - 2 < nz:
+            stage2(step - 2)
+    other, other_far = x * 2 + 1 - c, (1 - x) * 2 + 1 - c
+    for k in range(nz):
+        zz = zs(k)
+        for i, (sh, yy) in enumerate(((other, y), (other_far, y), (other, 1 - y), (other_far, 1 - y))):
+            wait_recv(at(sh, zz, yy), core_s.at[k, i], core_r.at[k, i], core_peer)
+    for k in range(len(partners)):
+        wait_recv(meta_out.at[dp], m_s.at[k], m_r.at[k], x_peer)
+    for copy in sent:
+        copy.wait_send()
+    local.wait()
+
+
+RA = 192
+
+
+def gather_weights(master, norms, steps, bands, lens, owners):
+    nz = Sizes.z
+    vm = pl.BlockSpec(memory_space=pltpu.VMEM)
+    sm = pl.BlockSpec(memory_space=pltpu.SMEM)
+    dma = pltpu.SemaphoreType.DMA
+    return pl.pallas_call(
+        gather_kernel,
+        name="gather_weights",
+        out_shape=(
+            jax.ShapeDtypeStruct((4, nz, 2, CAP, R, W), bf16),
+            jax.ShapeDtypeStruct((nz * 2, 8, W), f32),
+        ),
+        in_specs=[vm, vm, vm, vm, vm, sm],
+        out_specs=(pl.BlockSpec(memory_space=pl.ANY), vm),
+        scratch_shapes=[
+            pltpu.VMEM((R, W), f32), pltpu.VMEM((CAP, R, W), bf16), pltpu.VMEM((8, W), f32),
+            dma((nz, 4)), dma((nz, 4)), dma((nz,)), dma((nz,)), dma((nz,)), dma((nz,)), dma((nz, 2)), dma((nz, 2)),
+            dma((nz,)), dma((nz,)), dma((nz, 2)), dma((nz, 2)), dma((8,)), dma((8,)), dma,
+        ],
+        compiler_params=pltpu.CompilerParams(collective_id=0, has_side_effects=True, vmem_limit_bytes=16 << 20),
+    )(master, norms, steps, bands, lens, owners)
+
+
+def dot(left, right):
+    return jnp.dot(left, right, preferred_element_type=f32)
+
+
+def dot_cols(left, right):
+    return lax.dot_general(left, right, (((1,), (1,)), ((), ())), preferred_element_type=f32)
+
+
+def dot_rows(left, right):
+    return lax.dot_general(left, right, (((0,), (0,)), ((), ())), preferred_element_type=f32)
+
+
+def normalise(values):
+    centred = values - jnp.mean(values, axis=-1, keepdims=True)
+    inverse = lax.rsqrt(jnp.mean(centred * centred, axis=-1, keepdims=True) + norm_eps)
+    return centred * inverse, inverse
+
+
+def panels(ref, h, first, size):
+    return jnp.concatenate([ref[h, p, first : first + size, :] for p in range(ref.shape[1])], axis=1)
+
+
+def cat_pieces(first, size):
+    pieces = []
+    row = first
+    while row < first + size:
+        block, inside = divmod(row, R // 4)
+        count = min(R // 4 - inside, first + size - row)
+        pieces.append((QB + block, inside, row - first, count))
+        row += count
+    return pieces
+
+
+def compute_kernel(
+    tok_hbm, cot_hbm, wide_hbm, narrow_hbm, meta, steps, bands, lens, owners,
+    grads, out_delta, in_delta, norm_grads,
+    wq, wc, tok, cot, low1, xhat1, inv1, qkv, probs, att, acc, x1, low2, xhat2, inv2, e2, da2, dx1, e1, da1, gb,
+    w_sem, t_sem, g_sem,
+):
+    head = lax.axis_index("head")
+    tokens_here = tok.shape[0]
+    items_here = tokens_here // SEQ
+    shards_all = wq.shape[0]
+    rows = block_rows(owners)
+
+    def weight_copies(h, blocks):
+        copies = []
+        for j in blocks:
+            if j < QB:
+                src, dst = wide_hbm.at[h, rows[j]], wq.at[h, :, pl.ds(j * W, W), :]
+            else:
+                src, dst = narrow_hbm.at[h, rows[j]], wc.at[h, :, pl.ds((j - QB) * (R // 4), R // 4), :]
+            copies.append(pltpu.make_async_copy(src, dst, w_sem.at[h, j]))
+        return copies
+
+    def grad_copies(h, blocks):
+        return [pltpu.make_async_copy(gb.at[h, j], grads.at[h, rows[j]], g_sem.at[h, j]) for j in blocks]
+
+    first_token = pl.multiple_of(head * tokens_here, tokens_here)
+    tok_copy = pltpu.make_async_copy(tok_hbm.at[pl.ds(first_token, tokens_here), :], tok, t_sem.at[0])
+    cot_copy = pltpu.make_async_copy(cot_hbm.at[pl.ds(first_token, tokens_here), :], cot, t_sem.at[1])
+    tok_copy.start()
+    for h in range(shards_all):
+        for copy in weight_copies(h, range(QB + 2)):
+            copy.start()
+    cot_copy.start()
+    for h in range(shards_all):
+        for copy in weight_copies(h, range(QB + 2, QB + CB)):
+            copy.start()
+
+    lane = lax.broadcasted_iota(jnp.int32, (8, W), 1)
+    chunks = []
+    for pair in range(meta.shape[0] // 2):
+        chunks.append(jnp.where(lane < W // 2, meta[2 * pair], pltpu.roll(meta[2 * pair + 1], W // 2, 1)))
+    norms = jnp.concatenate(chunks, axis=1).astype(bf16).astype(f32)
+    gain1, shift1, gain2, shift2 = (norms[i : i + 1, :] for i in range(4))
+    sums = meta[0]
+    for d in range(1, meta.shape[0]):
+        sums = sums + meta[d]
+    items = steps.shape[1]
+    table = bands[...] == lax.broadcasted_iota(jnp.int32, (NBANDS, items), 0)
+    weight_of = jnp.sum(jnp.where(table, sums[:, 64:65], 0.0), axis=0, keepdims=True)
+    count_of = jnp.sum(jnp.where(table, sums[:, 65:66], 0.0), axis=0, keepdims=True)
+    scales = jnp.exp(-2.0 * steps[...].astype(f32) / TSTEPS) * count_of / weight_of
+    item_lane = lax.broadcasted_iota(jnp.int32, (1, items), 1)
+    position = lax.broadcasted_iota(jnp.int32, (SEQ, 1), 0)
+    columns = []
+    for i in range(items_here):
+        here = item_lane == head * items_here + i
+        scale = jnp.sum(jnp.where(here, scales, 0.0), axis=1, keepdims=True)
+        columns.append(jnp.where(position < lens[head * items_here + i], scale, 0.0))
+    token_scale = jnp.concatenate(columns, axis=0)
+
+    tok_copy.wait()
+    scaled, inverse = normalise(tok[...])
+    xhat1[...] = scaled
+    inv1[...] = inverse
+    low1[...] = (scaled * gain1 + shift1).astype(bf16)
+    acc[...] = jnp.zeros_like(acc)
+
+    head_lane = lax.broadcasted_iota(jnp.int32, (1, W), 1)
+    head_masks = [head_lane < HD, head_lane >= HD]
+    key_pos = lax.broadcasted_iota(jnp.int32, (1, SEQ), 1)
+
+    def only(values, a):
+        return jnp.where(head_masks[a], values, jnp.zeros_like(values))
+
+    def attention(h, _):
+        for copy in weight_copies(h, range(QB + 2)):
+            copy.wait()
+        weight = panels(wq, h, 0, D)
+        projected = dot(low1[...], weight)
+        qkv[h, 0] = (projected[:, :W].astype(bf16).astype(f32) * (1.0 / math.sqrt(HD))).astype(bf16)
+        qkv[h, 1] = projected[:, W : 2 * W].astype(bf16)
+        qkv[h, 2] = projected[:, 2 * W :].astype(bf16)
+        for i in range(items_here):
+            here = slice(i * SEQ, (i + 1) * SEQ)
+            query, key, value = qkv[h, 0, here, :], qkv[h, 1, here, :], qkv[h, 2, here, :]
+            valid = key_pos < lens[head * items_here + i]
+            both = []
+            for a in range(2):
+                scores = jnp.where(valid, dot_cols(only(query, a), key), -1e30)
+                exps = jnp.exp(scores - jnp.max(scores, axis=-1, keepdims=True))
+                prob = (exps * (1.0 / jnp.sum(exps, axis=-1, keepdims=True))).astype(bf16)
+                probs[h, i, a] = prob
+                both.append(prob)
+            stacked = jnp.concatenate([only(value, 0), only(value, 1)], axis=0)
+            att[h, here, :] = dot(jnp.concatenate(both, axis=1), stacked).astype(bf16)
+        acc[...] += dot(att[h], panels(wc, h, 0, W))
+        return 0
+
+    lax.fori_loop(0, shards_all, attention, 0)
+
+    cot_copy.wait()
+    x1[...] = tok[...] + acc[...]
+    scaled, inverse = normalise(x1[...])
+    xhat2[...] = scaled
+    inv2[...] = inverse
+    low2[...] = (scaled * gain2 + shift2).astype(bf16)
+    dx2 = cot[...] * token_scale
+    cot[...] = dx2
+    e2[...] = dx2.astype(bf16)
+    da2[...] = jnp.zeros_like(da2)
+
+    def put(h, first, result):
+        for block, inside, row, count in cat_pieces(first, result.shape[0]):
+            for p in range(4):
+                gb[h, block, pl.ds(p * (R // 4) + inside, count), :] = result[
+                    row : row + count, p * W : (p + 1) * W
+                ].astype(bf16)
+
+    def feed_forward(h, _):
+        for copy in weight_copies(h, range(QB + 2, QB + CB)):
+            copy.wait()
+        up = panels(wc, h, W, D)
+        down = panels(wc, h, W + D, D)
+        hidden = dot(low2[...], up)
+        root = math.sqrt(2.0 / math.pi)
+        square = hidden * hidden
+        bend = jnp.tanh(root * hidden * (1.0 + 0.044715 * square))
+        half = 0.5 * (1.0 + bend)
+        active = (hidden * half).astype(bf16)
+        slope = half + 0.5 * hidden * (1.0 - bend * bend) * (root + (3.0 * 0.044715 * root) * square)
+        acc[...] += dot(active, down)
+        back = (dot_cols(e2[...], down) * slope).astype(bf16)
+        put(h, W + D, dot_rows(active, e2[...]))
+        put(h, W, dot_rows(low2[...], back))
+        da2[...] += dot_cols(back, up)
+        for copy in grad_copies(h, range(QB + 2, QB + CB)):
+            copy.start()
+        return 0
+
+    lax.fori_loop(0, shards_all, feed_forward, 0)
+    out_delta[...] = acc[...].astype(bf16)
+
+    def norm_backward(grad, scaled, inverse, gain):
+        grad_scaled = grad * gain
+        centre = jnp.mean(grad_scaled, axis=-1, keepdims=True)
+        slope = jnp.mean(grad_scaled * scaled, axis=-1, keepdims=True)
+        return inverse * (grad_scaled - centre - scaled * slope)
+
+    grad2 = da2[...]
+    norm_grads[...] = jnp.zeros_like(norm_grads)
+    norm_grads[2:3, :] = jnp.sum(grad2 * xhat2[...], axis=0, keepdims=True)
+    norm_grads[3:4, :] = jnp.sum(grad2, axis=0, keepdims=True)
+    change = norm_backward(grad2, xhat2[...], inv2[...], gain2)
+    dx1[...] = change
+    e1[...] = (cot[...] + change).astype(bf16)
+    da1[...] = jnp.zeros_like(da1)
+
+    def attention_back(h, _):
+        put(h, 0, dot_rows(att[h], e1[...]))
+        d_att = dot_cols(e1[...], panels(wc, h, 0, W)).astype(bf16)
+        parts = []
+        for i in range(items_here):
+            here = slice(i * SEQ, (i + 1) * SEQ)
+            query, key, value = qkv[h, 0, here, :], qkv[h, 1, here, :], qkv[h, 2, here, :]
+            d_here = d_att[here, :]
+            shared = d_here.astype(f32) * att[h, here, :].astype(f32)
+            slopes = []
+            for a in range(2):
+                along = jnp.sum(only(shared, a), axis=-1, keepdims=True)
+                slopes.append((probs[h, i, a].astype(f32) * (dot_cols(only(d_here, a), value) - along)).astype(bf16))
+            stack = lambda values: jnp.concatenate([only(values, 0), only(values, 1)], axis=0)
+            tall = jnp.concatenate(slopes, axis=0)
+            d_query = dot(jnp.concatenate(slopes, axis=1), stack(key)) * (1.0 / math.sqrt(HD))
+            d_key = dot_rows(tall, stack(query))
+            d_value = dot_rows(jnp.concatenate([probs[h, i, 0], probs[h, i, 1]], axis=0), stack(d_here))
+            parts.append(jnp.concatenate([d_query, d_key, d_value], axis=1).astype(bf16))
+        d_qkv = jnp.concatenate(parts, axis=0)
+        d_weight = dot_rows(low1[...], d_qkv).astype(bf16)
+        for j in range(QB):
+            for p in range(3):
+                gb[h, j, p * W : (p + 1) * W, :] = d_weight[j * W : (j + 1) * W, p * W : (p + 1) * W]
+        da1[...] += dot_cols(d_qkv, panels(wq, h, 0, D))
+        for copy in grad_copies(h, range(QB + 2)):
+            copy.start()
+        return 0
+
+    lax.fori_loop(0, shards_all, attention_back, 0)
+    grad1 = da1[...]
+    norm_grads[0:1, :] = jnp.sum(grad1 * xhat1[...], axis=0, keepdims=True)
+    norm_grads[1:2, :] = jnp.sum(grad1, axis=0, keepdims=True)
+    in_delta[...] = (dx1[...] + norm_backward(grad1, xhat1[...], inv1[...], gain1)).astype(bf16)
+    for h in range(shards_all):
+        for copy in grad_copies(h, range(QB + CB)):
+            copy.wait()
+
+
+def compute_items(tokens, cotangent, gathered, meta, steps, bands, lens, owners):
+    head_count = lax.axis_size("head")
+    tokens_here = tokens.shape[0] // head_count
+    items_here = tokens_here // SEQ
+    slots = gathered.shape[1] * gathered.shape[2] * CAP
+    wide = gathered.reshape(4, slots, 3, W, W)
+    narrow = gathered.reshape(4, slots, 4, R // 4, W)
+    vm = pl.BlockSpec(memory_space=pltpu.VMEM)
+    sm = pl.BlockSpec(memory_space=pltpu.SMEM)
+    hbm = pl.BlockSpec(memory_space=pl.ANY)
+    dma = pltpu.SemaphoreType.DMA
+    square = (tokens_here, D)
+    return pl.pallas_call(
+        compute_kernel,
+        name="compute_items",
+        out_shape=(
+            jax.ShapeDtypeStruct((4, slots, R, W), bf16),
+            jax.ShapeDtypeStruct(square, bf16),
+            jax.ShapeDtypeStruct(square, bf16),
+            jax.ShapeDtypeStruct((8, D), f32),
+        ),
+        in_specs=[hbm, hbm, hbm, hbm, vm, vm, vm, sm, sm],
+        out_specs=(hbm, vm, vm, vm),
+        scratch_shapes=[
+            pltpu.VMEM((4, 3, D, W), bf16), pltpu.VMEM((4, 4, W + 2 * D, W), bf16),
+            pltpu.VMEM(square, f32), pltpu.VMEM(square, f32),
+            pltpu.VMEM(square, bf16), pltpu.VMEM(square, f32), pltpu.VMEM((tokens_here, 1), f32),
+            pltpu.VMEM((4, 3, tokens_here, W), bf16), pltpu.VMEM((4, items_here, 2, SEQ, SEQ), bf16),
+            pltpu.VMEM((4, tokens_here, W), bf16), pltpu.VMEM(square, f32), pltpu.VMEM(square, f32),
+            pltpu.VMEM(square, bf16), pltpu.VMEM(square, f32), pltpu.VMEM((tokens_here, 1), f32),
+            pltpu.VMEM(square, bf16), pltpu.VMEM(square, f32), pltpu.VMEM(square, f32), pltpu.VMEM(square, bf16),
+            pltpu.VMEM(square, f32), pltpu.VMEM((4, QB + CB, R, W), bf16),
+            dma((4, QB + CB)), dma((2,)), dma((4, QB + CB)),
+        ],
+        compiler_params=pltpu.CompilerParams(vmem_limit_bytes=56 << 20),
+    )(tokens, cotangent, wide, narrow, meta, steps, bands, lens, owners)
+
+
+def reduce_kernel(
+    grads, out_delta, in_delta, norm_grads, total, out_all, in_all, norm_total,
+    held, from_core, rxa, rya, ryb, rxb, rz, n_core, n_x, n_y, n_z, norm_sum,
+    l_sem, c_s, c_r, xa_s, xa_r, ya_s, ya_r, yb_s, yb_r, xb_s, xb_r, z_s, z_r, n_s, n_r, o_s, o_r, o_l,
+):
+    z, y, x, c = place(Sizes)
+    nz = Sizes.z
+    x_peer, y_peer, core_peer = device(z, y, 1 - x, c), device(z, 1 - y, x, c), device(z, y, x, 1 - c)
+    z_peers = [device(lax.rem(z + k, nz), y, x, c) for k in range(1, nz)]
+    greet([x_peer, y_peer, core_peer] + z_peers)
+
+    def remote(src, dst, send, recv, peer):
+        return pltpu.make_async_remote_copy(
+            src_ref=src, dst_ref=dst, send_sem=send, recv_sem=recv, device_id=peer, device_id_type=MESH
+        )
+
+    sent = []
+
+    def push(*args):
+        copy = remote(*args)
+        copy.start()
+        sent.append(copy)
+
+    def wait_recv(dst, send, recv):
+        remote(dst, dst, send, recv, x_peer).wait_recv()
+
+    def chunk(k):
+        return lax.rem(z + 1 + k, nz)
+
+    here, far = x * 2 + c, (1 - x) * 2 + c
+    a_rows, b_rows = pl.ds(0, RA), pl.ds(RA, R - RA)
+    tokens_here = out_delta.shape[0]
+    head = x * 2 + c
+
+    def own_tokens(ref, who):
+        return ref.at[pl.ds(pl.multiple_of(who * tokens_here, tokens_here), tokens_here), :]
+
+    for k in range(nz):
+        zz = chunk(k)
+        for j in range(2):
+            mine, theirs = j * 2 + c, j * 2 + 1 - c
+            pltpu.make_async_copy(grads.at[mine, zz], held.at[j, zz], l_sem.at[k, j]).start()
+            push(grads.at[theirs, zz], from_core.at[j, zz], c_s.at[k, j], c_r.at[k, j], core_peer)
+
+    outs = ((out_delta, out_all), (in_delta, in_all))
+    for i, (src, dst) in enumerate(outs):
+        pltpu.make_async_copy(src, own_tokens(dst, head), o_l.at[i]).start()
+        push(src, own_tokens(dst, head), o_s.at[i, 0], o_r.at[i, 0], x_peer)
+        push(src, own_tokens(dst, head), o_s.at[i, 1], o_r.at[i, 1], core_peer)
+    push(norm_grads, n_core, n_s.at[0], n_r.at[0], core_peer)
+
+    def add(dst, src, rows, count):
+        for r in rows:
+            dst(r)[...] = dst(r)[...] + src(r)[...]
+
+    def stage0(k):
+        zz = chunk(k)
+        for j in range(2):
+            pltpu.make_async_copy(grads.at[j * 2 + c, zz], held.at[j, zz], l_sem.at[k, j]).wait()
+            wait_recv(from_core.at[j, zz], c_s.at[k, j], c_r.at[k, j])
+
+        def one(i, _):
+            j, yy, r = i // (2 * CAP), lax.rem(i // CAP, 2), lax.rem(i, CAP)
+            held[j, zz, yy, r] = held[j, zz, yy, r] + from_core[j, zz, yy, r]
+            return 0
+
+        lax.fori_loop(0, 2 * 2 * CAP, one, 0)
+        push(held.at[1 - x, zz, :, :, a_rows, :], rxa.at[zz], xa_s.at[k], xa_r.at[k], x_peer)
+        push(held.at[:, zz, 1 - y, :, b_rows, :], ryb.at[zz], yb_s.at[k], yb_r.at[k], y_peer)
+
+    def stage1(k):
+        zz = chunk(k)
+        wait_recv(rxa.at[zz], xa_s.at[k], xa_r.at[k])
+
+        def one(i, _):
+            yy, r = i // CAP, lax.rem(i, CAP)
+            held[x, zz, yy, r, a_rows, :] = held[x, zz, yy, r, a_rows, :] + rxa[zz, yy, r]
+            return 0
+
+        lax.fori_loop(0, 2 * CAP, one, 0)
+        push(held.at[x, zz, 1 - y, :, a_rows, :], rya.at[zz], ya_s.at[k], ya_r.at[k], y_peer)
+        wait_recv(ryb.at[zz], yb_s.at[k], yb_r.at[k])
+
+        def two(i, _):
+            j, r = i // CAP, lax.rem(i, CAP)
+            held[j, zz, y, r, b_rows, :] = held[j, zz, y, r, b_rows, :] + ryb[zz, j, r]
+            return 0
+
+        lax.fori_loop(0, 2 * CAP, two, 0)
+        push(held.at[1 - x, zz, y, :, b_rows, :], rxb.at[zz], xb_s.at[k], xb_r.at[k], x_peer)
+
+    def stage2(k):
+        zz = chunk(k)
+        wait_recv(rya.at[zz], ya_s.at[k], ya_r.at[k])
+        wait_recv(rxb.at[zz], xb_s.at[k], xb_r.at[k])
+
+        def one(r, _):
+            held[x, zz, y, r, a_rows, :] = held[x, zz, y, r, a_rows, :] + rya[zz, r]
+            held[x, zz, y, r, b_rows, :] = held[x, zz, y, r, b_rows, :] + rxb[zz, r]
+            return 0
+
+        lax.fori_loop(0, CAP, one, 0)
+        if k < nz - 1:
+            push(held.at[x, zz, y], rz.at[k], z_s.at[k], z_r.at[k], z_peers[k])
+
+    for step in range(nz + 2):
+        if step < nz:
+            stage0(step)
+        if step == 0:
+            wait_recv(n_core, n_s.at[0], n_r.at[0])
+            norm_sum[0] = norm_grads[...] + n_core[...]
+            push(norm_sum.at[0], n_x, n_s.at[1], n_r.at[1], x_peer)
+        if step == 1:
+            wait_recv(n_x, n_s.at[1], n_r.at[1])
+            norm_sum[1] = norm_sum[0] + n_x[...]
+            push(norm_sum.at[1], n_y, n_s.at[2], n_r.at[2], y_peer)
+        if step == 2:
+            wait_recv(n_y, n_s.at[2], n_r.at[2])
+            norm_sum[2] = norm_sum[1] + n_y[...]
+            for k, peer in enumerate(z_peers):
+                push(norm_sum.at[2], n_z.at[k], n_s.at[3 + k], n_r.at[3 + k], peer)
+            for i, (src, dst) in enumerate(outs):
+                whose = (1 - x) * 2 + c
+                wait_recv(own_tokens(dst, whose), o_s.at[i, 0], o_r.at[i, 0])
+                push(own_tokens(dst, whose), own_tokens(dst, whose), o_s.at[i, 2], o_r.at[i, 2], core_peer)
+        if 0 <= step - 1 < nz:
+            stage1(step - 1)
+        if 0 <= step - 2 < nz:
+            stage2(step - 2)
+
+    for k in range(nz - 1):
+        wait_recv(rz.at[k], z_s.at[k], z_r.at[k])
+        wait_recv(n_z.at[k], n_s.at[3 + k], n_r.at[3 + k])
+    norm_total[...] = norm_sum[2] + ((n_z[0] + n_z[1]) + n_z[2])
+
+    def last(r, _):
+        mine = held[x, z, y, r].astype(f32)
+        total[r] = mine + ((rz[0, r].astype(f32) + rz[1, r].astype(f32)) + rz[2, r].astype(f32))
+        return 0
+
+    lax.fori_loop(0, CAP, last, 0)
+    for i, (src, dst) in enumerate(outs):
+        pltpu.make_async_copy(src, own_tokens(dst, head), o_l.at[i]).wait()
+        for m, whose in ((1, x * 2 + 1 - c), (2, (1 - x) * 2 + 1 - c)):
+            wait_recv(own_tokens(dst, whose), o_s.at[i, m], o_r.at[i, m])
+    for copy in sent:
+        copy.wait_send()
+
+
+def reduce_gradients(grads, out_delta, in_delta, norm_grads, tokens_all):
+    nz = Sizes.z
+    grads = grads.reshape(4, nz, 2, CAP, R, W)
+    vm = pl.BlockSpec(memory_space=pltpu.VMEM)
+    hbm = pl.BlockSpec(memory_space=pl.ANY)
+    dma = pltpu.SemaphoreType.DMA
+    rb = R - RA
+    vec = pltpu.VMEM((8, D), f32)
+    return pl.pallas_call(
+        reduce_kernel,
+        name="reduce_gradients",
+        out_shape=(
+            jax.ShapeDtypeStruct((CAP, R, W), f32),
+            jax.ShapeDtypeStruct((tokens_all, D), bf16),
+            jax.ShapeDtypeStruct((tokens_all, D), bf16),
+            jax.ShapeDtypeStruct((8, D), f32),
+        ),
+        in_specs=[hbm, hbm, hbm, vm],
+        out_specs=(vm, hbm, hbm, vm),
+        scratch_shapes=[
+            pltpu.VMEM((2, nz, 2, CAP, R, W), bf16), pltpu.VMEM((2, nz, 2, CAP, R, W), bf16),
+            pltpu.VMEM((nz, 2, CAP, RA, W), bf16), pltpu.VMEM((nz, CAP, RA, W), bf16),
+            pltpu.VMEM((nz, 2, CAP, rb, W), bf16), pltpu.VMEM((nz, CAP, rb, W), bf16),
+            pltpu.VMEM((nz - 1, CAP, R, W), bf16),
+            vec, vec, vec, pltpu.VMEM((nz - 1, 8, D), f32), pltpu.VMEM((3, 8, D), f32),
+            dma((nz, 2)), dma((nz, 2)), dma((nz, 2)), dma((nz,)), dma((nz,)), dma((nz,)), dma((nz,)),
+            dma((nz,)), dma((nz,)), dma((nz,)), dma((nz,)), dma((nz,)), dma((nz,)), dma((8,)), dma((8,)),
+            dma((2, 3)), dma((2, 3)), dma((2,)),
+        ],
+        compiler_params=pltpu.CompilerParams(collective_id=1, has_side_effects=True, vmem_limit_bytes=48 << 20),
+    )(grads, out_delta, in_delta, norm_grads)
+
+
+def update_kernel(
+    total, norm_total, master, first, second, norm_master, norm_first, norm_second, owners,
+    new_master, new_first, new_second, new_norm, new_norm_first, new_norm_second, wide, narrow,
+):
+    dp = lax.axis_index("dp")
+    rows = block_rows(owners)
+    held = 0
+    for j in range(owners.shape[0]):
+        held = held + jnp.where(owners[j] == dp, 1, 0)
+    for r in range(CAP):
+        for p in range(3):
+            wide[pl.ds(p, W, stride=3), :] = total[r, p * W : (p + 1) * W, :]
+        for p in range(4):
+            narrow[pl.ds(p, R // 4, stride=4), :] = total[r, p * (R // 4) : (p + 1) * (R // 4), :]
+        grad = jnp.where(slot_is_wide(rows, dp * CAP + r), wide[...], narrow[...])
+        results = adamw_update(master[:, r, :], first[:, r, :], second[:, r, :], grad, weight_decay, learn_rate)
+        for ref, result in zip((new_master, new_first, new_second), results):
+            ref[:, r, :] = jnp.where(r < held, result, 0.0)
+    pair = norm_total[:, pl.ds(pl.multiple_of((dp // 2) * W, W), W)]
+    mine = jnp.where(lax.rem(dp, 2) == 1, pltpu.roll(pair, W // 2, 1), pair)[0:4, 0 : norm_master.shape[1]]
+    results = adamw_update(norm_master[...], norm_first[...], norm_second[...], mine, 0.0, norm_rate)
+    for ref, result in zip((new_norm, new_norm_first, new_norm_second), results):
+        ref[...] = result
+
+
+def update_owned(total, norm_total, slots, norms, owners):
+    vm = pl.BlockSpec(memory_space=pltpu.VMEM)
+    sm = pl.BlockSpec(memory_space=pltpu.SMEM)
+    return pl.pallas_call(
+        update_kernel,
+        name="update_owned",
+        out_shape=tuple(jax.ShapeDtypeStruct(a.shape, f32) for a in slots + norms),
+        in_specs=[vm] * 8 + [sm],
+        out_specs=(vm,) * 6,
+        scratch_shapes=[pltpu.VMEM((R, W), f32), pltpu.VMEM((R, W), f32)],
+        compiler_params=pltpu.CompilerParams(vmem_limit_bytes=24 << 20),
+    )(total, norm_total, *slots, *norms, owners)
+
+
+def fast_shards(
+    tokens, cotangent, timesteps, bands, lengths, owners,
+    master_slots, first_slots, second_slots, norm_master, norm_first, norm_second,
+):
+    def tiles(slots):
+        return jnp.transpose(slots.reshape(CAP, R, W), (1, 0, 2))
+
+    def flat(slots):
+        return jnp.transpose(slots, (1, 0, 2)).reshape(CAP, R * W)
+
+    steps, bands_row, lens_row = (v.reshape(1, -1) for v in (timesteps, bands, lengths))
+    slots = tuple(tiles(s) for s in (master_slots, first_slots, second_slots))
+    norms = (norm_master, norm_first, norm_second)
+    gathered, meta = gather_weights(slots[0], norm_master, steps, bands_row, lens_row, owners)
+    grads, out_delta, in_delta, norm_grads = compute_items(
+        tokens, cotangent, gathered, meta, steps, bands_row, lengths, owners
+    )
+    total, out_all, in_all, norm_total = reduce_gradients(grads, out_delta, in_delta, norm_grads, tokens.shape[0])
+    updated = update_owned(total, norm_total, slots, norms, owners)
+    table = bands[:, None] == jnp.arange(NBANDS, dtype=jnp.int32)[None, :]
+    sums = jnp.sum(meta[:, :, 64:66], axis=0)
+    weight_of = jnp.sum(jnp.where(table, sums[None, :, 0], 0.0), axis=1)
+    count_of = jnp.sum(jnp.where(table, sums[None, :, 1], 0.0), axis=1)
+    scale = jnp.exp(-2.0 * timesteps.astype(f32) / TSTEPS) * count_of / weight_of
+    valid = jnp.arange(SEQ, dtype=jnp.int32)[None, :] < lengths[:, None]
+    token_scale = jnp.where(valid, scale[:, None], 0.0).reshape(-1, 1)
+    return (
+        tokens + out_all.astype(f32),
+        cotangent * token_scale + in_all.astype(f32),
+        *(flat(s) for s in updated[:3]),
+        *updated[3:],
+    )
+
+
 def solution(mesh):
+    fits = dict(mesh.shape) == {"dp": 8, "head": 4}
     placed = (
         P("dp", None),
         P("dp", None),
@@ -286,7 +999,7 @@
         P(None, "dp"),
     )
     return jax.shard_map(
-        shards,
+        fast_shards if fits else shards,
         mesh=mesh,
         in_specs=placed,
         out_specs=(

time: 481 us -> 189 us (0.39); the launches traced: 472 us -> 189 us
  waiting for transfers between devices: 263 us -> 0 us
  Pallas kernels: 0 us -> 169 us
  blocking collectives: 62.9 us -> 0 us
  other arithmetic: 55.8 us -> 6.86 us
  matrix products: 41.4 us -> 0 us
  local copies, waits for them, and re-layouts: 33.8 us -> 11.7 us
  between operations: 14.9 us -> 0.84 us
    psum x4 -> x0, waiting for transfers between devices: 231 us -> none  [the longest x1 79.6 us: shards(): lax.psum(jnp.dot(activated_low, down_weight, preferred_element_type=jnp.f...]
    pallas_call x0 -> x4, Pallas kernels: none -> 169 us  [the longest x1 78.9 us: reduce_gradients(): pl.pallas_call(reduce_kernel, name='reduce_gradients', out_shape=(jax.Sha...]
    dot_general x18 -> x0, matrix products: 41.4 us -> none  [the longest x4 13.5 us: contract_cols(): lax.dot_general(left_side, right_side, (((1,), (1,)), ((), ())), preferre...]
    psum x2 -> x0, blocking collectives: 40.6 us -> none  [the longest x1 21.4 us: shards(): lax.psum(norm_grads.astype(jnp.bfloat16), 'dp').astype(jnp.float32)]
    all_gather x1 -> x0, waiting for transfers between devices: 32.1 us -> none  [shards(): lax.all_gather(master_slots.astype(jnp.bfloat16), 'dp', axis=0, tiled=True)]
    reduce_sum x12 -> x2, other arithmetic: 23 us -> 0.26 us  [the longest x1 0.18 us: fast_shards(): count_of = jnp.sum(jnp.where(table, sums[None, :, 1], 0.0), axis=1)]
    all_gather x1 -> x0, blocking collectives: 22.3 us -> none  [shards(): lax.all_gather(norm_master.astype(jnp.bfloat16), 'dp', axis=1, tiled=True)]
    reshape x10 -> x0, local copies, waits for them, and re-layouts: 10 us -> none  [the longest x2 5.49 us: shards(): contract_cols(grad_low_one, out_weight).astype(jnp.bfloat16)]
  transfers between devices with their start and end apart: 5 -> 0, of which waited for: 5 -> 0; matrix products, arithmetic and copies ran while one was open for 8% -> 0% of each run, Pallas kernels for 0% -> 0%
where the time goes in v1:
time: 189 us
  Pallas kernels  169 us (89%)
  local copies, waits for them, and re-layouts  11.7 us (6%)
  other arithmetic  6.86 us (4%)
    pallas_call x1, Pallas kernels, reduce_gradients(): pl.pallas_call(reduce_kernel, name='reduce_gradients', out_shape=(jax.Sha...  78.9 us
    pallas_call x1, Pallas kernels, gather_weights(): pl.pallas_call(gather_kernel, name='gather_weights', out_shape=(jax.Shape...  53.8 us
    pallas_call x1, Pallas kernels, compute_items(): pl.pallas_call(compute_kernel, name='compute_items', out_shape=(jax.Shape...  30.3 us
    unnamed x47, local copies, waits for them, and re-layouts  11.6 us
    add x1, other arithmetic, fast_shards(): cotangent * token_scale + in_all.astype(f32)  6.52 us
    pallas_call x1, Pallas kernels, update_owned(): pl.pallas_call(update_kernel, name='update_owned', out_shape=tuple((jax.S...  6.33 us

profile of v1, /device:TPU:0, one launch (start us, length us, event | category | flops | bytes accessed | tf_op | source)
XLA Modules:
  0.0 188.8 jit_solution(1164356294474713312)
XLA Ops:
  0.6 0.0 copy-start.1
  0.6 1.1 copy-done.1
  1.8 0.7 copy-done.10
  2.5 0.7 copy-done.12
  3.1 0.7 copy-done.14
  3.8 0.7 copy-done.16
  4.4 0.7 copy-done.18
  5.1 53.8 %gather_weights.1 = (bf16[4,4,2,3,384,128]{5,4,3,2,1,0:T(8,128)(2,1)S(1)}, f32[8,8,128]{2,1,0:T(8,128)S(1)}) custom-call(f32[384,3,128]{2,1,0:T(4,128)S(1)} %bitcast.29, f32[4,64]{1,0:T(4,128)S(1)} %copy-done.10, s32[1,8]{1,0:T(1,128)S(1)} %bitcast.37, s32[1,8]{1,0:T(1,128)S(1)} %bitcast.34, s32[1,8]{1,0:T(1,128)S(1)} %bitcast.35, s32[16]{0:T(128)S(1)} %copy-done.18), custom_call_target="tpu_custom_call" | custom-call | tf_op jit(solution)/shard_map/gather_weights/pallas_call | solution.py:445
  58.9 3.6 %copy-done = bf16[4,4,2,3,384,128]{5,4,3,2,1,0:T(8,128)(2,1)} copy-done((bf16[4,4,2,3,384,128]{5,4,3,2,1,0:T(8,128)(2,1)}, bf16[4,4,2,3,384,128]{5,4,3,2,1,0:T(8,128)(2,1)S(1)}, u32[]{:S(2)}) %copy-start) | copy-done | bytes 9437208
  62.6 0.6 copy-done.7
  63.2 30.3 %compute_items.1 = (bf16[4,24,384,128]{3,2,1,0:T(8,128)(2,1)}, bf16[512,512]{1,0:T(8,128)(2,1)}, bf16[512,512]{1,0:T(8,128)(2,1)}, f32[8,512]{1,0:T(8,128)}) custom-call(f32[2048,512]{1,0:T(8,128)} %tok_hbm.1, f32[2048,512]{1,0:T(8,128)} %cot_hbm.1, bf16[4,24,3,128,128]{4,3,2,1,0:T(8,128)(2,1)} %bitcast.27, bf16[4,24,4,96,128]{4,3,2,1,0:T(8,128)(2,1)} %bitcast.28, ...), custom_call_target="tpu_custom_call" | custom-call | tf_op jit(solution)/shard_map/compute_items/pallas_call | solution.py:704
  93.5 0.0 copy-start.5
  93.5 1.0 copy-done.5
  94.6 1.0 copy-done.6
  95.6 0.7 copy-done.9
  96.3 0.0 copy-start.19
  96.3 0.0 copy-start.20
  96.4 78.9 %reduce_gradients.1 = (f32[3,384,128]{2,1,0:T(8,128)S(1)}, bf16[2048,512]{1,0:T(8,128)(2,1)S(1)}, bf16[2048,512]{1,0:T(8,128)(2,1)S(1)}, f32[8,512]{1,0:T(8,128)S(1)}) custom-call(bf16[4,4,2,3,384,128]{5,4,3,2,1,0:T(8,128)(2,1)} %bitcast.38, bf16[512,512]{1,0:T(8,128)(2,1)S(1)} %copy-done.5, bf16[512,512]{1,0:T(8,128)(2,1)S(1)} %copy-done.6, ...), custom_call_target="tpu_custom_call" | custom-call | tf_op jit(solution)/shard_map/reduce_gradients/pallas_call | solution.py:887
  175.4 6.3 %update_owned.1 = (f32[384,3,128]{2,1,0:T(4,128)}, f32[384,3,128]{2,1,0:T(4,128)}, f32[384,3,128]{2,1,0:T(4,128)}, f32[4,64]{1,0:T(4,128)}, f32[4,64]{1,0:T(4,128)}, /*index=5*/f32[4,64]{1,0:T(4,128)}) custom-call(f32[3,384,128]{2,1,0:T(8,128)S(1)} %get-tuple-element.32.total, f32[8,512]{1,0:T(8,128)S(1)} %get-tuple-element.33.norm_total, ...), custom_call_target="tpu_custom_call" | custom-call | tf_op jit(solution)/shard_map/update_owned/pallas_call | solution.py:940
  181.8 0.1 slice_reduce_fusion
  181.8 0.2 slice_reduce_fusion.2
  182.0 0.2 select_reduce_fusion.1
  182.2 0.1 select_bitcast_fusion
  182.3 6.5 %convert_add_fusion = (f32[2048,512]{1,0:T(8,128)}, f32[2048,512]{1,0:T(8,128)}) fusion(bf16[2048,512]{1,0:T(8,128)(2,1)S(1)} %get-tuple-element.31, f32[2048,512]{1,0:T(8,128)} %cot_hbm.1, f32[2048]{0:T(1024)S(1)} %bitcast.39, f32[2048,512]{1,0:T(8,128)S(1)} %copy-done.22, bf16[2048,512]{1,0:T(8,128)(2,1)S(1)} %get-tuple-element.30), kind=kLoop, calls=%fused_computation | loop fusion | flops 5242880 | bytes 20979712 | tf_op jit(solution)/shard_map/add | solution.py:979
  (33 shorter events, 0.1 us)
Async XLA Ops:
  0.6 1.1 copy-start.1
  1.8 0.7 copy-start.10
  2.5 0.7 copy-start.12
  3.1 0.7 copy-start.14
  3.8 0.7 copy-start.16
  4.4 0.7 copy-start.18
  58.9 3.7 %copy-start = (bf16[4,4,2,3,384,128]{5,4,3,2,1,0:T(8,128)(2,1)}, bf16[4,4,2,3,384,128]{5,4,3,2,1,0:T(8,128)(2,1)S(1)}, u32[]{:S(2)}) copy-start(bf16[4,4,2,3,384,128]{5,4,3,2,1,0:T(8,128)(2,1)S(1)} %get-tuple-element.24) | copy-start | bytes 28311556
  62.6 0.6 copy-start.7
  93.5 1.0 copy-start.5
  94.6 1.0 copy-start.6
  95.6 0.7 copy-start.9
  96.3 79.0 %copy-start.2 = (f32[3,49152]{1,0:T(4,128)S(1)}, f32[3,49152]{1,0:T(4,128)}, u32[]{:S(2)}) copy-start(f32[3,49152]{1,0:T(4,128)} %param.18) | copy-start | bytes 1769476
  96.3 79.0 %copy-start.3 = (f32[3,49152]{1,0:T(4,128)S(1)}, f32[3,49152]{1,0:T(4,128)}, u32[]{:S(2)}) copy-start(f32[3,49152]{1,0:T(4,128)} %param.19) | copy-start | bytes 1769476
  96.3 79.0 %copy-start.4 = (f32[3,49152]{1,0:T(4,128)S(1)}, f32[3,49152]{1,0:T(4,128)}, u32[]{:S(2)}) copy-start(f32[3,49152]{1,0:T(4,128)} %param.20) | copy-start | bytes 1769476
  96.3 79.0 %copy-start.11 = (f32[4,64]{1,0:T(4,128)S(1)}, f32[4,64]{1,0:T(4,128)}, u32[]{:S(2)}) copy-start(f32[4,64]{1,0:T(4,128)} %norm_master.1) | copy-start | bytes 3076
  96.3 79.1 %copy-start.19 = (s32[16]{0:T(128)S(1)}, s32[16]{0:T(128)}, u32[]{:S(2)}) copy-start(s32[16]{0:T(128)} %owners.5) | copy-start | bytes 196
  96.3 79.1 %copy-start.20 = (f32[4,64]{1,0:T(4,128)S(1)}, f32[4,64]{1,0:T(4,128)}, u32[]{:S(2)}) copy-start(f32[4,64]{1,0:T(4,128)} %norm_first.1) | copy-start | bytes 3076
  96.4 79.1 %copy-start.21 = (f32[4,64]{1,0:T(4,128)S(1)}, f32[4,64]{1,0:T(4,128)}, u32[]{:S(2)}) copy-start(f32[4,64]{1,0:T(4,128)} %norm_second.1) | copy-start | bytes 3076
  96.4 85.4 %copy-start.8 = (f32[8,8,128]{2,1,0:T(8,128)S(1)}, f32[8,8,128]{2,1,0:T(8,128)}, u32[]{:S(2)}) copy-start(f32[8,8,128]{2,1,0:T(8,128)} %copy-done.7) | copy-start | bytes 98308
  96.4 85.6 %copy-start.13 = (s32[8]{0:T(128)S(1)}, s32[8]{0:T(128)}, u32[]{:S(2)}) copy-start(s32[8]{0:T(128)} %param.15) | copy-start | bytes 100
  96.4 85.8 %copy-start.17 = (s32[8]{0:T(128)S(1)}, s32[8]{0:T(128)}, u32[]{:S(2)}) copy-start(s32[8]{0:T(128)} %param.14) | copy-start | bytes 100
  96.4 85.8 %copy-start.15 = (s32[8]{0:T(128)S(1)}, s32[8]{0:T(128)}, u32[]{:S(2)}) copy-start(s32[8]{0:T(128)} %lens.1) | copy-start | bytes 100
  96.4 85.9 %copy-start.22 = (f32[2048,512]{1,0:T(8,128)S(1)}, f32[2048,512]{1,0:T(8,128)}, u32[]{:S(2)}) copy-start(f32[2048,512]{1,0:T(8,128)} %tok_hbm.1) | copy-start | bytes 12582916

commit v2 on v0

--- a/solution.py
+++ b/solution.py
@@ -3,6 +3,8 @@
 import jax
 import jax.numpy as jnp
 from jax import lax
+from jax.experimental import pallas as pl
+from jax.experimental.pallas import tpu as pltpu
 from jax.sharding import PartitionSpec as P
 
 D = 512
@@ -270,7 +272,677 @@
     )
 
 
+W = 128
+R = 384
+QB = 4
+CB = 12
+MESH = pl.DeviceIdType.MESH
+bf16 = jnp.bfloat16
+f32 = jnp.float32
+
+
+def place(sizes):
+    dp = lax.axis_index("dp")
+    head = lax.axis_index("head")
+    return dp // sizes.y, lax.rem(dp, sizes.y), head // sizes.c, lax.rem(head, sizes.c)
+
+
+class Sizes:
+    z, y, x, c = 4, 2, 2, 2
+
+
+def device(z, y, x, c):
+    return (z * Sizes.y + y, x * Sizes.c + c)
+
+
+def greet(partners):
+    barrier = pltpu.get_barrier_semaphore()
+    for partner in partners:
+        pl.semaphore_signal(barrier, inc=1, device_id=partner, device_id_type=MESH)
+    pl.semaphore_wait(barrier, len(partners))
+
+
+def block_rows(owners):
+    ids = [owners[j] for j in range(owners.shape[0])]
+    rows = []
+    for j, mine in enumerate(ids):
+        row = mine * CAP
+        for other in ids[:j]:
+            row = row + jnp.where(other == mine, 1, 0)
+        rows.append(row)
+    return rows
+
+
+def slot_is_wide(rows, slot_row):
+    flag = rows[0] == slot_row
+    for row in rows[1:QB]:
+        flag = jnp.logical_or(flag, row == slot_row)
+    return flag
+
+
+def dot(left, right):
+    return jnp.dot(left, right, preferred_element_type=f32)
+
+
+def dot_cols(left, right):
+    return lax.dot_general(left, right, (((1,), (1,)), ((), ())), preferred_element_type=f32)
+
+
+def dot_rows(left, right):
+    return lax.dot_general(left, right, (((0,), (0,)), ((), ())), preferred_element_type=f32)
+
+
+def normalise(values):
+    centred = values - jnp.mean(values, axis=-1, keepdims=True)
+    inverse = lax.rsqrt(jnp.mean(centred * centred, axis=-1, keepdims=True) + norm_eps)
+    return centred * inverse, inverse
+
+
+def panels(ref, h, first, size):
+    return jnp.concatenate([ref[h, p, first : first + size, :] for p in range(ref.shape[1])], axis=1)
+
+
+def cat_pieces(first, size):
+    pieces = []
+    row = first
+    while row < first + size:
+        block, inside = divmod(row, R // 4)
+        count = min(R // 4 - inside, first + size - row)
+        pieces.append((QB + block, inside, row - first, count))
+        row += count
+    return pieces
+
+
+RA = 192
+GA = 192
+
+
+def layer_kernel(
+    tok_hbm, cot_hbm, master_hbm, norms_hbm, steps_hbm, bands_hbm, lens_row_hbm, lens_hbm, owners_hbm,
+    total, out_all, in_all, norm_total,
+    wv, master, flat, own, mine, meta, norms_v, steps, bands, lens_row, lens, owners, block_at,
+    tok, cot, low1, xhat1, inv1, qkv, probs, att, acc, low2, xhat2, inv2, e2, da2, dx1, e1, da1, out_low, in_low,
+    theirs, held, from_core, rxa, sa, rya, sb, ryb, sbx, rxb, fz, rz, norm_part, norm_sum, n_core, n_x, n_y, n_z,
+    i_sem, z_s, z_r, ya_s, ya_r, xa_s, xa_r, xb_s, xb_r, yb_s, yb_r, core_s, core_r, m_s, m_r,
+    cs, cr, as_, ar, say_s, say_r, sby_s, sby_r, sbx_s, sbx_r, fz_s, fz_r, n_s, n_r, o_s, o_r, o_l,
+):
+    z, y, x, c = place(Sizes)
+    nz = Sizes.z
+    dp, head = z * 2 + y, x * 2 + c
+    dp_peers = [device(lax.rem(z + k, nz), (y + j) % 2, x, c) for k in range(nz) for j in range(2) if k or j]
+    z_peers = [device(lax.rem(z + k, nz), y, x, c) for k in range(1, nz)]
+    x_peer, y_peer, core_peer = device(z, y, 1 - x, c), device(z, 1 - y, x, c), device(z, y, x, 1 - c)
+    peers = dp_peers + [x_peer, core_peer]
+    barrier = pltpu.get_barrier_semaphore()
+    for peer in peers:
+        pl.semaphore_signal(barrier, inc=1, device_id=peer, device_id_type=MESH)
+
+    tokens_here = tok.shape[0]
+    items_here = tokens_here // SEQ
+    first_token = pl.multiple_of(head * tokens_here, tokens_here)
+    fetches = [
+        pltpu.make_async_copy(src, dst, i_sem.at[n])
+        for n, (src, dst) in enumerate((
+            (owners_hbm, owners), (master_hbm, master), (steps_hbm, steps), (bands_hbm, bands),
+            (lens_row_hbm, lens_row), (norms_hbm, norms_v), (lens_hbm, lens),
+            (tok_hbm.at[pl.ds(first_token, tokens_here), :], tok),
+            (cot_hbm.at[pl.ds(first_token, tokens_here), :], cot),
+        ))
+    ]
+    for fetch in fetches:
+        fetch.start()
+
+    def remote(src, dst, send, recv, peer):
+        return pltpu.make_async_remote_copy(
+            src_ref=src, dst_ref=dst, send_sem=send, recv_sem=recv, device_id=peer, device_id_type=MESH
+        )
+
+    sent = []
+
+    def push(*args):
+        copy = remote(*args)
+        copy.start()
+        sent.append(copy)
+
+    def wait_recv(dst, send, recv):
+        remote(dst, dst, send, recv, x_peer).wait_recv()
+
+    fetches[0].wait()
+    rows = block_rows(owners)
+    fetches[1].wait()
+    for r in range(CAP):
+        flat[...] = master[:, r, :]
+        wide = jnp.concatenate([flat[pl.ds(p, W, stride=3), :] for p in range(3)], axis=0)
+        narrow = jnp.concatenate([flat[pl.ds(p, R // 4, stride=4), :] for p in range(4)], axis=0)
+        own[r] = jnp.where(slot_is_wide(rows, dp * CAP + r), wide, narrow).astype(bf16)
+
+    for n in (2, 3, 4, 5):
+        fetches[n].wait()
+    items = steps.shape[1]
+    item_weight = jnp.exp(-2.0 * steps[...].astype(f32) / TSTEPS)
+    item_length = lens_row[...].astype(f32)
+    table = bands[...] == lax.broadcasted_iota(jnp.int32, (NBANDS, items), 0)
+    ones = table.astype(f32)
+    mine[...] = jnp.zeros_like(mine)
+    mine[0:4, 0 : W // 2] = norms_v[...]
+    mine[:, W // 2 : W // 2 + 1] = jnp.sum(ones * (item_weight * item_length), axis=1, keepdims=True)
+    mine[:, W // 2 + 1 : W // 2 + 2] = jnp.sum(ones * item_length, axis=1, keepdims=True)
+    meta[dp] = mine[...]
+
+    pl.semaphore_wait(barrier, len(peers))
+
+    shard, far = x * 2 + c, (1 - x) * 2 + c
+    part_a, part_b = pl.ds(0, GA), pl.ds(GA, R - GA)
+
+    def slab(sh, zz, yy, part=slice(None)):
+        return wv.at[sh, pl.ds((zz * 2 + yy) * CAP, CAP), part, :]
+
+    def order(k):
+        return (z, z + 1 - 2 * lax.rem(z, 2), 2 - z // 2, 3 - 3 * (z // 2))[k]
+
+    up, down, inner = z < nz - 1, z > 0, lax.rem(z, nz - 1) != 0
+    own_up = remote(own, slab(shard, z, y), z_s.at[0], z_r.at[z], device(z + 1, y, x, c))
+    own_down = remote(own, slab(shard, z, y), z_s.at[1], z_r.at[z], device(z - 1, y, x, c))
+    pl.when(up)(own_up.start)
+    pl.when(down)(own_down.start)
+    for k, peer in enumerate(dp_peers):
+        push(mine, meta.at[dp], m_s.at[k], m_r.at[k], peer)
+    on_ward = []
+
+    def gather0(k):
+        zz = order(k)
+        if k:
+            wait_recv(slab(shard, zz, y), z_s.at[0], z_r.at[zz])
+            goal = 3 - z if k == 1 else 3 * (z - 1)
+            copy = remote(slab(shard, zz, y), slab(shard, zz, y), z_s.at[1 + k], z_r.at[zz], device(goal, y, x, c))
+            pl.when(inner)(copy.start)
+            on_ward.append(copy)
+        whole = slab(shard, zz, y) if k else own
+        first, second = whole.at[:, part_a, :], whole.at[:, part_b, :]
+        push(first, slab(shard, zz, y, part_a), ya_s.at[k], ya_r.at[k], y_peer)
+        push(second, slab(shard, zz, y, part_b), xb_s.at[k], xb_r.at[k], x_peer)
+        push(second, slab(shard, zz, y, part_b), yb_s.at[k, 0], yb_r.at[k, 0], y_peer)
+        push(first, slab(shard, zz, y, part_a), xa_s.at[k, 0], xa_r.at[k, 0], x_peer)
+        push(whole, slab(shard, zz, y), core_s.at[k, 0], core_r.at[k, 0], core_peer)
+
+    def gather1(k):
+        zz = order(k)
+        there = slab(shard, zz, 1 - y, part_a)
+        wait_recv(there, ya_s.at[k], ya_r.at[k])
+        push(there, there, xa_s.at[k, 1], xa_r.at[k, 1], x_peer)
+        there = slab(far, zz, y, part_b)
+        wait_recv(there, xb_s.at[k], xb_r.at[k])
+        push(there, there, yb_s.at[k, 1], yb_r.at[k, 1], y_peer)
+        wait_recv(slab(shard, zz, 1 - y, part_b), yb_s.at[k, 0], yb_r.at[k, 0])
+        push(slab(shard, zz, 1 - y), slab(shard, zz, 1 - y), core_s.at[k, 1], core_r.at[k, 1], core_peer)
+
+    def gather2(k):
+        zz = order(k)
+        wait_recv(slab(far, zz, y, part_a), xa_s.at[k, 0], xa_r.at[k, 0])
+        push(slab(far, zz, y), slab(far, zz, y), core_s.at[k, 2], core_r.at[k, 2], core_peer)
+        wait_recv(slab(far, zz, 1 - y, part_a), xa_s.at[k, 1], xa_r.at[k, 1])
+        wait_recv(slab(far, zz, 1 - y, part_b), yb_s.at[k, 1], yb_r.at[k, 1])
+        push(slab(far, zz, 1 - y), slab(far, zz, 1 - y), core_s.at[k, 3], core_r.at[k, 3], core_peer)
+
+    own_copy = pltpu.make_async_copy(own, slab(shard, z, y), i_sem.at[9])
+    own_copy.start()
+    gather0(0)
+
+    for row in range(nz * 2 * CAP):
+        block = 0
+        for j, block_row in enumerate(rows):
+            block = block + jnp.where(block_row == row, j, 0)
+        block_at[row] = block
+    for k in range(len(dp_peers)):
+        wait_recv(meta.at[dp], m_s.at[k], m_r.at[k])
+    lane = lax.broadcasted_iota(jnp.int32, (8, W), 1)
+    chunks = []
+    for pair in range(meta.shape[0] // 2):
+        chunks.append(jnp.where(lane < W // 2, meta[2 * pair], pltpu.roll(meta[2 * pair + 1], W // 2, 1)))
+    norms = jnp.concatenate(chunks, axis=1).astype(bf16).astype(f32)
+    gain1, shift1, gain2, shift2 = (norms[i : i + 1, :] for i in range(4))
+    sums = meta[0]
+    for d in range(1, meta.shape[0]):
+        sums = sums + meta[d]
+    weight_of = jnp.sum(jnp.where(table, sums[:, W // 2 : W // 2 + 1], 0.0), axis=0, keepdims=True)
+    count_of = jnp.sum(jnp.where(table, sums[:, W // 2 + 1 : W // 2 + 2], 0.0), axis=0, keepdims=True)
+    scales = item_weight * count_of / weight_of
+    item_lane = lax.broadcasted_iota(jnp.int32, (1, items), 1)
+    position = lax.broadcasted_iota(jnp.int32, (SEQ, 1), 0)
+    fetches[6].wait()
+    columns = []
+    for i in range(items_here):
+        here = item_lane == head * items_here + i
+        scale = jnp.sum(jnp.where(here, scales, 0.0), axis=1, keepdims=True)
+        columns.append(jnp.where(position < lens[head * items_here + i], scale, 0.0))
+    fetches[7].wait()
+    scaled, inverse = normalise(tok[...])
+    xhat1[...] = scaled
+    inv1[...] = inverse
+    low1[...] = (scaled * gain1 + shift1).astype(bf16)
+    acc[...] = jnp.zeros_like(acc)
+    fetches[8].wait()
+    for i, column in enumerate(columns):
+        cot[i * SEQ : (i + 1) * SEQ, :] = cot[i * SEQ : (i + 1) * SEQ, :] * column
+    e2[...] = cot[...].astype(bf16)
+    own_copy.wait()
+
+    for step in range(1, nz + 2):
+        if step < nz:
+            gather0(step)
+        if step - 1 < nz:
+            gather1(step - 1)
+        if step >= 2:
+            gather2(step - 2)
+
+    def core_arrived(kinds):
+        for k in range(nz):
+            zz = order(k)
+            for kind in kinds:
+                sh = (x if kind < 2 else 1 - x) * 2 + 1 - c
+                wait_recv(slab(sh, zz, y if kind in (0, 2) else 1 - y), core_s.at[k, kind], core_r.at[k, kind])
+
+    head_lane = lax.broadcasted_iota(jnp.int32, (1, W), 1)
+    head_masks = [head_lane < HD, head_lane >= HD]
+    key_pos = lax.broadcasted_iota(jnp.int32, (1, SEQ), 1)
+
+    def only(values, a):
+        return jnp.where(head_masks[a], values, jnp.zeros_like(values))
+
+    def stack(values):
+        return jnp.concatenate([only(values, 0), only(values, 1)], axis=0)
+
+    def wide_matrix(h):
+        return jnp.concatenate(
+            [
+                jnp.concatenate([wv[h, rows[j], p * W : (p + 1) * W, :] for j in range(QB)], axis=0)
+                for p in range(3)
+            ],
+            axis=1,
+        )
+
+    def narrow_matrix(h, first, size):
+        pieces = cat_pieces(first, size)
+        return jnp.concatenate(
+            [
+                jnp.concatenate(
+                    [wv[h, rows[b], pl.ds(p * (R // 4) + inside, count), :] for b, inside, _, count in pieces], axis=0
+                )
+                for p in range(4)
+            ],
+            axis=1,
+        )
+
+    def attention(i, _):
+        h = lax.rem(x + i // 2, 2) * 2 + lax.rem(c + i, 2)
+        projected = dot(low1[...], wide_matrix(h))
+        qkv[h, 0] = (projected[:, :W].astype(bf16).astype(f32) * (1.0 / math.sqrt(HD))).astype(bf16)
+        qkv[h, 1] = projected[:, W : 2 * W].astype(bf16)
+        qkv[h, 2] = projected[:, 2 * W :].astype(bf16)
+        for i in range(items_here):
+            here = slice(i * SEQ, (i + 1) * SEQ)
+            query, key, value = qkv[h, 0, here, :], qkv[h, 1, here, :], qkv[h, 2, here, :]
+            valid = key_pos < lens[head * items_here + i]
+            both = []
+            for a in range(2):
+                scores = jnp.where(valid, dot_cols(only(query, a), key), -1e30)
+                exps = jnp.exp(scores - jnp.max(scores, axis=-1, keepdims=True))
+                prob = (exps * (1.0 / jnp.sum(exps, axis=-1, keepdims=True))).astype(bf16)
+                probs[h, i, a] = prob
+                both.append(prob)
+            att[h, here, :] = dot(jnp.concatenate(both, axis=1), stack(value)).astype(bf16)
+        acc[...] += dot(att[h], narrow_matrix(h, 0, W))
+        return 0
+
+    core_arrived((0, 1, 2, 3))
+    lax.fori_loop(0, 4, attention, 0)
+    acc[...] += tok[...]
+    scaled, inverse = normalise(acc[...])
+    xhat2[...] = scaled
+    inv2[...] = inverse
+    low2[...] = (scaled * gain2 + shift2).astype(bf16)
+    da2[...] = jnp.zeros_like(da2)
+
+    def shard_of(i):
+        return lax.rem(1 - x + i, 2) * 2 + (1 - c if i < 2 else c)
+
+    def put(dst, extra, first, result):
+        for block, inside, row, count in cat_pieces(first, result.shape[0]):
+            for p in range(4):
+                here = pl.ds(p * (R // 4) + inside, count)
+                part = result[row : row + count, p * W : (p + 1) * W]
+                if extra is not None and (block >= QB + 2 or first < W):
+                    part = part + extra[block, here, :].astype(f32)
+                dst[block, here, :] = part.astype(bf16)
+
+    def feed_forward(h, dst, extra):
+        up_matrix = narrow_matrix(h, W, D)
+        down_matrix = narrow_matrix(h, W + D, D)
+        hidden = dot(low2[...], up_matrix)
+        root = math.sqrt(2.0 / math.pi)
+        square = hidden * hidden
+        bend = jnp.tanh(root * hidden * (1.0 + 0.044715 * square))
+        half = 0.5 * (1.0 + bend)
+        active = (hidden * half).astype(bf16)
+        slope = half + 0.5 * hidden * (1.0 - bend * bend) * (root + (3.0 * 0.044715 * root) * square)
+        acc[...] += dot(active, down_matrix)
+        back = (dot_cols(e2[...], down_matrix) * slope).astype(bf16)
+        put(dst, extra, W + D, dot_rows(active, e2[...]))
+        put(dst, extra, W, dot_rows(low2[...], back))
+        da2[...] += dot_cols(back, up_matrix)
+
+    wide_blocks, deep_blocks = pl.ds(0, QB + 2), pl.ds(QB + 2, CB - 2)
+    x_part, y_part = pl.ds(0, RA), pl.ds(RA, R - RA)
+
+    def core_push(i, part, n):
+        return remote(theirs.at[i, part], from_core.at[i, part], cs.at[n, i], cr.at[n, i], core_peer)
+
+    def ff_theirs(i, _):
+        feed_forward(lax.rem(1 - x + i, 2) * 2 + 1 - c, theirs.at[i], None)
+        core_push(i, deep_blocks, 0).start()
+        return 0
+
+    def x_push(part, n):
+        return remote(held.at[0, part, x_part, :], rxa.at[part], as_.at[n], ar.at[n], x_peer)
+
+    def ff_mine(i, _):
+        core_push(i, deep_blocks, 0).wait_recv()
+        feed_forward(lax.rem(1 - x + i, 2) * 2 + c, held.at[i], from_core.at[i])
+        pl.when(i == 0)(x_push(deep_blocks, 0).start)
+        return 0
+
+    lax.fori_loop(0, 2, ff_theirs, 0)
+    lax.fori_loop(0, 2, ff_mine, 0)
+
+    def own_tokens(ref, who):
+        return ref.at[pl.ds(pl.multiple_of(who * tokens_here, tokens_here), tokens_here), :]
+
+    outs = ((out_low, out_all), (in_low, in_all))
+
+    def spread(i):
+        src, dst = outs[i]
+        pltpu.make_async_copy(src, own_tokens(dst, head), o_l.at[i]).start()
+        push(src, own_tokens(dst, head), o_s.at[i, 0], o_r.at[i, 0], x_peer)
+        push(src, own_tokens(dst, head), o_s.at[i, 1], o_r.at[i, 1], core_peer)
+
+    out_low[...] = acc[...].astype(bf16)
+    spread(0)
+
+    def norm_backward(grad, scaled, inverse, gain):
+        grad_scaled = grad * gain
+        centre = jnp.mean(grad_scaled, axis=-1, keepdims=True)
+        slope = jnp.mean(grad_scaled * scaled, axis=-1, keepdims=True)
+        return inverse * (grad_scaled - centre - scaled * slope)
+
+    grad2 = da2[...]
+    norm_part[...] = jnp.zeros_like(norm_part)
+    norm_part[2:3, :] = jnp.sum(grad2 * xhat2[...], axis=0, keepdims=True)
+    norm_part[3:4, :] = jnp.sum(grad2, axis=0, keepdims=True)
+    change = cot[...] + norm_backward(grad2, xhat2[...], inv2[...], gain2)
+    dx1[...] = change
+    e1[...] = change.astype(bf16)
+    da1[...] = jnp.zeros_like(da1)
+
+    def attention_back(h, dst, extra):
+        put(dst, extra, 0, dot_rows(att[h], e1[...]))
+        if extra is not None:
+            for p in range(4):
+                here = pl.ds(p * (R // 4) + W - R // 4, R // 2 - W)
+                dst[QB + 1, here, :] = dst[QB + 1, here, :] + extra[QB + 1, here, :]
+        d_att = dot_cols(e1[...], narrow_matrix(h, 0, W)).astype(bf16)
+        parts = []
+        for i in range(items_here):
+            here = slice(i * SEQ, (i + 1) * SEQ)
+            query, key, value = qkv[h, 0, here, :], qkv[h, 1, here, :], qkv[h, 2, here, :]
+            d_here = d_att[here, :]
+            shared = d_here.astype(f32) * att[h, here, :].astype(f32)
+            slopes = []
+            for a in range(2):
+                along = jnp.sum(only(shared, a), axis=-1, keepdims=True)
+                slopes.append((probs[h, i, a].astype(f32) * (dot_cols(only(d_here, a), value) - along)).astype(bf16))
+            tall = jnp.concatenate(slopes, axis=0)
+            d_query = dot(jnp.concatenate(slopes, axis=1), stack(key)) * (1.0 / math.sqrt(HD))
+            d_key = dot_rows(tall, stack(query))
+            d_value = dot_rows(jnp.concatenate([probs[h, i, 0], probs[h, i, 1]], axis=0), stack(d_here))
+            parts.append(jnp.concatenate([d_query, d_key, d_value], axis=1).astype(bf16))
+        d_qkv = jnp.concatenate(parts, axis=0)
+        d_weight = dot_rows(low1[...], d_qkv)
+        for j in range(QB):
+            for p in range(3):
+                part = d_weight[j * W : (j + 1) * W, p * W : (p + 1) * W]
+                if extra is not None:
+                    part = part + extra[j, p * W : (p + 1) * W, :].astype(f32)
+                dst[j, p * W : (p + 1) * W, :] = part.astype(bf16)
+        da1[...] += dot_cols(d_qkv, wide_matrix(h))
+
+    def att_theirs(i, _):
+        attention_back(lax.rem(1 - x + i, 2) * 2 + 1 - c, theirs.at[i], None)
+        core_push(i, wide_blocks, 1).start()
+        return 0
+
+    def att_mine(i, _):
+        core_push(i, wide_blocks, 1).wait_recv()
+        attention_back(lax.rem(1 - x + i, 2) * 2 + c, held.at[i], from_core.at[i])
+        pl.when(i == 0)(x_push(wide_blocks, 1).start)
+        return 0
+
+    lax.fori_loop(0, 2, att_theirs, 0)
+    lax.fori_loop(0, 2, att_mine, 0)
+
+    def chunk(k):
+        return lax.rem(z + 1 + k, nz)
+
+    def block_of(zz, yy, r):
+        return block_at[(zz * 2 + yy) * CAP + r]
+
+    for k in range(nz):
+        zz = chunk(k)
+        for j in range(2):
+            for r in range(CAP):
+                sb[k, j, r] = held[j, block_of(zz, 1 - y, r), y_part, :]
+        push(sb.at[k], ryb.at[k], sby_s.at[k], sby_r.at[k], y_peer)
+
+    grad1 = da1[...]
+    norm_part[0:1, :] = jnp.sum(grad1 * xhat1[...], axis=0, keepdims=True)
+    norm_part[1:2, :] = jnp.sum(grad1, axis=0, keepdims=True)
+    push(norm_part, n_core, n_s.at[0], n_r.at[0], core_peer)
+    in_low[...] = (dx1[...] + norm_backward(grad1, xhat1[...], inv1[...], gain1)).astype(bf16)
+
+    x_push(deep_blocks, 0).wait_recv()
+
+    def add_deep(j, _):
+        held[1, j, x_part, :] = held[1, j, x_part, :] + rxa[j]
+        return 0
+
+    lax.fori_loop(QB + 2, QB + CB, add_deep, 0)
+    x_push(wide_blocks, 1).wait_recv()
+    lax.fori_loop(0, QB + 2, add_deep, 0)
+    for k in range(nz):
+        zz = chunk(k)
+        for r in range(CAP):
+            sa[k, r] = held[1, block_of(zz, 1 - y, r), x_part, :]
+        push(sa.at[k], rya.at[k], say_s.at[k], say_r.at[k], y_peer)
+
+    def reduce1(k):
+        zz = chunk(k)
+        wait_recv(ryb.at[k], sby_s.at[k], sby_r.at[k])
+        for r in range(CAP):
+            sbx[k, r] = held[0, block_of(zz, y, r), y_part, :] + ryb[k, 0, r]
+        push(sbx.at[k], rxb.at[k], sbx_s.at[k], sbx_r.at[k], x_peer)
+
+    def reduce2(k):
+        zz = chunk(k)
+        wait_recv(rya.at[k], say_s.at[k], say_r.at[k])
+        for r in range(CAP):
+            fz[k, r, x_part, :] = held[1, block_of(zz, y, r), x_part, :] + rya[k, r]
+        wait_recv(rxb.at[k], sbx_s.at[k], sbx_r.at[k])
+        for r in range(CAP):
+            part = held[1, block_of(zz, y, r), y_part, :].astype(f32) + ryb[k, 1, r].astype(f32)
+            fz[k, r, y_part, :] = (part + rxb[k, r].astype(f32)).astype(bf16)
+        if k < nz - 1:
+            push(fz.at[k], rz.at[k], fz_s.at[k], fz_r.at[k], z_peers[k])
+
+    for k in range(nz):
+        reduce1(k)
+        if k == 0:
+            spread(1)
+            wait_recv(n_core, n_s.at[0], n_r.at[0])
+            norm_sum[0] = norm_part[...] + n_core[...]
+            push(norm_sum.at[0], n_x, n_s.at[1], n_r.at[1], x_peer)
+        if k == 1:
+            wait_recv(n_x, n_s.at[1], n_r.at[1])
+            norm_sum[1] = norm_sum[0] + n_x[...]
+            push(norm_sum.at[1], n_y, n_s.at[2], n_r.at[2], y_peer)
+        if k == 2:
+            wait_recv(n_y, n_s.at[2], n_r.at[2])
+            norm_sum[2] = norm_sum[1] + n_y[...]
+            for m, peer in enumerate(z_peers):
+                push(norm_sum.at[2], n_z.at[m], n_s.at[3 + m], n_r.at[3 + m], peer)
+        if k >= 1:
+            reduce2(k - 1)
+
+    def pass_on(i):
+        src, dst = outs[i]
+        there = own_tokens(dst, (1 - x) * 2 + c)
+        wait_recv(there, o_s.at[i, 0], o_r.at[i, 0])
+        push(there, there, o_s.at[i, 2], o_r.at[i, 2], core_peer)
+
+    pass_on(0)
+    reduce2(nz - 1)
+    pass_on(1)
+
+    for k in range(nz - 1):
+        wait_recv(rz.at[k], fz_s.at[k], fz_r.at[k])
+        wait_recv(n_z.at[k], n_s.at[3 + k], n_r.at[3 + k])
+    norm_total[...] = norm_sum[2] + ((n_z[0] + n_z[1]) + n_z[2])
+    for r in range(CAP):
+        others = (rz[0, r].astype(f32) + rz[1, r].astype(f32)) + rz[2, r].astype(f32)
+        total[r] = fz[nz - 1, r].astype(f32) + others
+    for i, (src, dst) in enumerate(outs):
+        pltpu.make_async_copy(src, own_tokens(dst, head), o_l.at[i]).wait()
+        for m, whose in ((1, x * 2 + 1 - c), (2, (1 - x) * 2 + 1 - c)):
+            wait_recv(own_tokens(dst, whose), o_s.at[i, m], o_r.at[i, m])
+    for copy in sent:
+        copy.wait_send()
+    for copy in on_ward:
+        pl.when(inner)(copy.wait_send)
+    pl.when(up)(own_up.wait_send)
+    pl.when(down)(own_down.wait_send)
+    for i in range(2):
+        core_push(i, deep_blocks, 0).wait_send()
+        core_push(i, wide_blocks, 1).wait_send()
+    x_push(deep_blocks, 0).wait_send()
+    x_push(wide_blocks, 1).wait_send()
+
+
+def layer(tokens, cotangent, master, norms, steps, bands, lens_row, lens, owners):
+    nz = Sizes.z
+    here = tokens.shape[0] // lax.axis_size("head")
+    items_here = here // SEQ
+    items = lens.shape[0]
+    vm = pl.BlockSpec(memory_space=pltpu.VMEM)
+    hbm = pl.BlockSpec(memory_space=pltpu.HBM)
+    dma = pltpu.SemaphoreType.DMA
+    V, S = pltpu.VMEM, pltpu.SMEM
+    square = (here, D)
+    blocks = QB + CB
+    rb = R - RA
+    low, full = V(square, bf16), V(square, f32)
+    scratch = [
+        V((4, nz * 2 * CAP, R, W), bf16), V((R, CAP, W), f32), V((R, W), f32), V((CAP, R, W), bf16),
+        V((8, W), f32), V((nz * 2, 8, W), f32), V(norms.shape, f32),
+        V((1, items), jnp.int32), V((1, items), jnp.int32), V((1, items), jnp.int32),
+        S((items,), jnp.int32), S(owners.shape, jnp.int32), S((nz * 2 * CAP,), jnp.int32),
+        full, full, low, full, V((here, 1), f32), V((4, 3, here, W), bf16),
+        V((4, items_here, 2, SEQ, SEQ), bf16), V((4, here, W), bf16), full, low, full, V((here, 1), f32),
+        low, full, full, low, full, low, low,
+        V((2, blocks, R, W), bf16), V((2, blocks, R, W), bf16), V((2, blocks, R, W), bf16),
+        V((blocks, RA, W), bf16), V((nz, CAP, RA, W), bf16), V((nz, CAP, RA, W), bf16),
+        V((nz, 2, CAP, rb, W), bf16), V((nz, 2, CAP, rb, W), bf16), V((nz, CAP, rb, W), bf16),
+        V((nz, CAP, rb, W), bf16), V((nz, CAP, R, W), bf16), V((nz - 1, CAP, R, W), bf16),
+        V((8, D), f32), V((3, 8, D), f32), V((8, D), f32), V((8, D), f32), V((8, D), f32), V((nz - 1, 8, D), f32),
+        dma((10,)), dma((5,)), dma((nz,)), dma((nz,)), dma((nz,)), dma((nz, 2)), dma((nz, 2)), dma((nz,)), dma((nz,)),
+        dma((nz, 2)), dma((nz, 2)), dma((nz, 4)), dma((nz, 4)), dma((8,)), dma((8,)),
+        dma((2, 2)), dma((2, 2)), dma((2,)), dma((2,)), dma((nz,)), dma((nz,)), dma((nz,)), dma((nz,)),
+        dma((nz,)), dma((nz,)), dma((nz,)), dma((nz,)), dma((8,)), dma((8,)), dma((2, 3)), dma((2, 3)), dma((2,)),
+    ]
+    return pl.pallas_call(
+        layer_kernel,
+        name="layer",
+        out_shape=(
+            jax.ShapeDtypeStruct((CAP, R, W), f32),
+            jax.ShapeDtypeStruct(tokens.shape, bf16),
+            jax.ShapeDtypeStruct(tokens.shape, bf16),
+            jax.ShapeDtypeStruct((8, D), f32),
+        ),
+        in_specs=[hbm] * 9,
+        out_specs=(vm, hbm, hbm, vm),
+        scratch_shapes=scratch,
+        compiler_params=pltpu.CompilerParams(collective_id=0, has_side_effects=True, vmem_limit_bytes=60 << 20),
+    )(tokens, cotangent, master, norms, steps, bands, lens_row, lens, owners)
+
+
+def update_kernel(
+    total, norm_total, master, first, second, norm_master, norm_first, norm_second, owners,
+    new_master, new_first, new_second, new_norm, new_norm_first, new_norm_second, wide, narrow,
+):
+    dp = lax.axis_index("dp")
+    rows = block_rows(owners)
+    held = 0
+    for j in range(owners.shape[0]):
+        held = held + jnp.where(owners[j] == dp, 1, 0)
+    for r in range(CAP):
+        for p in range(3):
+            wide[pl.ds(p, W, stride=3), :] = total[r, p * W : (p + 1) * W, :]
+        for p in range(4):
+            narrow[pl.ds(p, R // 4, stride=4), :] = total[r, p * (R // 4) : (p + 1) * (R // 4), :]
+        grad = jnp.where(slot_is_wide(rows, dp * CAP + r), wide[...], narrow[...])
+        results = adamw_update(master[:, r, :], first[:, r, :], second[:, r, :], grad, weight_decay, learn_rate)
+        for ref, result in zip((new_master, new_first, new_second), results):
+            ref[:, r, :] = jnp.where(r < held, result, 0.0)
+    pair = norm_total[:, pl.ds(pl.multiple_of((dp // 2) * W, W), W)]
+    mine = jnp.where(lax.rem(dp, 2) == 1, pltpu.roll(pair, W // 2, 1), pair)[0:4, 0 : norm_master.shape[1]]
+    results = adamw_update(norm_master[...], norm_first[...], norm_second[...], mine, 0.0, norm_rate)
+    for ref, result in zip((new_norm, new_norm_first, new_norm_second), results):
+        ref[...] = result
+
+
+def update_owned(total, norm_total, slots, norms, owners):
+    vm = pl.BlockSpec(memory_space=pltpu.VMEM)
+    sm = pl.BlockSpec(memory_space=pltpu.SMEM)
+    return pl.pallas_call(
+        update_kernel,
+        name="update_owned",
+        out_shape=tuple(jax.ShapeDtypeStruct(a.shape, f32) for a in slots + norms),
+        in_specs=[vm] * 8 + [sm],
+        out_specs=(vm,) * 6,
+        scratch_shapes=[pltpu.VMEM((R, W), f32), pltpu.VMEM((R, W), f32)],
+        compiler_params=pltpu.CompilerParams(vmem_limit_bytes=24 << 20),
+    )(total, norm_total, *slots, *norms, owners)
+
+
+def fast_shards(
+    tokens, cotangent, timesteps, bands, lengths, owners,
+    master_slots, first_slots, second_slots, norm_master, norm_first, norm_second,
+):
+    def tiles(slots):
+        return jnp.transpose(slots.reshape(CAP, R, W), (1, 0, 2))
+
+    def flat(slots):
+        return jnp.transpose(slots, (1, 0, 2)).reshape(CAP, R * W)
+
+    steps, bands_row, lens_row = (v.reshape(1, -1) for v in (timesteps, bands, lengths))
+    slots = tuple(tiles(s) for s in (master_slots, first_slots, second_slots))
+    norms = (norm_master, norm_first, norm_second)
+    total, out_all, in_all, norm_total = layer(
+        tokens, cotangent, slots[0], norm_master, steps, bands_row, lens_row, lengths, owners
+    )
+    updated = update_owned(total, norm_total, slots, norms, owners)
+    return (out_all.astype(f32), in_all.astype(f32), *(flat(s) for s in updated[:3]), *updated[3:])
+
+
 def solution(mesh):
+    fits = dict(mesh.shape) == {"dp": 8, "head": 4}
     placed = (
         P("dp", None),
         P("dp", None),
@@ -286,7 +958,7 @@
         P(None, "dp"),
     )
     return jax.shard_map(
-        shards,
+        fast_shards if fits else shards,
         mesh=mesh,
         in_specs=placed,
         out_specs=(

time: 481 us -> 153 us (0.32)
  the two profiles are of different devices: /device:TPU:0 before, /device:TPU:9 now
where the time goes in v2:
time: 153 us; the launch traced here: 152 us
  Pallas kernels  145 us (95%)
  other arithmetic  6.96 us (5%)
    pallas_call x1, Pallas kernels, layer(): pl.pallas_call(layer_kernel, name='layer', out_shape=(jax.ShapeDtypeStruc...  138 us
    pallas_call x1, Pallas kernels, update_owned(): pl.pallas_call(update_kernel, name='update_owned', out_shape=tuple((jax.S...  6.34 us
    convert_element_type x1, other arithmetic, fast_shards(): out_all.astype(f32)  4.35 us

profile of v2, /device:TPU:9, one launch (start us, length us, event | category | flops | bytes accessed | tf_op | source)
XLA Modules:
  0.0 152.4 jit_solution(10724236352802696537)
XLA Ops:
  0.6 138.3 %layer.1 = (f32[3,384,128]{2,1,0:T(8,128)}, bf16[2048,512]{1,0:T(8,128)(2,1)}, bf16[2048,512]{1,0:T(8,128)(2,1)}, f32[8,512]{1,0:T(8,128)}) custom-call(f32[2048,512]{1,0:T(8,128)} %tok_hbm.1, f32[2048,512]{1,0:T(8,128)} %cot_hbm.1, f32[384,3,128]{2,1,0:T(4,128)} %bitcast.21, f32[4,64]{1,0:T(4,128)} %norm_master.1, s32[1,8]{1,0:T(1,128)} %bitcast.26, ...), custom_call_target="tpu_custom_call" | custom-call | tf_op jit(solution)/shard_map/layer/pallas_call | solution.py:869
  138.9 0.0 copy-start.9
  138.9 4.3 %convert_element_type.6 = f32[2048,512]{1,0:T(8,128)} convert(bf16[2048,512]{1,0:T(8,128)(2,1)} %get-tuple-element.18) | non-fusion elementwise | flops 1048576 | bytes 6291456 | tf_op jit(solution)/shard_map/convert_element_type | solution.py:941
  143.3 0.0 copy-start
  143.3 0.0 copy-start.1
  143.3 0.0 copy-start.2
  143.3 0.0 copy-start.3
  143.3 0.0 copy-start.4
  143.3 0.0 copy-start.5
  143.3 0.0 copy-start.6
  143.3 0.0 copy-start.7
  143.3 0.0 copy-start.8
  143.4 0.0 copy-done.9
  143.4 2.6 %convert_element_type.7 = f32[2048,512]{1,0:T(8,128)} convert(bf16[2048,512]{1,0:T(8,128)(2,1)S(1)} %copy-done.9) | non-fusion elementwise | flops 1048576 | bytes 6291456 | tf_op jit(solution)/shard_map/convert_element_type | solution.py:941
  146.0 0.0 copy-done
  146.0 0.0 copy-done.1
  146.0 0.0 copy-done.2
  146.0 0.0 copy-done.3
  146.0 0.0 copy-done.4
  146.0 0.0 copy-done.5
  146.0 0.0 copy-done.6
  146.0 0.0 copy-done.7
  146.0 0.0 copy-done.8
  146.0 6.3 %update_owned.1 = (f32[384,3,128]{2,1,0:T(4,128)}, f32[384,3,128]{2,1,0:T(4,128)}, f32[384,3,128]{2,1,0:T(4,128)}, f32[4,64]{1,0:T(4,128)}, f32[4,64]{1,0:T(4,128)}, /*index=5*/f32[4,64]{1,0:T(4,128)}) custom-call(f32[3,384,128]{2,1,0:T(8,128)S(1)} %copy-done.3, f32[8,512]{1,0:T(8,128)S(1)} %copy-done.4, f32[384,3,128]{2,1,0:T(4,128)S(1)} %bitcast.22, ...), custom_call_target="tpu_custom_call" | custom-call | tf_op jit(solution)/shard_map/update_owned/pallas_call | solution.py:913
Async XLA Ops:
  138.9 4.4 %copy-start.9 = (bf16[2048,512]{1,0:T(8,128)(2,1)S(1)}, bf16[2048,512]{1,0:T(8,128)(2,1)}, u32[]{:S(2)}) copy-start(bf16[2048,512]{1,0:T(8,128)(2,1)} %get-tuple-element.19) | copy-start | bytes 6291460
  143.3 2.7 %copy-start = (f32[3,49152]{1,0:T(4,128)S(1)}, f32[3,49152]{1,0:T(4,128)}, u32[]{:S(2)}) copy-start(f32[3,49152]{1,0:T(4,128)} %param.18) | copy-start | bytes 1769476
  143.3 2.7 %copy-start.1 = (f32[3,49152]{1,0:T(4,128)S(1)}, f32[3,49152]{1,0:T(4,128)}, u32[]{:S(2)}) copy-start(f32[3,49152]{1,0:T(4,128)} %param.19) | copy-start | bytes 1769476
  143.3 2.7 %copy-start.2 = (f32[3,49152]{1,0:T(4,128)S(1)}, f32[3,49152]{1,0:T(4,128)}, u32[]{:S(2)}) copy-start(f32[3,49152]{1,0:T(4,128)} %param.20) | copy-start | bytes 1769476
  143.3 2.7 %copy-start.3 = (f32[3,384,128]{2,1,0:T(8,128)S(1)}, f32[3,384,128]{2,1,0:T(8,128)}, u32[]{:S(2)}) copy-start(f32[3,384,128]{2,1,0:T(8,128)} %get-tuple-element.20.total) | copy-start | bytes 1769476
  143.3 2.7 %copy-start.4 = (f32[8,512]{1,0:T(8,128)S(1)}, f32[8,512]{1,0:T(8,128)}, u32[]{:S(2)}) copy-start(f32[8,512]{1,0:T(8,128)} %get-tuple-element.21.norm_total) | copy-start | bytes 49156
  143.3 2.7 %copy-start.5 = (f32[4,64]{1,0:T(4,128)S(1)}, f32[4,64]{1,0:T(4,128)}, u32[]{:S(2)}) copy-start(f32[4,64]{1,0:T(4,128)} %norm_master.1) | copy-start | bytes 3076
  143.3 2.7 %copy-start.6 = (f32[4,64]{1,0:T(4,128)S(1)}, f32[4,64]{1,0:T(4,128)}, u32[]{:S(2)}) copy-start(f32[4,64]{1,0:T(4,128)} %norm_first.1) | copy-start | bytes 3076
  143.3 2.7 %copy-start.7 = (f32[4,64]{1,0:T(4,128)S(1)}, f32[4,64]{1,0:T(4,128)}, u32[]{:S(2)}) copy-start(f32[4,64]{1,0:T(4,128)} %norm_second.1) | copy-start | bytes 3076
  143.3 2.7 %copy-start.8 = (s32[16]{0:T(128)S(1)}, s32[16]{0:T(128)}, u32[]{:S(2)}) copy-start(s32[16]{0:T(128)} %owners.1) | copy-start | bytes 196

commit v3 on v0

--- a/solution.py
+++ b/solution.py
@@ -3,6 +3,8 @@
 import jax
 import jax.numpy as jnp
 from jax import lax
+from jax.experimental import pallas as pl
+from jax.experimental.pallas import tpu as pltpu
 from jax.sharding import PartitionSpec as P
 
 D = 512
@@ -270,7 +272,851 @@
     )
 
 
+W = 128
+R = 384
+QB = 4
+CB = 12
+MESH = pl.DeviceIdType.MESH
+bf16 = jnp.bfloat16
+f32 = jnp.float32
+
+
+def place(sizes):
+    dp = lax.axis_index("dp")
+    head = lax.axis_index("head")
+    return dp // sizes.y, lax.rem(dp, sizes.y), head // sizes.c, lax.rem(head, sizes.c)
+
+
+class Sizes:
+    z, y, x, c = 4, 2, 2, 2
+
+
+def device(z, y, x, c):
+    return (z * Sizes.y + y, x * Sizes.c + c)
+
+
+def greet(partners):
+    barrier = pltpu.get_barrier_semaphore()
+    for partner in partners:
+        pl.semaphore_signal(barrier, inc=1, device_id=partner, device_id_type=MESH)
+    pl.semaphore_wait(barrier, len(partners))
+
+
+def block_rows(owners):
+    ids = [owners[j] for j in range(owners.shape[0])]
+    rows = []
+    for j, mine in enumerate(ids):
+        row = mine * CAP
+        for other in ids[:j]:
+            row = row + jnp.where(other == mine, 1, 0)
+        rows.append(row)
+    return rows
+
+
+def slot_is_wide(rows, slot_row):
+    flag = rows[0] == slot_row
+    for row in rows[1:QB]:
+        flag = jnp.logical_or(flag, row == slot_row)
+    return flag
+
+
+def dot(left, right):
+    return jnp.dot(left, right, preferred_element_type=f32)
+
+
+def dot_cols(left, right):
+    return lax.dot_general(left, right, (((1,), (1,)), ((), ())), preferred_element_type=f32)
+
+
+def dot_rows(left, right):
+    return lax.dot_general(left, right, (((0,), (0,)), ((), ())), preferred_element_type=f32)
+
+
+def normalise(values):
+    centred = values - jnp.mean(values, axis=-1, keepdims=True)
+    inverse = lax.rsqrt(jnp.mean(centred * centred, axis=-1, keepdims=True) + norm_eps)
+    return centred * inverse, inverse
+
+
+def panels(ref, h, first, size):
+    return jnp.concatenate([ref[h, p, first : first + size, :] for p in range(ref.shape[1])], axis=1)
+
+
+def cat_pieces(first, size):
+    pieces = []
+    row = first
+    while row < first + size:
+        block, inside = divmod(row, R // 4)
+        count = min(R // 4 - inside, first + size - row)
+        pieces.append((QB + block, inside, row - first, count))
+        row += count
+    return pieces
+
+
+RA = 192
+GA = 192
+TILE = 128
+
+
+def layer_kernel(
+    tok_hbm, cot_hbm, master_hbm, norms_hbm, steps_hbm, bands_hbm, lens_row_hbm, lens_hbm, owners_hbm,
+    total, out_all, in_all, norm_total,
+    wv, master, flat, mine, meta, norms_v, steps, bands, lens_row, lens, owners, block_at,
+    tok, cot, low1, xhat1, inv1, qkv, probs, sums, att, acc, low2, xhat2, inv2, e2, actives, slopes, da, e1,
+    out_low, in_low,
+    grads, from_core, rxa, sa, rya, sb, ryb, sbx, rxb, fz, rz, norm_part, norm_sum, n_core, n_x, n_y, n_z,
+    i_sem, z_s, z_r, ya_s, ya_r, xa_s, xa_r, xb_s, xb_r, yb_s, yb_r, core_s, core_r, m_s, m_r,
+    cs, cr, as_, ar, say_s, say_r, sby_s, sby_r, sbx_s, sbx_r, fz_s, fz_r, n_s, n_r, o_s, o_r, o_l,
+):
+    z, y, x, c = place(Sizes)
+    nz = Sizes.z
+    dp, head = z * 2 + y, x * 2 + c
+    dp_peers = [device(lax.rem(z + k, nz), (y + j) % 2, x, c) for k in range(nz) for j in range(2) if k or j]
+    x_peer, y_peer, core_peer = device(z, y, 1 - x, c), device(z, 1 - y, x, c), device(z, y, x, 1 - c)
+    peers = dp_peers + [x_peer, core_peer]
+    barrier = pltpu.get_barrier_semaphore()
+    for peer in peers:
+        pl.semaphore_signal(barrier, inc=1, device_id=peer, device_id_type=MESH)
+
+    tokens_here = tok.shape[0]
+    items_here = tokens_here // SEQ
+    tiles = tokens_here // TILE
+    first_token = pl.multiple_of(head * tokens_here, tokens_here)
+    fetches = [
+        pltpu.make_async_copy(src, dst, i_sem.at[n])
+        for n, (src, dst) in enumerate((
+            (owners_hbm, owners), (master_hbm, master), (steps_hbm, steps), (bands_hbm, bands),
+            (lens_row_hbm, lens_row), (norms_hbm, norms_v), (lens_hbm, lens),
+            (tok_hbm.at[pl.ds(first_token, tokens_here), :], tok),
+            (cot_hbm.at[pl.ds(first_token, tokens_here), :], cot),
+        ))
+    ]
+    for fetch in fetches:
+        fetch.start()
+
+    def loop(first, last, body):
+        def step(i, _):
+            body(i)
+            return 0
+
+        lax.fori_loop(first, last, step, 0)
+
+    def remote(src, dst, send, recv, peer):
+        return pltpu.make_async_remote_copy(
+            src_ref=src, dst_ref=dst, send_sem=send, recv_sem=recv, device_id=peer, device_id_type=MESH
+        )
+
+    def same(ref, send, recv, peer):
+        return remote(ref, ref, send, recv, peer)
+
+    shard, far = x * 2 + c, (1 - x) * 2 + c
+    fetches[0].wait()
+    rows = block_rows(owners)
+    fetches[1].wait()
+    for r in range(CAP):
+        flat[...] = master[:, r, :]
+        wide = jnp.concatenate([flat[pl.ds(p, W, stride=3), :] for p in range(3)], axis=0)
+        narrow = jnp.concatenate([flat[pl.ds(p, R // 4, stride=4), :] for p in range(4)], axis=0)
+        wv[shard, dp * CAP + r] = jnp.where(slot_is_wide(rows, dp * CAP + r), wide, narrow).astype(bf16)
+
+    for n in (2, 3, 4, 5):
+        fetches[n].wait()
+    items = steps.shape[1]
+    item_weight = jnp.exp(-2.0 * steps[...].astype(f32) / TSTEPS)
+    item_length = lens_row[...].astype(f32)
+    table = bands[...] == lax.broadcasted_iota(jnp.int32, (NBANDS, items), 0)
+    ones = table.astype(f32)
+    mine[...] = jnp.zeros_like(mine)
+    mine[0:4, 0 : W // 2] = norms_v[...]
+    mine[:, W // 2 : W // 2 + 1] = jnp.sum(ones * (item_weight * item_length), axis=1, keepdims=True)
+    mine[:, W // 2 + 1 : W // 2 + 2] = jnp.sum(ones * item_length, axis=1, keepdims=True)
+    meta[dp] = mine[...]
+
+    pl.semaphore_wait(barrier, len(peers))
+
+    part_a, part_b = pl.ds(0, GA), pl.ds(GA, R - GA)
+
+    def slab(sh, zz, yy, part=slice(None)):
+        return wv.at[sh, pl.ds((zz * 2 + yy) * CAP, CAP), part, :]
+
+    def order(k):
+        late, low = k // 2, z // 2
+        return (1 - late) * (z + k * (1 - 2 * lax.rem(z, 2))) + late * (k + low * (3 - 2 * k))
+
+    up, down, inner = z < nz - 1, z > 0, lax.rem(z, nz - 1) != 0
+    own_up = same(slab(shard, z, y), z_s.at[0], z_r.at[z], device(z + 1, y, x, c))
+    own_down = same(slab(shard, z, y), z_s.at[nz], z_r.at[z], device(z - 1, y, x, c))
+    pl.when(up)(own_up.start)
+    pl.when(down)(own_down.start)
+
+    def meta_copy(k):
+        return remote(mine, meta.at[dp], m_s.at[k], m_r.at[k], dp_peers[k])
+
+    for k in range(len(dp_peers)):
+        meta_copy(k).start()
+
+    def along_z(k):
+        zz = order(k)
+        late = k // 2
+        goal = (1 - late) * (3 - z) + late * 3 * (z - 1)
+        return same(slab(shard, zz, y), z_s.at[k], z_r.at[zz], device(goal, y, x, c))
+
+    def first_copies(k):
+        zz = order(k)
+        one, two = slab(shard, zz, y, part_a), slab(shard, zz, y, part_b)
+        return (
+            same(one, ya_s.at[k], ya_r.at[k], y_peer),
+            same(two, xb_s.at[k], xb_r.at[k], x_peer),
+            same(two, yb_s.at[k, 0], yb_r.at[k, 0], y_peer),
+            same(one, xa_s.at[k, 0], xa_r.at[k, 0], x_peer),
+            same(slab(shard, zz, y), core_s.at[k, 0], core_r.at[k, 0], core_peer),
+        )
+
+    def second_copies(k):
+        zz = order(k)
+        return (
+            same(slab(shard, zz, 1 - y, part_a), xa_s.at[k, 1], xa_r.at[k, 1], x_peer),
+            same(slab(far, zz, y, part_b), yb_s.at[k, 1], yb_r.at[k, 1], y_peer),
+            same(slab(shard, zz, 1 - y), core_s.at[k, 1], core_r.at[k, 1], core_peer),
+        )
+
+    def third_copies(k):
+        zz = order(k)
+        return (
+            same(slab(far, zz, y), core_s.at[k, 2], core_r.at[k, 2], core_peer),
+            same(slab(far, zz, 1 - y), core_s.at[k, 3], core_r.at[k, 3], core_peer),
+        )
+
+    def gather0(k):
+        @pl.when(k > 0)
+        def _():
+            along_z(k).wait_recv()
+            pl.when(inner)(along_z(k).start)
+
+        for copy in first_copies(k):
+            copy.start()
+
+    def gather1(k):
+        zz = order(k)
+        over_x, over_y, core = second_copies(k)
+        same(slab(shard, zz, 1 - y, part_a), ya_s.at[k], ya_r.at[k], y_peer).wait_recv()
+        over_x.start()
+        same(slab(far, zz, y, part_b), xb_s.at[k], xb_r.at[k], x_peer).wait_recv()
+        over_y.start()
+        same(slab(shard, zz, 1 - y, part_b), yb_s.at[k, 0], yb_r.at[k, 0], y_peer).wait_recv()
+        core.start()
+
+    def gather2(k):
+        zz = order(k)
+        near, apart = third_copies(k)
+        same(slab(far, zz, y, part_a), xa_s.at[k, 0], xa_r.at[k, 0], x_peer).wait_recv()
+        near.start()
+        same(slab(far, zz, 1 - y, part_a), xa_s.at[k, 1], xa_r.at[k, 1], x_peer).wait_recv()
+        same(slab(far, zz, 1 - y, part_b), yb_s.at[k, 1], yb_r.at[k, 1], y_peer).wait_recv()
+        apart.start()
+
+    gather0(0)
+
+    def find_block(row):
+        block = 0
+        for j, block_row in enumerate(rows):
+            block = block + jnp.where(block_row == row, j, 0)
+        block_at[row] = block
+
+    loop(0, nz * 2 * CAP, find_block)
+    for k in range(len(dp_peers)):
+        meta_copy(k).wait_recv()
+    lane = lax.broadcasted_iota(jnp.int32, (8, W), 1)
+    chunks = []
+    for pair in range(meta.shape[0] // 2):
+        chunks.append(jnp.where(lane < W // 2, meta[2 * pair], pltpu.roll(meta[2 * pair + 1], W // 2, 1)))
+    norms = jnp.concatenate(chunks, axis=1).astype(bf16).astype(f32)
+    gain1, shift1, gain2, shift2 = (norms[i : i + 1, :] for i in range(4))
+    band_sums = meta[0]
+    for d in range(1, meta.shape[0]):
+        band_sums = band_sums + meta[d]
+    weight_of = jnp.sum(jnp.where(table, band_sums[:, W // 2 : W // 2 + 1], 0.0), axis=0, keepdims=True)
+    count_of = jnp.sum(jnp.where(table, band_sums[:, W // 2 + 1 : W // 2 + 2], 0.0), axis=0, keepdims=True)
+    scales = item_weight * count_of / weight_of
+    item_lane = lax.broadcasted_iota(jnp.int32, (1, items), 1)
+    position = lax.broadcasted_iota(jnp.int32, (TILE, 1), 0)
+    fetches[6].wait()
+    fetches[7].wait()
+    fetches[8].wait()
+
+    def tile(t):
+        return pl.ds(pl.multiple_of(t * TILE, TILE), TILE)
+
+    def first_norm(t):
+        here = tile(t)
+        scaled, inverse = normalise(tok[here, :])
+        xhat1[here, :] = scaled
+        inv1[here, :] = inverse
+        low1[here, :] = (scaled * gain1 + shift1).astype(bf16)
+        item = head * items_here + t // (SEQ // TILE)
+        scale = jnp.sum(jnp.where(item_lane == item, scales, 0.0), axis=1, keepdims=True)
+        inside = position + lax.rem(t, SEQ // TILE) * TILE < lens[item]
+        scaled_cot = cot[here, :] * jnp.where(inside, scale, 0.0)
+        cot[here, :] = scaled_cot
+        e2[here, :] = scaled_cot.astype(bf16)
+        acc[here, :] = jnp.zeros((TILE, D), f32)
+
+    loop(0, tiles, first_norm)
+
+    def gather(step):
+        pl.when(step < nz)(lambda: gather0(step))
+        pl.when(step <= nz)(lambda: gather1(step - 1))
+        pl.when(step >= 2)(lambda: gather2(step - 2))
+
+    loop(1, nz + 2, gather)
+
+    def all_here(k):
+        zz = order(k)
+        for kind, (xx, yy) in enumerate(((x, y), (x, 1 - y), (1 - x, y), (1 - x, 1 - y))):
+            same(slab(xx * 2 + 1 - c, zz, yy), core_s.at[k, kind], core_r.at[k, kind], core_peer).wait_recv()
+
+    loop(0, nz, all_here)
+
+    head_lane = lax.broadcasted_iota(jnp.int32, (1, W), 1)
+    head_masks = [head_lane < HD, head_lane >= HD]
+    key_pos = lax.broadcasted_iota(jnp.int32, (1, SEQ), 1)
+    item_rows = [slice(i * SEQ, (i + 1) * SEQ) for i in range(items_here)]
+
+    def only(values, a):
+        return jnp.where(head_masks[a], values, jnp.zeros_like(values))
+
+    def stack(values):
+        return jnp.concatenate([only(values, 0), only(values, 1)], axis=0)
+
+    def wide_matrix(h):
+        return jnp.concatenate(
+            [
+                jnp.concatenate([wv[h, rows[j], p * W : (p + 1) * W, :] for j in range(QB)], axis=0)
+                for p in range(3)
+            ],
+            axis=1,
+        )
+
+    def narrow_matrix(h, first, size):
+        pieces = cat_pieces(first, size)
+        return jnp.concatenate(
+            [
+                jnp.concatenate(
+                    [wv[h, rows[b], pl.ds(p * (R // 4) + inside, count), :] for b, inside, _, count in pieces], axis=0
+                )
+                for p in range(4)
+            ],
+            axis=1,
+        )
+
+    key_row = lax.broadcasted_iota(jnp.int32, (2 * SEQ, W), 0)
+    head_ones = jnp.where((key_row < SEQ) == head_masks[0], 1.0, 0.0).astype(bf16)
+
+    def attention(h):
+        projected = dot(low1[...], wide_matrix(h))
+        qkv[h, 0] = (projected[:, :W].astype(bf16).astype(f32) * (1.0 / math.sqrt(HD))).astype(bf16)
+        qkv[h, 1] = projected[:, W : 2 * W].astype(bf16)
+        qkv[h, 2] = projected[:, 2 * W :].astype(bf16)
+        for i, here in enumerate(item_rows):
+            query, key, value = qkv[h, 0, here, :], qkv[h, 1, here, :], qkv[h, 2, here, :]
+            valid = key_pos < lens[head * items_here + i]
+            both = []
+            for a in range(2):
+                scores = jnp.where(valid, dot_cols(only(query, a), key), -1e30)
+                exps = jnp.exp(scores - jnp.max(scores, axis=-1, keepdims=True)).astype(bf16)
+                probs[h, i, a] = exps
+                both.append(exps)
+            mixed = dot(jnp.concatenate(both, axis=1), jnp.concatenate([stack(value), head_ones], axis=1))
+            inverse = 1.0 / mixed[:, W:]
+            sums[h, here, :] = inverse
+            att[h, here, :] = (mixed[:, :W] * inverse).astype(bf16)
+        acc[...] += dot(att[h], narrow_matrix(h, 0, W))
+
+    loop(0, 4, attention)
+
+    def second_norm(t):
+        here = tile(t)
+        state = acc[here, :] + tok[here, :]
+        acc[here, :] = state
+        scaled, inverse = normalise(state)
+        xhat2[here, :] = scaled
+        inv2[here, :] = inverse
+        low2[here, :] = (scaled * gain2 + shift2).astype(bf16)
+        da[here, :] = jnp.zeros((TILE, D), f32)
+
+    loop(0, tiles, second_norm)
+
+    def shard_of(i):
+        return lax.rem(1 - x + i, 2) * 2 + lax.rem(c + 1 + i // 2, 2)
+
+    def feed_forward(i):
+        h = shard_of(i)
+        hidden = dot(low2[...], narrow_matrix(h, W, D))
+        root = math.sqrt(2.0 / math.pi)
+        square = hidden * hidden
+        bend = jnp.tanh(root * hidden * (1.0 + 0.044715 * square))
+        half = 0.5 * (1.0 + bend)
+        active = (hidden * half).astype(bf16)
+        slope = half + 0.5 * hidden * (1.0 - bend * bend) * (root + (3.0 * 0.044715 * root) * square)
+        actives[i] = active
+        slopes[i] = slope.astype(bf16)
+        acc[...] += dot(active, narrow_matrix(h, W + D, D))
+
+    loop(0, 4, feed_forward)
+
+    def own_tokens(ref, who):
+        return ref.at[pl.ds(pl.multiple_of(who * tokens_here, tokens_here), tokens_here), :]
+
+    outs = ((out_low, out_all), (in_low, in_all))
+
+    def out_copies(i):
+        src, dst = outs[i]
+        there, across = own_tokens(dst, head), own_tokens(dst, (1 - x) * 2 + c)
+        return (
+            pltpu.make_async_copy(src, there, o_l.at[i]),
+            remote(src, there, o_s.at[i, 0], o_r.at[i, 0], x_peer),
+            remote(src, there, o_s.at[i, 1], o_r.at[i, 1], core_peer),
+            same(across, o_s.at[i, 2], o_r.at[i, 2], core_peer),
+        )
+
+    out_low[...] = acc[...].astype(bf16)
+    for copy in out_copies(0)[:3]:
+        copy.start()
+
+    def put(i, first, result):
+        for block, inside, row, count in cat_pieces(first, result.shape[0]):
+            for p in range(4):
+                here = pl.ds(p * (R // 4) + inside, count)
+                grads[i, block, here, :] = result[row : row + count, p * W : (p + 1) * W].astype(bf16)
+
+    deep, low = (QB + 2, CB - 2), (0, QB + 2)
+    x_part, y_part = pl.ds(0, RA), pl.ds(RA, R - RA)
+
+    def core_push(i, n):
+        part = pl.ds(*(deep, low)[n])
+        return remote(grads.at[i, part], from_core.at[i, part], cs.at[n, i], cr.at[n, i], core_peer)
+
+    def x_push(n):
+        part = pl.ds(*(deep, low)[n])
+        return remote(grads.at[2, part, x_part, :], rxa.at[part], as_.at[n], ar.at[n], x_peer)
+
+    def hand_over(i, n):
+        first, count = (deep, low)[n]
+        pl.when(i < 2)(lambda: core_push(i, n).start())
+
+        @pl.when(i >= 2)
+        def _():
+            core_push(i - 2, n).wait_recv()
+
+            def add(j):
+                grads[i, j] = grads[i, j] + from_core[i - 2, j]
+
+            loop(first, first + count, add)
+            pl.when(i == 2)(lambda: x_push(n).start())
+
+    def feed_forward_back(i):
+        h = shard_of(i)
+        back = (dot_cols(e2[...], narrow_matrix(h, W + D, D)) * slopes[i].astype(f32)).astype(bf16)
+        put(i, W + D, dot_rows(actives[i], e2[...]))
+        put(i, W, dot_rows(low2[...], back))
+        da[...] += dot_cols(back, narrow_matrix(h, W, D))
+        hand_over(i, 0)
+
+    loop(0, 4, feed_forward_back)
+
+    def norm_backward(grad, scaled, inverse, gain):
+        grad_scaled = grad * gain
+        centre = jnp.mean(grad_scaled, axis=-1, keepdims=True)
+        slope = jnp.mean(grad_scaled * scaled, axis=-1, keepdims=True)
+        return inverse * (grad_scaled - centre - scaled * slope)
+
+    norm_part[...] = jnp.zeros_like(norm_part)
+
+    def second_norm_back(t):
+        here = tile(t)
+        grad, scaled = da[here, :], xhat2[here, :]
+        norm_part[2:3, :] += jnp.sum(grad * scaled, axis=0, keepdims=True)
+        norm_part[3:4, :] += jnp.sum(grad, axis=0, keepdims=True)
+        change = cot[here, :] + norm_backward(grad, scaled, inv2[here, :], gain2)
+        cot[here, :] = change
+        e1[here, :] = change.astype(bf16)
+        da[here, :] = jnp.zeros((TILE, D), f32)
+
+    loop(0, tiles, second_norm_back)
+
+    def attention_back(i):
+        h = shard_of(i)
+        put(i, 0, dot_rows(att[h], e1[...]))
+        d_all = dot_cols(e1[...], narrow_matrix(h, 0, W)) * sums[h]
+        shared_all = (d_all * att[h].astype(f32)).astype(bf16)
+        d_all = d_all.astype(bf16)
+        parts = []
+        for m, here in enumerate(item_rows):
+            query, key, value = qkv[h, 0, here, :], qkv[h, 1, here, :], qkv[h, 2, here, :]
+            d_here, shared = d_all[here, :], shared_all[here, :]
+            against = jnp.concatenate([value, jnp.full((SEQ, W), -1.0, bf16)], axis=1)
+            d_scores = []
+            for a in range(2):
+                change = dot_cols(jnp.concatenate([only(d_here, a), only(shared, a)], axis=1), against)
+                d_scores.append((probs[h, m, a].astype(f32) * change).astype(bf16))
+            d_query = dot(jnp.concatenate(d_scores, axis=1), stack(key)) * (1.0 / math.sqrt(HD))
+            d_key = dot_rows(jnp.concatenate(d_scores, axis=0), stack(query))
+            d_value = dot_rows(jnp.concatenate([probs[h, m, 0], probs[h, m, 1]], axis=0), stack(d_here))
+            parts.append(jnp.concatenate([d_query, d_key, d_value], axis=1).astype(bf16))
+        d_qkv = jnp.concatenate(parts, axis=0)
+        d_weight = dot_rows(low1[...], d_qkv).astype(bf16)
+        for j in range(QB):
+            for p in range(3):
+                grads[i, j, p * W : (p + 1) * W, :] = d_weight[j * W : (j + 1) * W, p * W : (p + 1) * W]
+        da[...] += dot_cols(d_qkv, wide_matrix(h))
+        hand_over(i, 1)
+
+    loop(0, 4, attention_back)
+
+    def chunk(k):
+        return lax.rem(z + 1 + k, nz)
+
+    def block_of(k, yy, r):
+        return block_at[(chunk(k) * 2 + yy) * CAP + r]
+
+    def over_y_first(k):
+        return remote(sb.at[k], ryb.at[k], sby_s.at[k], sby_r.at[k], y_peer)
+
+    def over_x_last(k):
+        return remote(sbx.at[k], rxb.at[k], sbx_s.at[k], sbx_r.at[k], x_peer)
+
+    def over_y_last(k):
+        return remote(sa.at[k], rya.at[k], say_s.at[k], say_r.at[k], y_peer)
+
+    def over_z(k):
+        return remote(fz.at[k], rz.at[k], fz_s.at[k], fz_r.at[k], device(chunk(k), y, x, c))
+
+    def send_b(k):
+        for r in range(CAP):
+            block = block_of(k, 1 - y, r)
+            for j in range(2):
+                sb[k, j, r] = grads[2 + j, block, y_part, :]
+        over_y_first(k).start()
+
+    loop(0, nz, send_b)
+
+    def first_norm_back(t):
+        here = tile(t)
+        grad, scaled = da[here, :], xhat1[here, :]
+        norm_part[0:1, :] += jnp.sum(grad * scaled, axis=0, keepdims=True)
+        norm_part[1:2, :] += jnp.sum(grad, axis=0, keepdims=True)
+        in_low[here, :] = (cot[here, :] + norm_backward(grad, scaled, inv1[here, :], gain1)).astype(bf16)
+
+    loop(0, tiles, first_norm_back)
+    for copy in out_copies(1)[:3]:
+        copy.start()
+
+    def norm_copies():
+        z_peers = [device(lax.rem(z + k, nz), y, x, c) for k in range(1, nz)]
+        return [
+            remote(norm_part, n_core, n_s.at[0], n_r.at[0], core_peer),
+            remote(norm_sum.at[0], n_x, n_s.at[1], n_r.at[1], x_peer),
+            remote(norm_sum.at[1], n_y, n_s.at[2], n_r.at[2], y_peer),
+        ] + [remote(norm_sum.at[2], n_z.at[k], n_s.at[3 + k], n_r.at[3 + k], p) for k, p in enumerate(z_peers)]
+
+    norm_copies()[0].start()
+
+    for n in range(2):
+        x_push(n).wait_recv()
+
+    def add_x(j):
+        grads[3, j, x_part, :] = grads[3, j, x_part, :] + rxa[j]
+
+    loop(0, QB + CB, add_x)
+
+    def send_a(k):
+        for r in range(CAP):
+            sa[k, r] = grads[3, block_of(k, 1 - y, r), x_part, :]
+        over_y_last(k).start()
+
+    loop(0, nz, send_a)
+
+    norm_copies()[0].wait_recv()
+    norm_sum[0] = norm_part[...] + n_core[...]
+    norm_copies()[1].start()
+
+    def reduce1(k):
+        over_y_first(k).wait_recv()
+        for r in range(CAP):
+            sbx[k, r] = grads[2, block_of(k, y, r), y_part, :] + ryb[k, 0, r]
+        over_x_last(k).start()
+
+    def reduce2(k):
+        over_y_last(k).wait_recv()
+        over_x_last(k).wait_recv()
+        for r in range(CAP):
+            block = block_of(k, y, r)
+            fz[k, r, x_part, :] = grads[3, block, x_part, :] + rya[k, r]
+            part = grads[3, block, y_part, :].astype(f32) + ryb[k, 1, r].astype(f32)
+            fz[k, r, y_part, :] = (part + rxb[k, r].astype(f32)).astype(bf16)
+        pl.when(k < nz - 1)(lambda: over_z(k).start())
+
+    def reduce_step(k):
+        pl.when(k < nz)(lambda: reduce1(k))
+        pl.when(k >= 1)(lambda: reduce2(k - 1))
+
+    loop(0, 2, reduce_step)
+    norm_copies()[1].wait_recv()
+    norm_sum[1] = norm_sum[0] + n_x[...]
+    norm_copies()[2].start()
+    for i in range(2):
+        if i == 0:
+            out_copies(i)[1].wait_recv()
+            out_copies(i)[3].start()
+    loop(2, 4, reduce_step)
+    norm_copies()[2].wait_recv()
+    norm_sum[2] = norm_sum[1] + n_y[...]
+    for copy in norm_copies()[3:]:
+        copy.start()
+    loop(4, nz + 1, reduce_step)
+    out_copies(1)[1].wait_recv()
+    out_copies(1)[3].start()
+
+    for k in range(nz - 1):
+        over_z(k).wait_recv()
+        norm_copies()[3 + k].wait_recv()
+    norm_total[...] = norm_sum[2] + ((n_z[0] + n_z[1]) + n_z[2])
+
+    def last(r):
+        others = (rz[0, r].astype(f32) + rz[1, r].astype(f32)) + rz[2, r].astype(f32)
+        total[r] = fz[nz - 1, r].astype(f32) + others
+
+    loop(0, CAP, last)
+
+    for i in range(2):
+        local, _, over_core, again = out_copies(i)
+        local.wait()
+        over_core.wait_recv()
+        again.wait_recv()
+        for copy in out_copies(i)[1:]:
+            copy.wait_send()
+    for copy in norm_copies():
+        copy.wait_send()
+    for k in range(len(dp_peers)):
+        meta_copy(k).wait_send()
+    pl.when(up)(own_up.wait_send)
+    pl.when(down)(own_down.wait_send)
+
+    def sent(k):
+        for copy in first_copies(k) + second_copies(k) + third_copies(k):
+            copy.wait_send()
+        pl.when(jnp.logical_and(k > 0, inner))(along_z(k).wait_send)
+        for copy in (over_y_first(k), over_x_last(k), over_y_last(k)):
+            copy.wait_send()
+        pl.when(k < nz - 1)(over_z(k).wait_send)
+
+    loop(0, nz, sent)
+    for n in range(2):
+        x_push(n).wait_send()
+        for i in range(2):
+            core_push(i, n).wait_send()
+
+
+def layer(tokens, cotangent, master, norms, steps, bands, lens_row, lens, owners):
+    nz = Sizes.z
+    here = tokens.shape[0] // lax.axis_size("head")
+    items_here = here // SEQ
+    items = lens.shape[0]
+    vm = pl.BlockSpec(memory_space=pltpu.VMEM)
+    hbm = pl.BlockSpec(memory_space=pltpu.HBM)
+    dma = pltpu.SemaphoreType.DMA
+    V, S = pltpu.VMEM, pltpu.SMEM
+    square = (here, D)
+    blocks = QB + CB
+    rb = R - RA
+    low, full = V(square, bf16), V(square, f32)
+    scratch = [
+        V((4, nz * 2 * CAP, R, W), bf16), V((R, CAP, W), f32), V((R, W), f32),
+        V((8, W), f32), V((nz * 2, 8, W), f32), V(norms.shape, f32),
+        V((1, items), jnp.int32), V((1, items), jnp.int32), V((1, items), jnp.int32),
+        S((items,), jnp.int32), S(owners.shape, jnp.int32), S((nz * 2 * CAP,), jnp.int32),
+        full, full, low, full, V((here, 1), f32), V((4, 3, here, W), bf16),
+        V((4, items_here, 2, SEQ, SEQ), bf16), V((4, here, W), f32), V((4, here, W), bf16),
+        full, low, full, V((here, 1), f32), low, V((4, here, D), bf16), V((4, here, D), bf16), full, low, low, low,
+        V((4, blocks, R, W), bf16), V((2, blocks, R, W), bf16),
+        V((blocks, RA, W), bf16), V((nz, CAP, RA, W), bf16), V((nz, CAP, RA, W), bf16),
+        V((nz, 2, CAP, rb, W), bf16), V((nz, 2, CAP, rb, W), bf16), V((nz, CAP, rb, W), bf16),
+        V((nz, CAP, rb, W), bf16), V((nz, CAP, R, W), bf16), V((nz - 1, CAP, R, W), bf16),
+        V((8, D), f32), V((3, 8, D), f32), V((8, D), f32), V((8, D), f32), V((8, D), f32), V((nz - 1, 8, D), f32),
+        dma((9,)), dma((nz + 1,)), dma((nz,)), dma((nz,)), dma((nz,)), dma((nz, 2)), dma((nz, 2)), dma((nz,)), dma((nz,)),
+        dma((nz, 2)), dma((nz, 2)), dma((nz, 4)), dma((nz, 4)), dma((8,)), dma((8,)),
+        dma((2, 2)), dma((2, 2)), dma((2,)), dma((2,)), dma((nz,)), dma((nz,)), dma((nz,)), dma((nz,)),
+        dma((nz,)), dma((nz,)), dma((nz,)), dma((nz,)), dma((8,)), dma((8,)), dma((2, 3)), dma((2, 3)), dma((2,)),
+    ]
+    return pl.pallas_call(
+        layer_kernel,
+        name="layer",
+        out_shape=(
+            jax.ShapeDtypeStruct((CAP, R, W), f32),
+            jax.ShapeDtypeStruct(tokens.shape, bf16),
+            jax.ShapeDtypeStruct(tokens.shape, bf16),
+            jax.ShapeDtypeStruct((8, D), f32),
+        ),
+        in_specs=[hbm] * 9,
+        out_specs=(vm, hbm, hbm, vm),
+        scratch_shapes=scratch,
+        compiler_params=pltpu.CompilerParams(collective_id=0, has_side_effects=True, vmem_limit_bytes=56 << 20),
+    )(tokens, cotangent, master, norms, steps, bands, lens_row, lens, owners)
+
+
+def finish_kernel(
+    total_hbm, norm_hbm, master_hbm, first_hbm, second_hbm, norm_m, norm_f, norm_s, owners_hbm, out_all, in_all,
+    block_output, input_grad, new_master, new_first, new_second, new_norm, new_norm_first, new_norm_second,
+    out_low, in_low, out_full, in_full, states, results, flat, grad, total, norm_total, norm_master, norm_first, norm_second, owners, l_sem, s_sem, i_sem, r_sem,
+):
+    pieces = l_sem.shape[1]
+    size = out_low.shape[0] // pieces
+    pairs = ((out_all, out_low, out_full, block_output), (in_all, in_low, in_full, input_grad))
+
+    def piece(p):
+        return pl.ds(pl.multiple_of(p * size, size), size)
+
+    def fetch(n, p):
+        return pltpu.make_async_copy(pairs[n][0].at[piece(p), :], pairs[n][1].at[piece(p), :], l_sem.at[n, p])
+
+    def store(n, p):
+        return pltpu.make_async_copy(pairs[n][2].at[piece(p), :], pairs[n][3].at[piece(p), :], s_sem.at[n, p])
+
+    small_copies = [
+        pltpu.make_async_copy(src, dst, i_sem.at[3 + i])
+        for i, (src, dst) in enumerate((
+            (owners_hbm, owners), (total_hbm, total), (norm_hbm, norm_total),
+            (norm_m, norm_master), (norm_f, norm_first), (norm_s, norm_second),
+        ))
+    ]
+    state_copies = [
+        pltpu.make_async_copy(src, states.at[i], i_sem.at[i]) for i, src in enumerate((master_hbm, first_hbm, second_hbm))
+    ]
+    result_copies = [
+        pltpu.make_async_copy(results.at[i], dst, r_sem.at[i]) for i, dst in enumerate((new_master, new_first, new_second))
+    ]
+
+    def loop(count, body):
+        def step(i, _):
+            body(i)
+            return 0
+
+        lax.fori_loop(0, count, step, 0)
+
+    for copy in small_copies:
+        copy.start()
+    loop(pieces, lambda p: fetch(0, p).start())
+    for copy in state_copies:
+        copy.start()
+    loop(pieces, lambda p: fetch(1, p).start())
+
+    dp = lax.axis_index("dp")
+    small_copies[0].wait()
+    rows = block_rows(owners)
+    held = 0
+    for j in range(owners.shape[0]):
+        held = held + jnp.where(owners[j] == dp, 1, 0)
+
+    def spread(r):
+        is_wide = slot_is_wide(rows, dp * CAP + r)
+
+        @pl.when(is_wide)
+        def _():
+            for p in range(3):
+                flat[pl.ds(p, W, stride=3), :] = total[r, p * W : (p + 1) * W, :]
+
+        @pl.when(jnp.logical_not(is_wide))
+        def _():
+            for p in range(4):
+                flat[pl.ds(p, R // 4, stride=4), :] = total[r, p * (R // 4) : (p + 1) * (R // 4), :]
+
+    small_copies[1].wait()
+    for r in range(CAP):
+        spread(r)
+        grad[:, r, :] = flat[...]
+
+    def convert(n, p):
+        fetch(n, p).wait()
+        _, low, full, _ = pairs[n]
+        full[piece(p), :] = low[piece(p), :].astype(f32)
+        store(n, p).start()
+
+    loop(pieces, lambda p: convert(0, p))
+    for copy in state_copies:
+        copy.wait()
+    step = 32
+    slot = lax.broadcasted_iota(jnp.int32, (step, CAP, W), 1)
+
+    def update(i):
+        here = pl.ds(pl.multiple_of(i * step, step), step)
+        new = adamw_update(states[0, here], states[1, here], states[2, here], grad[here], weight_decay, learn_rate)
+        for n in range(3):
+            results[n, here] = jnp.where(slot < held, new[n], 0.0)
+
+    loop(R // step, update)
+    for copy in result_copies:
+        copy.start()
+    for copy in small_copies[2:]:
+        copy.wait()
+    pair = norm_total[:, pl.ds(pl.multiple_of((dp // 2) * W, W), W)]
+    mine = jnp.where(lax.rem(dp, 2) == 1, pltpu.roll(pair, W // 2, 1), pair)[0:4, 0 : norm_master.shape[1]]
+    new = adamw_update(norm_master[...], norm_first[...], norm_second[...], mine, 0.0, norm_rate)
+    for ref, value in zip((new_norm, new_norm_first, new_norm_second), new):
+        ref[...] = value
+    loop(pieces, lambda p: convert(1, p))
+    for n in range(2):
+        loop(pieces, lambda p: store(n, p).wait())
+    for copy in result_copies:
+        copy.wait()
+
+
+def finish(total, norm_total, slots, norms, owners, out_all, in_all):
+    vm = pl.BlockSpec(memory_space=pltpu.VMEM)
+    hbm = pl.BlockSpec(memory_space=pltpu.HBM)
+    dma = pltpu.SemaphoreType.DMA
+    V = pltpu.VMEM
+    pieces = 8
+    shape = out_all.shape
+    return pl.pallas_call(
+        finish_kernel,
+        name="finish",
+        out_shape=(
+            (jax.ShapeDtypeStruct(shape, f32),) * 2 + tuple(jax.ShapeDtypeStruct(a.shape, f32) for a in slots + norms)
+        ),
+        in_specs=[hbm] * 11,
+        out_specs=(hbm,) * 5 + (vm,) * 3,
+        scratch_shapes=[
+            V(shape, bf16), V(shape, bf16), V(shape, f32), V(shape, f32), V((3, R, CAP, W), f32), V((3, R, CAP, W), f32),
+            V((R, W), f32), V((R, CAP, W), f32),
+            V(total.shape, f32), V(norm_total.shape, f32), *(V(a.shape, f32) for a in norms),
+            pltpu.SMEM(owners.shape, jnp.int32), dma((2, pieces)), dma((2, pieces)), dma((9,)), dma((3,)),
+        ],
+        compiler_params=pltpu.CompilerParams(vmem_limit_bytes=60 << 20),
+    )(total, norm_total, *slots, *norms, owners, out_all, in_all)
+
+
+def fast_shards(
+    tokens, cotangent, timesteps, bands, lengths, owners,
+    master_slots, first_slots, second_slots, norm_master, norm_first, norm_second,
+):
+    def tiles(slots):
+        return jnp.transpose(slots.reshape(CAP, R, W), (1, 0, 2))
+
+    def flat(slots):
+        return jnp.transpose(slots, (1, 0, 2)).reshape(CAP, R * W)
+
+    steps, bands_row, lens_row = (v.reshape(1, -1) for v in (timesteps, bands, lengths))
+    slots = tuple(tiles(s) for s in (master_slots, first_slots, second_slots))
+    norms = (norm_master, norm_first, norm_second)
+    total, out_all, in_all, norm_total = layer(
+        tokens, cotangent, slots[0], norm_master, steps, bands_row, lens_row, lengths, owners
+    )
+    results = finish(total, norm_total, slots, norms, owners, out_all, in_all)
+    return (*results[:2], *(flat(s) for s in results[2:5]), *results[5:])
+
+
 def solution(mesh):
+    fits = dict(mesh.shape) == {"dp": 8, "head": 4}
     placed = (
         P("dp", None),
         P("dp", None),
@@ -286,7 +1132,7 @@
         P(None, "dp"),
     )
     return jax.shard_map(
-        shards,
+        fast_shards if fits else shards,
         mesh=mesh,
         in_specs=placed,
         out_specs=(

time: 481 us -> 147 us (0.31); the launches traced: 472 us -> 147 us
  waiting for transfers between devices: 263 us -> 0 us
  Pallas kernels: 0 us -> 146 us
  blocking collectives: 62.9 us -> 0 us
  other arithmetic: 55.8 us -> 0 us
  matrix products: 41.4 us -> 0 us
  local copies, waits for them, and re-layouts: 33.8 us -> 0 us
  between operations: 14.9 us -> 0.64 us
    psum x4 -> x0, waiting for transfers between devices: 231 us -> none  [the longest x1 79.6 us: shards(): lax.psum(jnp.dot(activated_low, down_weight, preferred_element_type=jnp.f...]
    pallas_call x0 -> x2, Pallas kernels: none -> 146 us  [the longest x1 139 us: layer(): pl.pallas_call(layer_kernel, name='layer', out_shape=(jax.ShapeDtypeStruc...]
    dot_general x18 -> x0, matrix products: 41.4 us -> none  [the longest x4 13.5 us: contract_cols(): lax.dot_general(left_side, right_side, (((1,), (1,)), ((), ())), preferre...]
    psum x2 -> x0, blocking collectives: 40.6 us -> none  [the longest x1 21.4 us: shards(): lax.psum(norm_grads.astype(jnp.bfloat16), 'dp').astype(jnp.float32)]
    all_gather x1 -> x0, waiting for transfers between devices: 32.1 us -> none  [shards(): lax.all_gather(master_slots.astype(jnp.bfloat16), 'dp', axis=0, tiled=True)]
    reduce_sum x12 -> x0, other arithmetic: 23 us -> none  [the longest x2 5.91 us: norm_forward(): average = jnp.mean(values, axis=-1, keepdims=True)]
    all_gather x1 -> x0, blocking collectives: 22.3 us -> none  [shards(): lax.all_gather(norm_master.astype(jnp.bfloat16), 'dp', axis=1, tiled=True)]
    unnamed x89 -> x0, local copies, waits for them, and re-layouts: 13.8 us -> none
  transfers between devices with their start and end apart: 5 -> 0, of which waited for: 5 -> 0; matrix products, arithmetic and copies ran while one was open for 8% -> 0% of each run, Pallas kernels for 0% -> 0%
where the time goes in v3:
time: 147 us
  Pallas kernels  146 us (99%)
    pallas_call x1, Pallas kernels, layer(): pl.pallas_call(layer_kernel, name='layer', out_shape=(jax.ShapeDtypeStruc...  139 us
    pallas_call x1, Pallas kernels, finish(): pl.pallas_call(finish_kernel, name='finish', out_shape=(jax.ShapeDtypeStr...  7.43 us

profile of v3, /device:TPU:0, one launch (start us, length us, event | category | flops | bytes accessed | tf_op | source)
XLA Modules:
  0.0 146.8 jit_solution(17843235291194201161)
XLA Ops:
  0.6 138.7 %layer.1 = (f32[3,384,128]{2,1,0:T(8,128)}, bf16[2048,512]{1,0:T(8,128)(2,1)}, bf16[2048,512]{1,0:T(8,128)(2,1)}, f32[8,512]{1,0:T(8,128)}) custom-call(f32[2048,512]{1,0:T(8,128)} %tok_hbm.1, f32[2048,512]{1,0:T(8,128)} %cot_hbm.1, f32[384,3,128]{2,1,0:T(4,128)} %bitcast.21, f32[4,64]{1,0:T(4,128)} %norm_m.1, s32[1,8]{1,0:T(1,128)} %bitcast.26, ...), custom_call_target="tpu_custom_call" | custom-call | tf_op jit(solution)/shard_map/layer/pallas_call | solution.py:951
  139.3 7.4 %finish.1 = (f32[2048,512]{1,0:T(8,128)}, f32[2048,512]{1,0:T(8,128)}, f32[384,3,128]{2,1,0:T(4,128)}, f32[384,3,128]{2,1,0:T(4,128)}, f32[384,3,128]{2,1,0:T(4,...) custom-call(f32[3,384,128]{2,1,0:T(8,128)} %get-tuple-element.20.total_hbm, ...), custom_call_target="tpu_custom_call" | custom-call | tf_op jit(solution)/shard_map/finish/pallas_call | solution.py:1080

commit v4 on v3

--- a/solution.py
+++ b/solution.py
@@ -353,7 +353,7 @@
     return pieces
 
 
-RA = 192
+RA = 288
 GA = 192
 TILE = 128
 
@@ -362,7 +362,7 @@
     tok_hbm, cot_hbm, master_hbm, norms_hbm, steps_hbm, bands_hbm, lens_row_hbm, lens_hbm, owners_hbm,
     total, out_all, in_all, norm_total,
     wv, master, flat, mine, meta, norms_v, steps, bands, lens_row, lens, owners, block_at,
-    tok, cot, low1, xhat1, inv1, qkv, probs, sums, att, acc, low2, xhat2, inv2, e2, actives, slopes, da, e1,
+    tok, cot, low1, xhat1, inv1, qkv, probs, sums, att, acc, low2, xhat2, inv2, e2, da, e1,
     out_low, in_low,
     grads, from_core, rxa, sa, rya, sb, ryb, sbx, rxb, fz, rz, norm_part, norm_sum, n_core, n_x, n_y, n_z,
     i_sem, z_s, z_r, ya_s, ya_r, xa_s, xa_r, xb_s, xb_r, yb_s, yb_r, core_s, core_r, m_s, m_r,
@@ -378,17 +378,23 @@
     for peer in peers:
         pl.semaphore_signal(barrier, inc=1, device_id=peer, device_id_type=MESH)
 
-    tokens_here = tok.shape[0]
+    tokens_here = tok.shape[1]
     items_here = tokens_here // SEQ
     tiles = tokens_here // TILE
-    first_token = pl.multiple_of(head * tokens_here, tokens_here)
+
+    def whose(p):
+        return lax.rem(x + p, 2) * 2 + c
+
+    def tokens_of(ref, who):
+        return ref.at[pl.ds(pl.multiple_of(who * tokens_here, tokens_here), tokens_here), :]
+
     fetches = [
         pltpu.make_async_copy(src, dst, i_sem.at[n])
         for n, (src, dst) in enumerate((
             (owners_hbm, owners), (master_hbm, master), (steps_hbm, steps), (bands_hbm, bands),
             (lens_row_hbm, lens_row), (norms_hbm, norms_v), (lens_hbm, lens),
-            (tok_hbm.at[pl.ds(first_token, tokens_here), :], tok),
-            (cot_hbm.at[pl.ds(first_token, tokens_here), :], cot),
+            (tokens_of(tok_hbm, whose(0)), tok.at[0]), (tokens_of(cot_hbm, whose(0)), cot.at[0]),
+            (tokens_of(tok_hbm, whose(1)), tok.at[1]), (tokens_of(cot_hbm, whose(1)), cot.at[1]),
         ))
     ]
     for fetch in fetches:
@@ -540,28 +546,27 @@
     scales = item_weight * count_of / weight_of
     item_lane = lax.broadcasted_iota(jnp.int32, (1, items), 1)
     position = lax.broadcasted_iota(jnp.int32, (TILE, 1), 0)
-    fetches[6].wait()
-    fetches[7].wait()
-    fetches[8].wait()
+    for n in range(6, 11):
+        fetches[n].wait()
 
     def tile(t):
         return pl.ds(pl.multiple_of(t * TILE, TILE), TILE)
 
-    def first_norm(t):
+    def first_norm(i):
+        p, t = i // tiles, lax.rem(i, tiles)
         here = tile(t)
-        scaled, inverse = normalise(tok[here, :])
-        xhat1[here, :] = scaled
-        inv1[here, :] = inverse
-        low1[here, :] = (scaled * gain1 + shift1).astype(bf16)
-        item = head * items_here + t // (SEQ // TILE)
+        scaled, inverse = normalise(tok[p, here, :])
+        xhat1[p, here, :] = scaled
+        inv1[p, here, :] = inverse
+        low1[p, here, :] = (scaled * gain1 + shift1).astype(bf16)
+        item = whose(p) * items_here + t // (SEQ // TILE)
         scale = jnp.sum(jnp.where(item_lane == item, scales, 0.0), axis=1, keepdims=True)
         inside = position + lax.rem(t, SEQ // TILE) * TILE < lens[item]
-        scaled_cot = cot[here, :] * jnp.where(inside, scale, 0.0)
-        cot[here, :] = scaled_cot
-        e2[here, :] = scaled_cot.astype(bf16)
-        acc[here, :] = jnp.zeros((TILE, D), f32)
-
-    loop(0, tiles, first_norm)
+        scaled_cot = cot[p, here, :] * jnp.where(inside, scale, 0.0)
+        cot[p, here, :] = scaled_cot
+        e2[p, here, :] = scaled_cot.astype(bf16)
+
+    loop(0, 2 * tiles, first_norm)
 
     def gather(step):
         pl.when(step < nz)(lambda: gather0(step))
@@ -609,17 +614,108 @@
             axis=1,
         )
 
+    deep, low = (QB + 2, CB - 2), (0, QB + 2)
+    x_part, y_part = pl.ds(0, RA), pl.ds(RA, R - RA)
+
+    def core_push(j, n):
+        part = pl.ds(*(deep, low)[n])
+        return remote(grads.at[j, part], from_core.at[j, part], cs.at[n, j], cr.at[n, j], core_peer)
+
+    def x_push(n):
+        part = pl.ds(*(deep, low)[n])
+        return remote(grads.at[2, part, x_part, :], rxa.at[part], as_.at[n], ar.at[n], x_peer)
+
+    def hand_over(i, n):
+        first, count = (deep, low)[n]
+        pl.when(i < 2)(lambda: core_push(i, n).start())
+
+        @pl.when(i >= 2)
+        def _():
+            core_push(i - 2, n).wait_recv()
+
+            def add(block):
+                grads[i, block] = grads[i, block] + from_core[i - 2, block]
+
+            loop(first, first + count, add)
+            pl.when(i == 2)(lambda: x_push(n).start())
+
+    pair_z, cross_z = z + 1 - 2 * lax.rem(z, 2), lax.rem(z + 2, nz)
+
+    def chunk(k):
+        return lax.rem(pair_z + lax.rem(k, 2) * (z - pair_z) + 2 * (1 - k // 2), nz)
+
+    def block_of(k, yy, r):
+        return block_at[(chunk(k) * 2 + yy) * CAP + r]
+
+    def over_y_first(k):
+        return remote(sb.at[k], ryb.at[k], sby_s.at[k], sby_r.at[k], y_peer)
+
+    def over_x_last(k):
+        return remote(sbx.at[k], rxb.at[k], sbx_s.at[k], sbx_r.at[k], x_peer)
+
+    def over_y_last(k):
+        return remote(sa.at[k], rya.at[k], say_s.at[k], say_r.at[k], y_peer)
+
+    def over_z(k):
+        goal = pair_z + lax.rem(k, 2) * (cross_z - pair_z)
+        return remote(fz.at[k], rz.at[k], fz_s.at[k], fz_r.at[k], device(goal, y, x, c))
+
+    def norm_copies():
+        z_peers = [device(lax.rem(z + k, nz), y, x, c) for k in range(1, nz)]
+        return [
+            remote(norm_part, n_core, n_s.at[0], n_r.at[0], core_peer),
+            remote(norm_sum.at[0], n_x, n_s.at[1], n_r.at[1], x_peer),
+            remote(norm_sum.at[1], n_y, n_s.at[2], n_r.at[2], y_peer),
+        ] + [remote(norm_sum.at[2], n_z.at[k], n_s.at[3 + k], n_r.at[3 + k], p) for k, p in enumerate(z_peers)]
+
+    def send_b(k):
+        for r in range(CAP):
+            block = block_of(k, 1 - y, r)
+            for j in range(2):
+                sb[k, j, r] = grads[2 + j, block, y_part, :]
+        over_y_first(k).start()
+
+    def add_x(j):
+        grads[3, j, x_part, :] = grads[3, j, x_part, :] + rxa[j]
+
+    def send_a(k):
+        for r in range(CAP):
+            sa[k, r] = grads[3, block_of(k, 1 - y, r), x_part, :]
+        over_y_last(k).start()
+
+    def reduce1(k):
+        over_y_first(k).wait_recv()
+        for r in range(CAP):
+            sbx[k, r] = grads[2, block_of(k, y, r), y_part, :] + ryb[k, 0, r]
+        over_x_last(k).start()
+
+    def reduce2(k):
+        over_y_last(k).wait_recv()
+        over_x_last(k).wait_recv()
+        for r in range(CAP):
+            block = block_of(k, y, r)
+            fz[k, r, x_part, :] = grads[3, block, x_part, :] + rya[k, r]
+            part = grads[3, block, y_part, :].astype(f32) + ryb[k, 1, r].astype(f32)
+            fz[k, r, y_part, :] = (part + rxb[k, r].astype(f32)).astype(bf16)
+        pl.when(lax.rem(k, 2) == 0)(lambda: over_z(k).start())
+
+    def cross():
+        over_z(0).wait_recv()
+        for r in range(CAP):
+            fz[1, r] = fz[1, r] + rz[0, r]
+        over_z(1).start()
+
     key_row = lax.broadcasted_iota(jnp.int32, (2 * SEQ, W), 0)
     head_ones = jnp.where((key_row < SEQ) == head_masks[0], 1.0, 0.0).astype(bf16)
 
-    def attention(h):
-        projected = dot(low1[...], wide_matrix(h))
+    def attention(p, h):
+        projected = dot(low1[p], wide_matrix(h))
         qkv[h, 0] = (projected[:, :W].astype(bf16).astype(f32) * (1.0 / math.sqrt(HD))).astype(bf16)
         qkv[h, 1] = projected[:, W : 2 * W].astype(bf16)
         qkv[h, 2] = projected[:, 2 * W :].astype(bf16)
         for i, here in enumerate(item_rows):
             query, key, value = qkv[h, 0, here, :], qkv[h, 1, here, :], qkv[h, 2, here, :]
-            valid = key_pos < lens[head * items_here + i]
+            valid = key_pos < lens[whose(p) * items_here + i]
             both = []
             for a in range(2):
                 scores = jnp.where(valid, dot_cols(only(query, a), key), -1e30)
@@ -632,121 +728,35 @@
             att[h, here, :] = (mixed[:, :W] * inverse).astype(bf16)
         acc[...] += dot(att[h], narrow_matrix(h, 0, W))
 
-    loop(0, 4, attention)
-
-    def second_norm(t):
-        here = tile(t)
-        state = acc[here, :] + tok[here, :]
-        acc[here, :] = state
-        scaled, inverse = normalise(state)
-        xhat2[here, :] = scaled
-        inv2[here, :] = inverse
-        low2[here, :] = (scaled * gain2 + shift2).astype(bf16)
-        da[here, :] = jnp.zeros((TILE, D), f32)
-
-    loop(0, tiles, second_norm)
-
-    def shard_of(i):
-        return lax.rem(1 - x + i, 2) * 2 + lax.rem(c + 1 + i // 2, 2)
-
-    def feed_forward(i):
-        h = shard_of(i)
-        hidden = dot(low2[...], narrow_matrix(h, W, D))
+    def put(i, first, result):
+        for block, inside, row, count in cat_pieces(first, result.shape[0]):
+            for p in range(4):
+                here = pl.ds(p * (R // 4) + inside, count)
+                grads[i, block, here, :] = result[row : row + count, p * W : (p + 1) * W].astype(bf16)
+
+    def shard_of(p, i):
+        return lax.rem(1 + x + p + i, 2) * 2 + lax.rem(c + 1 + i // 2, 2)
+
+    def feed_forward(p, i):
+        h = shard_of(p, i)
+        up_matrix, down_matrix = narrow_matrix(h, W, D), narrow_matrix(h, W + D, D)
+        hidden = dot(low2[...], up_matrix)
         root = math.sqrt(2.0 / math.pi)
         square = hidden * hidden
         bend = jnp.tanh(root * hidden * (1.0 + 0.044715 * square))
         half = 0.5 * (1.0 + bend)
         active = (hidden * half).astype(bf16)
         slope = half + 0.5 * hidden * (1.0 - bend * bend) * (root + (3.0 * 0.044715 * root) * square)
-        actives[i] = active
-        slopes[i] = slope.astype(bf16)
-        acc[...] += dot(active, narrow_matrix(h, W + D, D))
-
-    loop(0, 4, feed_forward)
-
-    def own_tokens(ref, who):
-        return ref.at[pl.ds(pl.multiple_of(who * tokens_here, tokens_here), tokens_here), :]
-
-    outs = ((out_low, out_all), (in_low, in_all))
-
-    def out_copies(i):
-        src, dst = outs[i]
-        there, across = own_tokens(dst, head), own_tokens(dst, (1 - x) * 2 + c)
-        return (
-            pltpu.make_async_copy(src, there, o_l.at[i]),
-            remote(src, there, o_s.at[i, 0], o_r.at[i, 0], x_peer),
-            remote(src, there, o_s.at[i, 1], o_r.at[i, 1], core_peer),
-            same(across, o_s.at[i, 2], o_r.at[i, 2], core_peer),
-        )
-
-    out_low[...] = acc[...].astype(bf16)
-    for copy in out_copies(0)[:3]:
-        copy.start()
-
-    def put(i, first, result):
-        for block, inside, row, count in cat_pieces(first, result.shape[0]):
-            for p in range(4):
-                here = pl.ds(p * (R // 4) + inside, count)
-                grads[i, block, here, :] = result[row : row + count, p * W : (p + 1) * W].astype(bf16)
-
-    deep, low = (QB + 2, CB - 2), (0, QB + 2)
-    x_part, y_part = pl.ds(0, RA), pl.ds(RA, R - RA)
-
-    def core_push(i, n):
-        part = pl.ds(*(deep, low)[n])
-        return remote(grads.at[i, part], from_core.at[i, part], cs.at[n, i], cr.at[n, i], core_peer)
-
-    def x_push(n):
-        part = pl.ds(*(deep, low)[n])
-        return remote(grads.at[2, part, x_part, :], rxa.at[part], as_.at[n], ar.at[n], x_peer)
-
-    def hand_over(i, n):
-        first, count = (deep, low)[n]
-        pl.when(i < 2)(lambda: core_push(i, n).start())
-
-        @pl.when(i >= 2)
-        def _():
-            core_push(i - 2, n).wait_recv()
-
-            def add(j):
-                grads[i, j] = grads[i, j] + from_core[i - 2, j]
-
-            loop(first, first + count, add)
-            pl.when(i == 2)(lambda: x_push(n).start())
-
-    def feed_forward_back(i):
-        h = shard_of(i)
-        back = (dot_cols(e2[...], narrow_matrix(h, W + D, D)) * slopes[i].astype(f32)).astype(bf16)
-        put(i, W + D, dot_rows(actives[i], e2[...]))
-        put(i, W, dot_rows(low2[...], back))
-        da[...] += dot_cols(back, narrow_matrix(h, W, D))
-        hand_over(i, 0)
-
-    loop(0, 4, feed_forward_back)
-
-    def norm_backward(grad, scaled, inverse, gain):
-        grad_scaled = grad * gain
-        centre = jnp.mean(grad_scaled, axis=-1, keepdims=True)
-        slope = jnp.mean(grad_scaled * scaled, axis=-1, keepdims=True)
-        return inverse * (grad_scaled - centre - scaled * slope)
-
-    norm_part[...] = jnp.zeros_like(norm_part)
-
-    def second_norm_back(t):
-        here = tile(t)
-        grad, scaled = da[here, :], xhat2[here, :]
-        norm_part[2:3, :] += jnp.sum(grad * scaled, axis=0, keepdims=True)
-        norm_part[3:4, :] += jnp.sum(grad, axis=0, keepdims=True)
-        change = cot[here, :] + norm_backward(grad, scaled, inv2[here, :], gain2)
-        cot[here, :] = change
-        e1[here, :] = change.astype(bf16)
-        da[here, :] = jnp.zeros((TILE, D), f32)
-
-    loop(0, tiles, second_norm_back)
-
-    def attention_back(i):
-        h = shard_of(i)
-        put(i, 0, dot_rows(att[h], e1[...]))
+        acc[...] += dot(active, down_matrix)
+        back = (dot_cols(e2[p], down_matrix) * slope).astype(bf16)
+        da[...] += dot_cols(back, up_matrix)
+        if p == 0:
+            put(i, W + D, dot_rows(active, e2[p]))
+            put(i, W, dot_rows(low2[...], back))
+            hand_over(i, 0)
+
+    def attention_back(p, i):
+        h = shard_of(p, i)
         d_all = dot_cols(e1[...], narrow_matrix(h, 0, W)) * sums[h]
         shared_all = (d_all * att[h].astype(f32)).astype(bf16)
         d_all = d_all.astype(bf16)
@@ -764,137 +774,130 @@
             d_value = dot_rows(jnp.concatenate([probs[h, m, 0], probs[h, m, 1]], axis=0), stack(d_here))
             parts.append(jnp.concatenate([d_query, d_key, d_value], axis=1).astype(bf16))
         d_qkv = jnp.concatenate(parts, axis=0)
-        d_weight = dot_rows(low1[...], d_qkv).astype(bf16)
-        for j in range(QB):
-            for p in range(3):
-                grads[i, j, p * W : (p + 1) * W, :] = d_weight[j * W : (j + 1) * W, p * W : (p + 1) * W]
         da[...] += dot_cols(d_qkv, wide_matrix(h))
-        hand_over(i, 1)
-
-    loop(0, 4, attention_back)
-
-    def chunk(k):
-        return lax.rem(z + 1 + k, nz)
-
-    def block_of(k, yy, r):
-        return block_at[(chunk(k) * 2 + yy) * CAP + r]
-
-    def over_y_first(k):
-        return remote(sb.at[k], ryb.at[k], sby_s.at[k], sby_r.at[k], y_peer)
-
-    def over_x_last(k):
-        return remote(sbx.at[k], rxb.at[k], sbx_s.at[k], sbx_r.at[k], x_peer)
-
-    def over_y_last(k):
-        return remote(sa.at[k], rya.at[k], say_s.at[k], say_r.at[k], y_peer)
-
-    def over_z(k):
-        return remote(fz.at[k], rz.at[k], fz_s.at[k], fz_r.at[k], device(chunk(k), y, x, c))
-
-    def send_b(k):
-        for r in range(CAP):
-            block = block_of(k, 1 - y, r)
-            for j in range(2):
-                sb[k, j, r] = grads[2 + j, block, y_part, :]
-        over_y_first(k).start()
-
-    loop(0, nz, send_b)
-
-    def first_norm_back(t):
-        here = tile(t)
-        grad, scaled = da[here, :], xhat1[here, :]
-        norm_part[0:1, :] += jnp.sum(grad * scaled, axis=0, keepdims=True)
-        norm_part[1:2, :] += jnp.sum(grad, axis=0, keepdims=True)
-        in_low[here, :] = (cot[here, :] + norm_backward(grad, scaled, inv1[here, :], gain1)).astype(bf16)
-
-    loop(0, tiles, first_norm_back)
-    for copy in out_copies(1)[:3]:
-        copy.start()
-
-    def norm_copies():
-        z_peers = [device(lax.rem(z + k, nz), y, x, c) for k in range(1, nz)]
-        return [
-            remote(norm_part, n_core, n_s.at[0], n_r.at[0], core_peer),
-            remote(norm_sum.at[0], n_x, n_s.at[1], n_r.at[1], x_peer),
-            remote(norm_sum.at[1], n_y, n_s.at[2], n_r.at[2], y_peer),
-        ] + [remote(norm_sum.at[2], n_z.at[k], n_s.at[3 + k], n_r.at[3 + k], p) for k, p in enumerate(z_peers)]
-
-    norm_copies()[0].start()
-
-    for n in range(2):
-        x_push(n).wait_recv()
-
-    def add_x(j):
-        grads[3, j, x_part, :] = grads[3, j, x_part, :] + rxa[j]
-
-    loop(0, QB + CB, add_x)
-
-    def send_a(k):
-        for r in range(CAP):
-            sa[k, r] = grads[3, block_of(k, 1 - y, r), x_part, :]
-        over_y_last(k).start()
-
-    loop(0, nz, send_a)
-
-    norm_copies()[0].wait_recv()
-    norm_sum[0] = norm_part[...] + n_core[...]
-    norm_copies()[1].start()
-
-    def reduce1(k):
-        over_y_first(k).wait_recv()
-        for r in range(CAP):
-            sbx[k, r] = grads[2, block_of(k, y, r), y_part, :] + ryb[k, 0, r]
-        over_x_last(k).start()
-
-    def reduce2(k):
-        over_y_last(k).wait_recv()
-        over_x_last(k).wait_recv()
-        for r in range(CAP):
-            block = block_of(k, y, r)
-            fz[k, r, x_part, :] = grads[3, block, x_part, :] + rya[k, r]
-            part = grads[3, block, y_part, :].astype(f32) + ryb[k, 1, r].astype(f32)
-            fz[k, r, y_part, :] = (part + rxb[k, r].astype(f32)).astype(bf16)
-        pl.when(k < nz - 1)(lambda: over_z(k).start())
-
-    def reduce_step(k):
-        pl.when(k < nz)(lambda: reduce1(k))
-        pl.when(k >= 1)(lambda: reduce2(k - 1))
-
-    loop(0, 2, reduce_step)
-    norm_copies()[1].wait_recv()
-    norm_sum[1] = norm_sum[0] + n_x[...]
-    norm_copies()[2].start()
-    for i in range(2):
-        if i == 0:
-            out_copies(i)[1].wait_recv()
-            out_copies(i)[3].start()
-    loop(2, 4, reduce_step)
+        if p == 0:
+            put(i, 0, dot_rows(att[h], e1[...]))
+            d_weight = dot_rows(low1[p], d_qkv).astype(bf16)
+            for j in range(QB):
+                for m in range(3):
+                    grads[i, j, m * W : (m + 1) * W, :] = d_weight[j * W : (j + 1) * W, m * W : (m + 1) * W]
+            hand_over(i, 1)
+
+    def norm_backward(grad, scaled, inverse, gain):
+        grad_scaled = grad * gain
+        centre = jnp.mean(grad_scaled, axis=-1, keepdims=True)
+        slope = jnp.mean(grad_scaled * scaled, axis=-1, keepdims=True)
+        return inverse * (grad_scaled - centre - scaled * slope)
+
+    def add_norm(p, row, grad, scaled):
+        if p == 0:
+            norm_part[row : row + 1, :] += jnp.sum(grad * scaled, axis=0, keepdims=True)
+            norm_part[row + 1 : row + 2, :] += jnp.sum(grad, axis=0, keepdims=True)
+
+    norm_part[...] = jnp.zeros_like(norm_part)
+
+    def out_copies(p, n):
+        src, dst = ((out_low, out_all), (in_low, in_all))[n]
+        there = tokens_of(dst, whose(p))
+        return (
+            pltpu.make_async_copy(src.at[p], there, o_l.at[p, n]),
+            remote(src.at[p], there, o_s.at[p, n], o_r.at[p, n], core_peer),
+        )
+
+    def layer_pass(p):
+        if p == 1:
+            loop(0, nz, send_b)
+            norm_copies()[0].start()
+
+        acc[...] = jnp.zeros_like(acc)
+        loop(0, 4, lambda h: attention(p, h))
+
+        def second_norm(t):
+            here = tile(t)
+            state = acc[here, :] + tok[p, here, :]
+            acc[here, :] = state
+            scaled, inverse = normalise(state)
+            xhat2[here, :] = scaled
+            inv2[here, :] = inverse
+            low2[here, :] = (scaled * gain2 + shift2).astype(bf16)
+            da[here, :] = jnp.zeros((TILE, D), f32)
+
+        loop(0, tiles, second_norm)
+        loop(0, 4, lambda i: feed_forward(p, i))
+        out_low[p] = acc[...].astype(bf16)
+        for copy in out_copies(p, 0):
+            copy.start()
+
+        if p == 1:
+            norm_copies()[0].wait_recv()
+            norm_sum[0] = norm_part[...] + n_core[...]
+            norm_copies()[1].start()
+            for n in range(2):
+                x_push(n).wait_recv()
+            loop(0, QB + CB, add_x)
+            loop(0, nz, send_a)
+            loop(0, nz, reduce1)
+            norm_copies()[1].wait_recv()
+            norm_sum[1] = norm_sum[0] + n_x[...]
+            norm_copies()[2].start()
+
+
+        def second_norm_back(t):
+            here = tile(t)
+            grad, scaled = da[here, :], xhat2[here, :]
+            add_norm(p, 2, grad, scaled)
+            change = cot[p, here, :] + norm_backward(grad, scaled, inv2[here, :], gain2)
+            cot[p, here, :] = change
+            e1[here, :] = change.astype(bf16)
+            da[here, :] = jnp.zeros((TILE, D), f32)
+
+        loop(0, tiles, second_norm_back)
+        if p == 1:
+            reduce2(0)
+
+        def attention_step(i):
+            attention_back(p, i)
+            if p == 1:
+                pl.when(i < 2)(lambda: reduce2(i + 1))
+                pl.when(i == 1)(cross)
+
+        loop(0, 4, attention_step)
+
+        def first_norm_back(t):
+            here = tile(t)
+            grad, scaled = da[here, :], xhat1[p, here, :]
+            add_norm(p, 0, grad, scaled)
+            in_low[p, here, :] = (cot[p, here, :] + norm_backward(grad, scaled, inv1[p, here, :], gain1)).astype(bf16)
+
+        loop(0, tiles, first_norm_back)
+        for copy in out_copies(p, 1):
+            copy.start()
+
+    layer_pass(0)
+    layer_pass(1)
     norm_copies()[2].wait_recv()
     norm_sum[2] = norm_sum[1] + n_y[...]
     for copy in norm_copies()[3:]:
         copy.start()
-    loop(4, nz + 1, reduce_step)
-    out_copies(1)[1].wait_recv()
-    out_copies(1)[3].start()
+    reduce2(nz - 1)
 
     for k in range(nz - 1):
-        over_z(k).wait_recv()
         norm_copies()[3 + k].wait_recv()
+    over_z(2).wait_recv()
+    over_z(1).wait_recv()
     norm_total[...] = norm_sum[2] + ((n_z[0] + n_z[1]) + n_z[2])
 
     def last(r):
-        others = (rz[0, r].astype(f32) + rz[1, r].astype(f32)) + rz[2, r].astype(f32)
+        others = rz[1, r].astype(f32) + rz[2, r].astype(f32)
         total[r] = fz[nz - 1, r].astype(f32) + others
 
     loop(0, CAP, last)
 
-    for i in range(2):
-        local, _, over_core, again = out_copies(i)
-        local.wait()
-        over_core.wait_recv()
-        again.wait_recv()
-        for copy in out_copies(i)[1:]:
-            copy.wait_send()
+    for p in range(2):
+        for n in range(2):
+            local, over_core = out_copies(p, n)
+            local.wait()
+            over_core.wait()
     for copy in norm_copies():
         copy.wait_send()
     for k in range(len(dp_peers)):
@@ -913,8 +916,8 @@
     loop(0, nz, sent)
     for n in range(2):
         x_push(n).wait_send()
-        for i in range(2):
-            core_push(i, n).wait_send()
+        for j in range(2):
+            core_push(j, n).wait_send()
 
 
 def layer(tokens, cotangent, master, norms, steps, bands, lens_row, lens, owners):
@@ -929,24 +932,25 @@
     square = (here, D)
     blocks = QB + CB
     rb = R - RA
-    low, full = V(square, bf16), V(square, f32)
+    low, full, two_low, two = V(square, bf16), V(square, f32), V((2, *square), bf16), V((2, *square), f32)
     scratch = [
         V((4, nz * 2 * CAP, R, W), bf16), V((R, CAP, W), f32), V((R, W), f32),
         V((8, W), f32), V((nz * 2, 8, W), f32), V(norms.shape, f32),
         V((1, items), jnp.int32), V((1, items), jnp.int32), V((1, items), jnp.int32),
         S((items,), jnp.int32), S(owners.shape, jnp.int32), S((nz * 2 * CAP,), jnp.int32),
-        full, full, low, full, V((here, 1), f32), V((4, 3, here, W), bf16),
+        two, two, two_low, two, V((2, here, 1), f32), V((4, 3, here, W), bf16),
         V((4, items_here, 2, SEQ, SEQ), bf16), V((4, here, W), f32), V((4, here, W), bf16),
-        full, low, full, V((here, 1), f32), low, V((4, here, D), bf16), V((4, here, D), bf16), full, low, low, low,
+        full, low, full, V((here, 1), f32), two_low,
+        full, low, two_low, two_low,
         V((4, blocks, R, W), bf16), V((2, blocks, R, W), bf16),
         V((blocks, RA, W), bf16), V((nz, CAP, RA, W), bf16), V((nz, CAP, RA, W), bf16),
         V((nz, 2, CAP, rb, W), bf16), V((nz, 2, CAP, rb, W), bf16), V((nz, CAP, rb, W), bf16),
         V((nz, CAP, rb, W), bf16), V((nz, CAP, R, W), bf16), V((nz - 1, CAP, R, W), bf16),
         V((8, D), f32), V((3, 8, D), f32), V((8, D), f32), V((8, D), f32), V((8, D), f32), V((nz - 1, 8, D), f32),
-        dma((9,)), dma((nz + 1,)), dma((nz,)), dma((nz,)), dma((nz,)), dma((nz, 2)), dma((nz, 2)), dma((nz,)), dma((nz,)),
+        dma((11,)), dma((nz + 1,)), dma((nz,)), dma((nz,)), dma((nz,)), dma((nz, 2)), dma((nz, 2)), dma((nz,)), dma((nz,)),
         dma((nz, 2)), dma((nz, 2)), dma((nz, 4)), dma((nz, 4)), dma((8,)), dma((8,)),
         dma((2, 2)), dma((2, 2)), dma((2,)), dma((2,)), dma((nz,)), dma((nz,)), dma((nz,)), dma((nz,)),
-        dma((nz,)), dma((nz,)), dma((nz,)), dma((nz,)), dma((8,)), dma((8,)), dma((2, 3)), dma((2, 3)), dma((2,)),
+        dma((nz,)), dma((nz,)), dma((nz,)), dma((nz,)), dma((8,)), dma((8,)), dma((2, 2)), dma((2, 2)), dma((2, 2)),
     ]
     return pl.pallas_call(
         layer_kernel,

time: 147 us -> 134 us (0.912)
  Pallas kernels: 146 us -> 133 us
    pallas_call x1, Pallas kernels: 139 us -> 125 us  [layer(): pl.pallas_call(layer_kernel, name='layer', out_shape=(jax.ShapeDtypeStruc...]
where the time goes in v4:
time: 134 us; the launch traced here: 133 us
  Pallas kernels  133 us (99%)
    pallas_call x1, Pallas kernels, layer(): pl.pallas_call(layer_kernel, name='layer', out_shape=(jax.ShapeDtypeStruc...  125 us
    pallas_call x1, Pallas kernels, finish(): pl.pallas_call(finish_kernel, name='finish', out_shape=(jax.ShapeDtypeStr...  7.43 us

profile of v4, /device:TPU:0, one launch (start us, length us, event | category | flops | bytes accessed | tf_op | source)
XLA Modules:
  0.0 133.5 jit_solution(14104166785499627127)
XLA Ops:
  0.6 125.4 %layer.1 = (f32[3,384,128]{2,1,0:T(8,128)}, bf16[2048,512]{1,0:T(8,128)(2,1)}, bf16[2048,512]{1,0:T(8,128)(2,1)}, f32[8,512]{1,0:T(8,128)}) custom-call(f32[2048,512]{1,0:T(8,128)} %tok_hbm.1, f32[2048,512]{1,0:T(8,128)} %cot_hbm.1, f32[384,3,128]{2,1,0:T(4,128)} %bitcast.21, f32[4,64]{1,0:T(4,128)} %norm_m.1, s32[1,8]{1,0:T(1,128)} %bitcast.26, ...), custom_call_target="tpu_custom_call" | custom-call | tf_op jit(solution)/shard_map/layer/pallas_call | solution.py:955
  126.1 7.4 %finish.1 = (f32[2048,512]{1,0:T(8,128)}, f32[2048,512]{1,0:T(8,128)}, f32[384,3,128]{2,1,0:T(4,128)}, f32[384,3,128]{2,1,0:T(4,128)}, f32[384,3,128]{2,1,0:T(4,...) custom-call(f32[3,384,128]{2,1,0:T(8,128)} %get-tuple-element.20.total_hbm, ...), custom_call_target="tpu_custom_call" | custom-call | tf_op jit(solution)/shard_map/finish/pallas_call | solution.py:1084

commit v5 on v4

--- a/solution.py
+++ b/solution.py
@@ -354,7 +354,7 @@
 
 
 RA = 288
-GA = 192
+GA, GB = 176, 336
 TILE = 128
 
 
@@ -362,10 +362,11 @@
     tok_hbm, cot_hbm, master_hbm, norms_hbm, steps_hbm, bands_hbm, lens_row_hbm, lens_hbm, owners_hbm,
     total, out_all, in_all, norm_total,
     wv, master, flat, mine, meta, norms_v, steps, bands, lens_row, lens, owners, block_at,
-    tok, cot, low1, xhat1, inv1, qkv, probs, sums, att, acc, low2, xhat2, inv2, e2, da, e1,
+    tok, cot, low1, xhat1, inv1, qkv, probs, sums, att, acc, low2, xhat2, inv2, e2, actives, d_qkvs, da, e1,
     out_low, in_low,
     grads, from_core, rxa, sa, rya, sb, ryb, sbx, rxb, fz, rz, norm_part, norm_sum, n_core, n_x, n_y, n_z,
     i_sem, z_s, z_r, ya_s, ya_r, xa_s, xa_r, xb_s, xb_r, yb_s, yb_r, core_s, core_r, m_s, m_r,
+    c_s, c_r, zc_s, zc_r, cc_s, cc_r,
     cs, cr, as_, ar, say_s, say_r, sby_s, sby_r, sbx_s, sbx_r, fz_s, fz_r, n_s, n_r, o_s, o_r, o_l,
 ):
     z, y, x, c = place(Sizes)
@@ -440,7 +441,7 @@
 
     pl.semaphore_wait(barrier, len(peers))
 
-    part_a, part_b = pl.ds(0, GA), pl.ds(GA, R - GA)
+    part_a, part_b, part_ab, part_c = pl.ds(0, GA), pl.ds(GA, GB - GA), pl.ds(0, GB), pl.ds(GB, R - GB)
 
     def slab(sh, zz, yy, part=slice(None)):
         return wv.at[sh, pl.ds((zz * 2 + yy) * CAP, CAP), part, :]
@@ -450,8 +451,8 @@
         return (1 - late) * (z + k * (1 - 2 * lax.rem(z, 2))) + late * (k + low * (3 - 2 * k))
 
     up, down, inner = z < nz - 1, z > 0, lax.rem(z, nz - 1) != 0
-    own_up = same(slab(shard, z, y), z_s.at[0], z_r.at[z], device(z + 1, y, x, c))
-    own_down = same(slab(shard, z, y), z_s.at[nz], z_r.at[z], device(z - 1, y, x, c))
+    own_up = same(slab(shard, z, y, part_ab), z_s.at[0], z_r.at[z], device(z + 1, y, x, c))
+    own_down = same(slab(shard, z, y, part_ab), z_s.at[nz], z_r.at[z], device(z - 1, y, x, c))
     pl.when(up)(own_up.start)
     pl.when(down)(own_down.start)
 
@@ -465,7 +466,27 @@
         zz = order(k)
         late = k // 2
         goal = (1 - late) * (3 - z) + late * 3 * (z - 1)
-        return same(slab(shard, zz, y), z_s.at[k], z_r.at[zz], device(goal, y, x, c))
+        return same(slab(shard, zz, y, part_ab), z_s.at[k], z_r.at[zz], device(goal, y, x, c))
+
+    def both(j, zz):
+        return wv.at[lax.rem(x + j, 2) * 2 + c, pl.ds(zz * 2 * CAP, 2 * CAP), part_c, :]
+
+    def last_z(j, n):
+        return same(both(j, z), zc_s.at[j, n], zc_r.at[j, n], device(lax.rem(z + n, nz), y, x, c))
+
+    def last_here(j, n):
+        zz = lax.rem(z + nz - n, nz)
+        return same(both(j, zz), zc_s.at[j, n], zc_r.at[j, n], x_peer)
+
+    def last_core(j, n):
+        return same(both(j, lax.rem(z + nz - n, nz)), cc_s.at[j, n], cc_r.at[j, n], core_peer)
+
+    own_c = slab(shard, z, y, part_c)
+    c_copies = (
+        same(own_c, c_s.at[0], c_r.at[0], y_peer),
+        same(own_c, c_s.at[1], c_r.at[1], x_peer),
+        same(slab(shard, z, 1 - y, part_c), c_s.at[2], c_r.at[2], x_peer),
+    )
 
     def first_copies(k):
         zz = order(k)
@@ -475,7 +496,7 @@
             same(two, xb_s.at[k], xb_r.at[k], x_peer),
             same(two, yb_s.at[k, 0], yb_r.at[k, 0], y_peer),
             same(one, xa_s.at[k, 0], xa_r.at[k, 0], x_peer),
-            same(slab(shard, zz, y), core_s.at[k, 0], core_r.at[k, 0], core_peer),
+            same(slab(shard, zz, y, part_ab), core_s.at[k, 0], core_r.at[k, 0], core_peer),
         )
 
     def second_copies(k):
@@ -483,14 +504,14 @@
         return (
             same(slab(shard, zz, 1 - y, part_a), xa_s.at[k, 1], xa_r.at[k, 1], x_peer),
             same(slab(far, zz, y, part_b), yb_s.at[k, 1], yb_r.at[k, 1], y_peer),
-            same(slab(shard, zz, 1 - y), core_s.at[k, 1], core_r.at[k, 1], core_peer),
+            same(slab(shard, zz, 1 - y, part_ab), core_s.at[k, 1], core_r.at[k, 1], core_peer),
         )
 
     def third_copies(k):
         zz = order(k)
         return (
-            same(slab(far, zz, y), core_s.at[k, 2], core_r.at[k, 2], core_peer),
-            same(slab(far, zz, 1 - y), core_s.at[k, 3], core_r.at[k, 3], core_peer),
+            same(slab(far, zz, y, part_ab), core_s.at[k, 2], core_r.at[k, 2], core_peer),
+            same(slab(far, zz, 1 - y, part_ab), core_s.at[k, 3], core_r.at[k, 3], core_peer),
         )
 
     def gather0(k):
@@ -521,7 +542,14 @@
         same(slab(far, zz, 1 - y, part_b), yb_s.at[k, 1], yb_r.at[k, 1], y_peer).wait_recv()
         apart.start()
 
+    c_copies[0].start()
+    c_copies[1].start()
     gather0(0)
+
+    def gather_last(n):
+        for j in range(2):
+            last_here(j, n).wait_recv()
+            last_core(j, n).start()
 
     def find_block(row):
         block = 0
@@ -566,19 +594,35 @@
         cot[p, here, :] = scaled_cot
         e2[p, here, :] = scaled_cot.astype(bf16)
 
+    c_copies[0].wait_recv()
+    c_copies[2].start()
     loop(0, 2 * tiles, first_norm)
+    c_copies[1].wait_recv()
+    c_copies[2].wait_recv()
+    for j in range(2):
+        last_core(j, 0).start()
 
     def gather(step):
         pl.when(step < nz)(lambda: gather0(step))
+
+        @pl.when(step == nz - 1)
+        def _():
+            for j in range(2):
+                for n in range(1, nz):
+                    last_z(j, n).start()
+
         pl.when(step <= nz)(lambda: gather1(step - 1))
         pl.when(step >= 2)(lambda: gather2(step - 2))
 
     loop(1, nz + 2, gather)
+    loop(1, nz, gather_last)
 
     def all_here(k):
         zz = order(k)
         for kind, (xx, yy) in enumerate(((x, y), (x, 1 - y), (1 - x, y), (1 - x, 1 - y))):
-            same(slab(xx * 2 + 1 - c, zz, yy), core_s.at[k, kind], core_r.at[k, kind], core_peer).wait_recv()
+            same(slab(xx * 2 + 1 - c, zz, yy, part_ab), core_s.at[k, kind], core_r.at[k, kind], core_peer).wait_recv()
+        for j in range(2):
+            last_core(j, k).wait_recv()
 
     loop(0, nz, all_here)
 
@@ -656,9 +700,9 @@
     def over_y_last(k):
         return remote(sa.at[k], rya.at[k], say_s.at[k], say_r.at[k], y_peer)
 
-    def over_z(k):
+    def over_z(k, r):
         goal = pair_z + lax.rem(k, 2) * (cross_z - pair_z)
-        return remote(fz.at[k], rz.at[k], fz_s.at[k], fz_r.at[k], device(goal, y, x, c))
+        return remote(fz.at[k, r], rz.at[k, r], fz_s.at[k, r], fz_r.at[k, r], device(goal, y, x, c))
 
     def norm_copies():
         z_peers = [device(lax.rem(z + k, nz), y, x, c) for k in range(1, nz)]
@@ -697,13 +741,13 @@
             fz[k, r, x_part, :] = grads[3, block, x_part, :] + rya[k, r]
             part = grads[3, block, y_part, :].astype(f32) + ryb[k, 1, r].astype(f32)
             fz[k, r, y_part, :] = (part + rxb[k, r].astype(f32)).astype(bf16)
-        pl.when(lax.rem(k, 2) == 0)(lambda: over_z(k).start())
+            pl.when(lax.rem(k, 2) == 0)(over_z(k, r).start)
 
     def cross():
-        over_z(0).wait_recv()
         for r in range(CAP):
+            over_z(0, r).wait_recv()
             fz[1, r] = fz[1, r] + rz[0, r]
-        over_z(1).start()
+            over_z(1, r).start()
 
     key_row = lax.broadcasted_iota(jnp.int32, (2 * SEQ, W), 0)
     head_ones = jnp.where((key_row < SEQ) == head_masks[0], 1.0, 0.0).astype(bf16)
@@ -747,7 +791,10 @@
         half = 0.5 * (1.0 + bend)
         active = (hidden * half).astype(bf16)
         slope = half + 0.5 * hidden * (1.0 - bend * bend) * (root + (3.0 * 0.044715 * root) * square)
-        acc[...] += dot(active, down_matrix)
+        if p == 0:
+            actives[i] = active
+        else:
+            acc[...] += dot(active, down_matrix)
         back = (dot_cols(e2[p], down_matrix) * slope).astype(bf16)
         da[...] += dot_cols(back, up_matrix)
         if p == 0:
@@ -774,14 +821,22 @@
             d_value = dot_rows(jnp.concatenate([probs[h, m, 0], probs[h, m, 1]], axis=0), stack(d_here))
             parts.append(jnp.concatenate([d_query, d_key, d_value], axis=1).astype(bf16))
         d_qkv = jnp.concatenate(parts, axis=0)
-        da[...] += dot_cols(d_qkv, wide_matrix(h))
         if p == 0:
+            d_qkvs[i] = d_qkv
             put(i, 0, dot_rows(att[h], e1[...]))
             d_weight = dot_rows(low1[p], d_qkv).astype(bf16)
             for j in range(QB):
                 for m in range(3):
                     grads[i, j, m * W : (m + 1) * W, :] = d_weight[j * W : (j + 1) * W, m * W : (m + 1) * W]
             hand_over(i, 1)
+        else:
+            da[...] += dot_cols(d_qkv, wide_matrix(h))
+
+    def late_output(i):
+        acc[...] += dot(actives[i], narrow_matrix(shard_of(0, i), W + D, D))
+
+    def late_input(i):
+        da[...] += dot_cols(d_qkvs[i], wide_matrix(shard_of(0, i)))
 
     def norm_backward(grad, scaled, inverse, gain):
         grad_scaled = grad * gain
@@ -804,11 +859,23 @@
             remote(src.at[p], there, o_s.at[p, n], o_r.at[p, n], core_peer),
         )
 
+    def block_result(p):
+        out_low[p] = acc[...].astype(bf16)
+        for copy in out_copies(p, 0):
+            copy.start()
+
+    def input_result(p):
+        def first_norm_back(t):
+            here = tile(t)
+            grad, scaled = da[here, :], xhat1[p, here, :]
+            add_norm(p, 0, grad, scaled)
+            in_low[p, here, :] = (cot[p, here, :] + norm_backward(grad, scaled, inv1[p, here, :], gain1)).astype(bf16)
+
+        loop(0, tiles, first_norm_back)
+        for copy in out_copies(p, 1):
+            copy.start()
+
     def layer_pass(p):
-        if p == 1:
-            loop(0, nz, send_b)
-            norm_copies()[0].start()
-
         acc[...] = jnp.zeros_like(acc)
         loop(0, 4, lambda h: attention(p, h))
 
@@ -824,23 +891,16 @@
 
         loop(0, tiles, second_norm)
         loop(0, 4, lambda i: feed_forward(p, i))
-        out_low[p] = acc[...].astype(bf16)
-        for copy in out_copies(p, 0):
-            copy.start()
-
         if p == 1:
-            norm_copies()[0].wait_recv()
-            norm_sum[0] = norm_part[...] + n_core[...]
-            norm_copies()[1].start()
+            block_result(1)
             for n in range(2):
                 x_push(n).wait_recv()
             loop(0, QB + CB, add_x)
             loop(0, nz, send_a)
             loop(0, nz, reduce1)
-            norm_copies()[1].wait_recv()
-            norm_sum[1] = norm_sum[0] + n_x[...]
-            norm_copies()[2].start()
-
+            norm_copies()[0].wait_recv()
+            norm_sum[0] = norm_part[...] + n_core[...]
+            norm_copies()[1].start()
 
         def second_norm_back(t):
             here = tile(t)
@@ -853,28 +913,32 @@
 
         loop(0, tiles, second_norm_back)
         if p == 1:
+            norm_copies()[1].wait_recv()
+            norm_sum[1] = norm_sum[0] + n_x[...]
+            norm_copies()[2].start()
             reduce2(0)
 
         def attention_step(i):
             attention_back(p, i)
             if p == 1:
-                pl.when(i < 2)(lambda: reduce2(i + 1))
-                pl.when(i == 1)(cross)
+                pl.when(i == 0)(lambda: reduce2(1))
+
+                @pl.when(i == 1)
+                def _():
+                    cross()
+                    reduce2(2)
 
         loop(0, 4, attention_step)
 
-        def first_norm_back(t):
-            here = tile(t)
-            grad, scaled = da[here, :], xhat1[p, here, :]
-            add_norm(p, 0, grad, scaled)
-            in_low[p, here, :] = (cot[p, here, :] + norm_backward(grad, scaled, inv1[p, here, :], gain1)).astype(bf16)
-
-        loop(0, tiles, first_norm_back)
-        for copy in out_copies(p, 1):
-            copy.start()
-
     layer_pass(0)
+    loop(0, nz, send_b)
+    loop(0, 4, late_output)
+    block_result(0)
+    loop(0, 4, late_input)
+    input_result(0)
+    norm_copies()[0].start()
     layer_pass(1)
+    input_result(1)
     norm_copies()[2].wait_recv()
     norm_sum[2] = norm_sum[1] + n_y[...]
     for copy in norm_copies()[3:]:
@@ -883,8 +947,9 @@
 
     for k in range(nz - 1):
         norm_copies()[3 + k].wait_recv()
-    over_z(2).wait_recv()
-    over_z(1).wait_recv()
+    for r in range(CAP):
+        over_z(2, r).wait_recv()
+        over_z(1, r).wait_recv()
     norm_total[...] = norm_sum[2] + ((n_z[0] + n_z[1]) + n_z[2])
 
     def last(r):
@@ -904,14 +969,20 @@
         meta_copy(k).wait_send()
     pl.when(up)(own_up.wait_send)
     pl.when(down)(own_down.wait_send)
+    for copy in c_copies:
+        copy.wait_send()
 
     def sent(k):
         for copy in first_copies(k) + second_copies(k) + third_copies(k):
             copy.wait_send()
         pl.when(jnp.logical_and(k > 0, inner))(along_z(k).wait_send)
+        for j in range(2):
+            last_core(j, k).wait_send()
+            pl.when(k > 0)(last_z(j, k).wait_send)
         for copy in (over_y_first(k), over_x_last(k), over_y_last(k)):
             copy.wait_send()
-        pl.when(k < nz - 1)(over_z(k).wait_send)
+        for r in range(CAP):
+            pl.when(k < nz - 1)(over_z(k, r).wait_send)
 
     loop(0, nz, sent)
     for n in range(2):
@@ -941,7 +1012,7 @@
         two, two, two_low, two, V((2, here, 1), f32), V((4, 3, here, W), bf16),
         V((4, items_here, 2, SEQ, SEQ), bf16), V((4, here, W), f32), V((4, here, W), bf16),
         full, low, full, V((here, 1), f32), two_low,
-        full, low, two_low, two_low,
+        V((4, here, D), bf16), V((4, here, 3 * W), bf16), full, low, two_low, two_low,
         V((4, blocks, R, W), bf16), V((2, blocks, R, W), bf16),
         V((blocks, RA, W), bf16), V((nz, CAP, RA, W), bf16), V((nz, CAP, RA, W), bf16),
         V((nz, 2, CAP, rb, W), bf16), V((nz, 2, CAP, rb, W), bf16), V((nz, CAP, rb, W), bf16),
@@ -949,8 +1020,9 @@
         V((8, D), f32), V((3, 8, D), f32), V((8, D), f32), V((8, D), f32), V((8, D), f32), V((nz - 1, 8, D), f32),
         dma((11,)), dma((nz + 1,)), dma((nz,)), dma((nz,)), dma((nz,)), dma((nz, 2)), dma((nz, 2)), dma((nz,)), dma((nz,)),
         dma((nz, 2)), dma((nz, 2)), dma((nz, 4)), dma((nz, 4)), dma((8,)), dma((8,)),
+        dma((3,)), dma((3,)), dma((2, nz)), dma((2, nz)), dma((2, nz)), dma((2, nz)),
         dma((2, 2)), dma((2, 2)), dma((2,)), dma((2,)), dma((nz,)), dma((nz,)), dma((nz,)), dma((nz,)),
-        dma((nz,)), dma((nz,)), dma((nz,)), dma((nz,)), dma((8,)), dma((8,)), dma((2, 2)), dma((2, 2)), dma((2, 2)),
+        dma((nz,)), dma((nz,)), dma((nz, CAP)), dma((nz, CAP)), dma((8,)), dma((8,)), dma((2, 2)), dma((2, 2)), dma((2, 2)),
     ]
     return pl.pallas_call(
         layer_kernel,

time: 134 us -> 129 us (0.963)
  Pallas kernels: 133 us -> 128 us
    pallas_call x1, Pallas kernels: 125 us -> 121 us  [layer(): pl.pallas_call(layer_kernel, name='layer', out_shape=(jax.ShapeDtypeStruc...]
where the time goes in v5:
time: 129 us
  Pallas kernels  128 us (99%)
    pallas_call x1, Pallas kernels, layer(): pl.pallas_call(layer_kernel, name='layer', out_shape=(jax.ShapeDtypeStruc...  121 us
    pallas_call x1, Pallas kernels, finish(): pl.pallas_call(finish_kernel, name='finish', out_shape=(jax.ShapeDtypeStr...  7.43 us

profile of v5, /device:TPU:0, one launch (start us, length us, event | category | flops | bytes accessed | tf_op | source)
XLA Modules:
  0.0 128.9 jit_solution(12892938543692396492)
XLA Ops:
  0.6 120.8 %layer.1 = (f32[3,384,128]{2,1,0:T(8,128)}, bf16[2048,512]{1,0:T(8,128)(2,1)}, bf16[2048,512]{1,0:T(8,128)(2,1)}, f32[8,512]{1,0:T(8,128)}) custom-call(f32[2048,512]{1,0:T(8,128)} %tok_hbm.1, f32[2048,512]{1,0:T(8,128)} %cot_hbm.1, f32[384,3,128]{2,1,0:T(4,128)} %bitcast.21, f32[4,64]{1,0:T(4,128)} %norm_m.1, s32[1,8]{1,0:T(1,128)} %bitcast.26, ...), custom_call_target="tpu_custom_call" | custom-call | tf_op jit(solution)/shard_map/layer/pallas_call | solution.py:1027
  121.5 7.4 %finish.1 = (f32[2048,512]{1,0:T(8,128)}, f32[2048,512]{1,0:T(8,128)}, f32[384,3,128]{2,1,0:T(4,128)}, f32[384,3,128]{2,1,0:T(4,128)}, f32[384,3,128]{2,1,0:T(4,...) custom-call(f32[3,384,128]{2,1,0:T(8,128)} %get-tuple-element.20.total_hbm, ...), custom_call_target="tpu_custom_call" | custom-call | tf_op jit(solution)/shard_map/finish/pallas_call | solution.py:1156

commit v6 on v5

--- a/solution.py
+++ b/solution.py
@@ -353,7 +353,7 @@
     return pieces
 
 
-RA = 288
+RA, RB = 192, 288
 GA, GB = 176, 336
 TILE = 128
 
@@ -364,9 +364,9 @@
     wv, master, flat, mine, meta, norms_v, steps, bands, lens_row, lens, owners, block_at,
     tok, cot, low1, xhat1, inv1, qkv, probs, sums, att, acc, low2, xhat2, inv2, e2, actives, d_qkvs, da, e1,
     out_low, in_low,
-    grads, from_core, rxa, sa, rya, sb, ryb, sbx, rxb, fz, rz, norm_part, norm_sum, n_core, n_x, n_y, n_z,
+    grads, from_core, rxa, sa, rya, sb, ryb, sbx, rxb, fz, rz, sc, rc, ryc, rxc, norm_part, norm_sum, n_core, n_x, n_y, n_z,
     i_sem, z_s, z_r, ya_s, ya_r, xa_s, xa_r, xb_s, xb_r, yb_s, yb_r, core_s, core_r, m_s, m_r,
-    c_s, c_r, zc_s, zc_r, cc_s, cc_r,
+    c_s, c_r, zc_s, zc_r, cc_s, cc_r, sc_s, sc_r, cy_s, cy_r, cx_s, cx_r,
     cs, cr, as_, ar, say_s, say_r, sby_s, sby_r, sbx_s, sbx_r, fz_s, fz_r, n_s, n_r, o_s, o_r, o_l,
 ):
     z, y, x, c = place(Sizes)
@@ -659,7 +659,7 @@
         )
 
     deep, low = (QB + 2, CB - 2), (0, QB + 2)
-    x_part, y_part = pl.ds(0, RA), pl.ds(RA, R - RA)
+    x_part, y_part, z_part = pl.ds(0, RA), pl.ds(RA, RB - RA), pl.ds(RB, R - RB)
 
     def core_push(j, n):
         part = pl.ds(*(deep, low)[n])
@@ -703,6 +703,43 @@
     def over_z(k, r):
         goal = pair_z + lax.rem(k, 2) * (cross_z - pair_z)
         return remote(fz.at[k, r], rz.at[k, r], fz_s.at[k, r], fz_r.at[k, r], device(goal, y, x, c))
+
+    def z_first(k):
+        goal = pair_z + lax.rem(k, 2) * (cross_z - pair_z)
+        return remote(sc.at[k], rc.at[k], sc_s.at[k], sc_r.at[k], device(goal, y, x, c))
+
+    def z_then_y():
+        return remote(sc.at[nz - 1, :, 1 - y], ryc, cy_s, cy_r, y_peer)
+
+    def z_then_x():
+        return remote(sc.at[nz - 1, 0, y], rxc, cx_s, cx_r, x_peer)
+
+    def send_c(k):
+        for r in range(2 * CAP):
+            block = block_of(k, r // CAP, r % CAP)
+            for j in range(2):
+                sc[k, j, r // CAP, r % CAP] = grads[2 + j, block, z_part, :]
+        pl.when(k == 0)(lambda: z_first(k).start())
+
+    def cross_c():
+        z_first(0).wait_recv()
+        for j in range(2):
+            sc[1, j] = sc[1, j] + rc[0, j]
+        z_first(1).start()
+        z_first(2).start()
+
+    def own_c():
+        z_first(1).wait_recv()
+        z_first(2).wait_recv()
+        for j in range(2):
+            sc[nz - 1, j] = sc[nz - 1, j] + (rc[1, j].astype(f32) + rc[2, j].astype(f32)).astype(bf16)
+        z_then_y().start()
+
+    def y_c():
+        z_then_y().wait_recv()
+        for j in range(2):
+            sc[nz - 1, j, y] = sc[nz - 1, j, y] + ryc[j]
+        z_then_x().start()
 
     def norm_copies():
         z_peers = [device(lax.rem(z + k, nz), y, x, c) for k in range(1, nz)]
@@ -878,6 +915,8 @@
     def layer_pass(p):
         acc[...] = jnp.zeros_like(acc)
         loop(0, 4, lambda h: attention(p, h))
+        if p == 1:
+            cross_c()
 
         def second_norm(t):
             here = tile(t)
@@ -890,14 +929,15 @@
             da[here, :] = jnp.zeros((TILE, D), f32)
 
         loop(0, tiles, second_norm)
-        loop(0, 4, lambda i: feed_forward(p, i))
         if p == 1:
-            block_result(1)
             for n in range(2):
                 x_push(n).wait_recv()
             loop(0, QB + CB, add_x)
             loop(0, nz, send_a)
             loop(0, nz, reduce1)
+        loop(0, 4, lambda i: feed_forward(p, i))
+        if p == 1:
+            block_result(1)
             norm_copies()[0].wait_recv()
             norm_sum[0] = norm_part[...] + n_core[...]
             norm_copies()[1].start()
@@ -921,16 +961,21 @@
         def attention_step(i):
             attention_back(p, i)
             if p == 1:
-                pl.when(i == 0)(lambda: reduce2(1))
+                @pl.when(i == 0)
+                def _():
+                    own_c()
+                    reduce2(1)
 
                 @pl.when(i == 1)
                 def _():
                     cross()
                     reduce2(2)
+                    y_c()
 
         loop(0, 4, attention_step)
 
     layer_pass(0)
+    loop(0, nz, send_c)
     loop(0, nz, send_b)
     loop(0, 4, late_output)
     block_result(0)
@@ -939,6 +984,7 @@
     norm_copies()[0].start()
     layer_pass(1)
     input_result(1)
+
     norm_copies()[2].wait_recv()
     norm_sum[2] = norm_sum[1] + n_y[...]
     for copy in norm_copies()[3:]:
@@ -947,6 +993,7 @@
 
     for k in range(nz - 1):
         norm_copies()[3 + k].wait_recv()
+    z_then_x().wait_recv()
     for r in range(CAP):
         over_z(2, r).wait_recv()
         over_z(1, r).wait_recv()
@@ -954,7 +1001,8 @@
 
     def last(r):
         others = rz[1, r].astype(f32) + rz[2, r].astype(f32)
-        total[r] = fz[nz - 1, r].astype(f32) + others
+        total[r, pl.ds(0, RB), :] = fz[nz - 1, r].astype(f32) + others
+        total[r, z_part, :] = sc[nz - 1, 1, y, r].astype(f32) + rxc[r].astype(f32)
 
     loop(0, CAP, last)
 
@@ -981,10 +1029,13 @@
             pl.when(k > 0)(last_z(j, k).wait_send)
         for copy in (over_y_first(k), over_x_last(k), over_y_last(k)):
             copy.wait_send()
+        pl.when(k < nz - 1)(z_first(k).wait_send)
         for r in range(CAP):
             pl.when(k < nz - 1)(over_z(k, r).wait_send)
 
     loop(0, nz, sent)
+    z_then_y().wait_send()
+    z_then_x().wait_send()
     for n in range(2):
         x_push(n).wait_send()
         for j in range(2):
@@ -1002,7 +1053,7 @@
     V, S = pltpu.VMEM, pltpu.SMEM
     square = (here, D)
     blocks = QB + CB
-    rb = R - RA
+    rb = RB - RA
     low, full, two_low, two = V(square, bf16), V(square, f32), V((2, *square), bf16), V((2, *square), f32)
     scratch = [
         V((4, nz * 2 * CAP, R, W), bf16), V((R, CAP, W), f32), V((R, W), f32),
@@ -1016,11 +1067,14 @@
         V((4, blocks, R, W), bf16), V((2, blocks, R, W), bf16),
         V((blocks, RA, W), bf16), V((nz, CAP, RA, W), bf16), V((nz, CAP, RA, W), bf16),
         V((nz, 2, CAP, rb, W), bf16), V((nz, 2, CAP, rb, W), bf16), V((nz, CAP, rb, W), bf16),
-        V((nz, CAP, rb, W), bf16), V((nz, CAP, R, W), bf16), V((nz - 1, CAP, R, W), bf16),
+        V((nz, CAP, rb, W), bf16), V((nz, CAP, RB, W), bf16), V((nz - 1, CAP, RB, W), bf16),
+        V((nz, 2, 2, CAP, R - RB, W), bf16), V((nz - 1, 2, 2, CAP, R - RB, W), bf16),
+        V((2, CAP, R - RB, W), bf16), V((CAP, R - RB, W), bf16),
         V((8, D), f32), V((3, 8, D), f32), V((8, D), f32), V((8, D), f32), V((8, D), f32), V((nz - 1, 8, D), f32),
         dma((11,)), dma((nz + 1,)), dma((nz,)), dma((nz,)), dma((nz,)), dma((nz, 2)), dma((nz, 2)), dma((nz,)), dma((nz,)),
         dma((nz, 2)), dma((nz, 2)), dma((nz, 4)), dma((nz, 4)), dma((8,)), dma((8,)),
         dma((3,)), dma((3,)), dma((2, nz)), dma((2, nz)), dma((2, nz)), dma((2, nz)),
+        dma((nz,)), dma((nz,)), dma, dma, dma, dma,
         dma((2, 2)), dma((2, 2)), dma((2,)), dma((2,)), dma((nz,)), dma((nz,)), dma((nz,)), dma((nz,)),
         dma((nz,)), dma((nz,)), dma((nz, CAP)), dma((nz, CAP)), dma((8,)), dma((8,)), dma((2, 2)), dma((2, 2)), dma((2, 2)),
     ]

time: 129 us -> 121 us (0.938)
  Pallas kernels: 128 us -> 120 us
    pallas_call x1, Pallas kernels: 121 us -> 112 us  [layer(): pl.pallas_call(layer_kernel, name='layer', out_shape=(jax.ShapeDtypeStruc...]
where the time goes in v6:
time: 121 us; the launch traced here: 120 us
  Pallas kernels  120 us (99%)
    pallas_call x1, Pallas kernels, layer(): pl.pallas_call(layer_kernel, name='layer', out_shape=(jax.ShapeDtypeStruc...  112 us
    pallas_call x1, Pallas kernels, finish(): pl.pallas_call(finish_kernel, name='finish', out_shape=(jax.ShapeDtypeStr...  7.43 us

profile of v6, /device:TPU:0, one launch (start us, length us, event | category | flops | bytes accessed | tf_op | source)
XLA Modules:
  0.0 120.4 jit_solution(2168541517837780846)
XLA Ops:
  0.6 112.3 %layer.1 = (f32[3,384,128]{2,1,0:T(8,128)}, bf16[2048,512]{1,0:T(8,128)(2,1)}, bf16[2048,512]{1,0:T(8,128)(2,1)}, f32[8,512]{1,0:T(8,128)}) custom-call(f32[2048,512]{1,0:T(8,128)} %tok_hbm.1, f32[2048,512]{1,0:T(8,128)} %cot_hbm.1, f32[384,3,128]{2,1,0:T(4,128)} %bitcast.21, f32[4,64]{1,0:T(4,128)} %norm_m.1, s32[1,8]{1,0:T(1,128)} %bitcast.26, ...), custom_call_target="tpu_custom_call" | custom-call | tf_op jit(solution)/shard_map/layer/pallas_call | solution.py:1081
  112.9 7.4 %finish.1 = (f32[2048,512]{1,0:T(8,128)}, f32[2048,512]{1,0:T(8,128)}, f32[384,3,128]{2,1,0:T(4,128)}, f32[384,3,128]{2,1,0:T(4,128)}, f32[384,3,128]{2,1,0:T(4,...) custom-call(f32[3,384,128]{2,1,0:T(8,128)} %get-tuple-element.20.total_hbm, ...), custom_call_target="tpu_custom_call" | custom-call | tf_op jit(solution)/shard_map/finish/pallas_call | solution.py:1210

commit v7 on v6

--- a/solution.py
+++ b/solution.py
@@ -295,13 +295,6 @@
     return (z * Sizes.y + y, x * Sizes.c + c)
 
 
-def greet(partners):
-    barrier = pltpu.get_barrier_semaphore()
-    for partner in partners:
-        pl.semaphore_signal(barrier, inc=1, device_id=partner, device_id_type=MESH)
-    pl.semaphore_wait(barrier, len(partners))
-
-
 def block_rows(owners):
     ids = [owners[j] for j in range(owners.shape[0])]
     rows = []
@@ -353,7 +346,7 @@
     return pieces
 
 
-RA, RB = 192, 288
+RA, RB = 224, 304
 GA, GB = 176, 336
 TILE = 128
 
@@ -719,14 +712,13 @@
             block = block_of(k, r // CAP, r % CAP)
             for j in range(2):
                 sc[k, j, r // CAP, r % CAP] = grads[2 + j, block, z_part, :]
-        pl.when(k == 0)(lambda: z_first(k).start())
+        pl.when(lax.rem(k, 2) == 0)(lambda: z_first(k).start())
 
     def cross_c():
         z_first(0).wait_recv()
         for j in range(2):
             sc[1, j] = sc[1, j] + rc[0, j]
         z_first(1).start()
-        z_first(2).start()
 
     def own_c():
         z_first(1).wait_recv()
@@ -915,8 +907,6 @@
     def layer_pass(p):
         acc[...] = jnp.zeros_like(acc)
         loop(0, 4, lambda h: attention(p, h))
-        if p == 1:
-            cross_c()
 
         def second_norm(t):
             here = tile(t)
@@ -938,6 +928,8 @@
         loop(0, 4, lambda i: feed_forward(p, i))
         if p == 1:
             block_result(1)
+            own_c()
+            reduce2(0)
             norm_copies()[0].wait_recv()
             norm_sum[0] = norm_part[...] + n_core[...]
             norm_copies()[1].start()
@@ -956,19 +948,14 @@
             norm_copies()[1].wait_recv()
             norm_sum[1] = norm_sum[0] + n_x[...]
             norm_copies()[2].start()
-            reduce2(0)
+            reduce2(1)
+            cross()
 
         def attention_step(i):
             attention_back(p, i)
             if p == 1:
-                @pl.when(i == 0)
-                def _():
-                    own_c()
-                    reduce2(1)
-
                 @pl.when(i == 1)
                 def _():
-                    cross()
                     reduce2(2)
                     y_c()
 
@@ -981,6 +968,7 @@
     block_result(0)
     loop(0, 4, late_input)
     input_result(0)
+    cross_c()
     norm_copies()[0].start()
     layer_pass(1)
     input_result(1)

time: 121 us -> 119 us (0.983)
  Pallas kernels: 120 us -> 118 us
    pallas_call x1, Pallas kernels: 112 us -> 111 us  [layer(): pl.pallas_call(layer_kernel, name='layer', out_shape=(jax.ShapeDtypeStruc...]
where the time goes in v7:
time: 119 us
  Pallas kernels  118 us (99%)
    pallas_call x1, Pallas kernels, layer(): pl.pallas_call(layer_kernel, name='layer', out_shape=(jax.ShapeDtypeStruc...  111 us
    pallas_call x1, Pallas kernels, finish(): pl.pallas_call(finish_kernel, name='finish', out_shape=(jax.ShapeDtypeStr...  7.43 us

profile of v7, /device:TPU:0, one launch (start us, length us, event | category | flops | bytes accessed | tf_op | source)
XLA Modules:
  0.0 119.0 jit_solution(10474512977216483590)
XLA Ops:
  0.6 110.9 %layer.1 = (f32[3,384,128]{2,1,0:T(8,128)}, bf16[2048,512]{1,0:T(8,128)(2,1)}, bf16[2048,512]{1,0:T(8,128)(2,1)}, f32[8,512]{1,0:T(8,128)}) custom-call(f32[2048,512]{1,0:T(8,128)} %tok_hbm.1, f32[2048,512]{1,0:T(8,128)} %cot_hbm.1, f32[384,3,128]{2,1,0:T(4,128)} %bitcast.21, f32[4,64]{1,0:T(4,128)} %norm_m.1, s32[1,8]{1,0:T(1,128)} %bitcast.26, ...), custom_call_target="tpu_custom_call" | custom-call | tf_op jit(solution)/shard_map/layer/pallas_call | solution.py:1069
  111.5 7.4 %finish.1 = (f32[2048,512]{1,0:T(8,128)}, f32[2048,512]{1,0:T(8,128)}, f32[384,3,128]{2,1,0:T(4,128)}, f32[384,3,128]{2,1,0:T(4,128)}, f32[384,3,128]{2,1,0:T(4,...) custom-call(f32[3,384,128]{2,1,0:T(8,128)} %get-tuple-element.20.total_hbm, ...), custom_call_target="tpu_custom_call" | custom-call | tf_op jit(solution)/shard_map/finish/pallas_call | solution.py:1198

commit v8 on v7

--- a/solution.py
+++ b/solution.py
@@ -1123,9 +1123,9 @@
 
     for copy in small_copies:
         copy.start()
-    loop(pieces, lambda p: fetch(0, p).start())
     for copy in state_copies:
         copy.start()
+    loop(pieces, lambda p: fetch(0, p).start())
     loop(pieces, lambda p: fetch(1, p).start())
 
     dp = lax.axis_index("dp")
@@ -1159,7 +1159,6 @@
         full[piece(p), :] = low[piece(p), :].astype(f32)
         store(n, p).start()
 
-    loop(pieces, lambda p: convert(0, p))
     for copy in state_copies:
         copy.wait()
     step = 32
@@ -1171,7 +1170,13 @@
         for n in range(3):
             results[n, here] = jnp.where(slot < held, new[n], 0.0)
 
-    loop(R // step, update)
+
+    def both(p):
+        convert(0, p)
+        for i in range(R // step // pieces):
+            update(p * (R // step // pieces) + i)
+
+    loop(pieces, both)
     for copy in result_copies:
         copy.start()
     for copy in small_copies[2:]:
@@ -1193,7 +1198,7 @@
     hbm = pl.BlockSpec(memory_space=pltpu.HBM)
     dma = pltpu.SemaphoreType.DMA
     V = pltpu.VMEM
-    pieces = 8
+    pieces = 4
     shape = out_all.shape
     return pl.pallas_call(
         finish_kernel,

time: 119 us -> 119 us (level)
  no operation moved by 1% of the time
where the time goes in v8:
time: 119 us; the launch traced here: 118 us
  Pallas kernels  118 us (99%)
    pallas_call x1, Pallas kernels, layer(): pl.pallas_call(layer_kernel, name='layer', out_shape=(jax.ShapeDtypeStruc...  111 us
    pallas_call x1, Pallas kernels, finish(): pl.pallas_call(finish_kernel, name='finish', out_shape=(jax.ShapeDtypeStr...  6.91 us

profile of v8, /device:TPU:0, one launch (start us, length us, event | category | flops | bytes accessed | tf_op | source)
XLA Modules:
  0.0 118.4 jit_solution(10783933422424807321)
XLA Ops:
  0.6 110.9 %layer.1 = (f32[3,384,128]{2,1,0:T(8,128)}, bf16[2048,512]{1,0:T(8,128)(2,1)}, bf16[2048,512]{1,0:T(8,128)(2,1)}, f32[8,512]{1,0:T(8,128)}) custom-call(f32[2048,512]{1,0:T(8,128)} %tok_hbm.1, f32[2048,512]{1,0:T(8,128)} %cot_hbm.1, f32[384,3,128]{2,1,0:T(4,128)} %bitcast.21, f32[4,64]{1,0:T(4,128)} %norm_m.1, s32[1,8]{1,0:T(1,128)} %bitcast.26, ...), custom_call_target="tpu_custom_call" | custom-call | tf_op jit(solution)/shard_map/layer/pallas_call | solution.py:1069
  111.5 6.9 %finish.1 = (f32[2048,512]{1,0:T(8,128)}, f32[2048,512]{1,0:T(8,128)}, f32[384,3,128]{2,1,0:T(4,128)}, f32[384,3,128]{2,1,0:T(4,128)}, f32[384,3,128]{2,1,0:T(4,...) custom-call(f32[3,384,128]{2,1,0:T(8,128)} %get-tuple-element.20.total_hbm, ...), custom_call_target="tpu_custom_call" | custom-call | tf_op jit(solution)/shard_map/finish/pallas_call | solution.py:1203

commit v9 on v8

--- a/solution.py
+++ b/solution.py
@@ -949,13 +949,13 @@
             norm_sum[1] = norm_sum[0] + n_x[...]
             norm_copies()[2].start()
             reduce2(1)
-            cross()
 
         def attention_step(i):
             attention_back(p, i)
             if p == 1:
                 @pl.when(i == 1)
                 def _():
+                    cross()
                     reduce2(2)
                     y_c()
 

time: 119 us -> 119 us (level)
  no operation moved by 1% of the time
where the time goes in v9:
time: 119 us; the launch traced here: 118 us
  Pallas kernels  118 us (99%)
    pallas_call x1, Pallas kernels, layer(): pl.pallas_call(layer_kernel, name='layer', out_shape=(jax.ShapeDtypeStruc...  111 us
    pallas_call x1, Pallas kernels, finish(): pl.pallas_call(finish_kernel, name='finish', out_shape=(jax.ShapeDtypeStr...  6.91 us

profile of v9, /device:TPU:0, one launch (start us, length us, event | category | flops | bytes accessed | tf_op | source)
XLA Modules:
  0.0 118.4 jit_solution(792474184309581074)
XLA Ops:
  0.6 110.9 %layer.1 = (f32[3,384,128]{2,1,0:T(8,128)}, bf16[2048,512]{1,0:T(8,128)(2,1)}, bf16[2048,512]{1,0:T(8,128)(2,1)}, f32[8,512]{1,0:T(8,128)}) custom-call(f32[2048,512]{1,0:T(8,128)} %tok_hbm.1, f32[2048,512]{1,0:T(8,128)} %cot_hbm.1, f32[384,3,128]{2,1,0:T(4,128)} %bitcast.21, f32[4,64]{1,0:T(4,128)} %norm_m.1, s32[1,8]{1,0:T(1,128)} %bitcast.26, ...), custom_call_target="tpu_custom_call" | custom-call | tf_op jit(solution)/shard_map/layer/pallas_call | solution.py:1069
  111.5 6.9 %finish.1 = (f32[2048,512]{1,0:T(8,128)}, f32[2048,512]{1,0:T(8,128)}, f32[384,3,128]{2,1,0:T(4,128)}, f32[384,3,128]{2,1,0:T(4,128)}, f32[384,3,128]{2,1,0:T(4,...) custom-call(f32[3,384,128]{2,1,0:T(8,128)} %get-tuple-element.20.total_hbm, ...), custom_call_target="tpu_custom_call" | custom-call | tf_op jit(solution)/shard_map/finish/pallas_call | solution.py:1203

commit v10 on v8

--- a/solution.py
+++ b/solution.py
@@ -348,7 +348,7 @@
 
 RA, RB = 224, 304
 GA, GB = 176, 336
-TILE = 128
+TILE = 256
 
 
 def layer_kernel(

time: 119 us -> 118 us (level)
    pallas_call x1, Pallas kernels: 111 us -> 110 us  [layer(): pl.pallas_call(layer_kernel, name='layer', out_shape=(jax.ShapeDtypeStruc...]
where the time goes in v10:
time: 118 us; the launch traced here: 117 us
  Pallas kernels  117 us (99%)
    pallas_call x1, Pallas kernels, layer(): pl.pallas_call(layer_kernel, name='layer', out_shape=(jax.ShapeDtypeStruc...  110 us
    pallas_call x1, Pallas kernels, finish(): pl.pallas_call(finish_kernel, name='finish', out_shape=(jax.ShapeDtypeStr...  6.91 us

profile of v10, /device:TPU:0, one launch (start us, length us, event | category | flops | bytes accessed | tf_op | source)
XLA Modules:
  0.0 117.2 jit_solution(13965706991309996436)
XLA Ops:
  0.6 109.6 %layer.1 = (f32[3,384,128]{2,1,0:T(8,128)}, bf16[2048,512]{1,0:T(8,128)(2,1)}, bf16[2048,512]{1,0:T(8,128)(2,1)}, f32[8,512]{1,0:T(8,128)}) custom-call(f32[2048,512]{1,0:T(8,128)} %tok_hbm.1, f32[2048,512]{1,0:T(8,128)} %cot_hbm.1, f32[384,3,128]{2,1,0:T(4,128)} %bitcast.21, f32[4,64]{1,0:T(4,128)} %norm_m.1, s32[1,8]{1,0:T(1,128)} %bitcast.26, ...), custom_call_target="tpu_custom_call" | custom-call | tf_op jit(solution)/shard_map/layer/pallas_call | solution.py:1069
  110.3 6.9 %finish.1 = (f32[2048,512]{1,0:T(8,128)}, f32[2048,512]{1,0:T(8,128)}, f32[384,3,128]{2,1,0:T(4,128)}, f32[384,3,128]{2,1,0:T(4,128)}, f32[384,3,128]{2,1,0:T(4,...) custom-call(f32[3,384,128]{2,1,0:T(8,128)} %get-tuple-element.20.total_hbm, ...), custom_call_target="tpu_custom_call" | custom-call | tf_op jit(solution)/shard_map/finish/pallas_call | solution.py:1203
